TPU v7x, 512 devices: a whole 4x8x8 slice. The times are simulated.
512 devices in a mesh: box: 64 (over y, x, core), samp: 8 (over z).
Axes of the slice: x: 4, y: 8, z: 8, core: 2. Of those that a mesh axis runs over, the one named last changes fastest.
Arguments:
- currents: bfloat16 [2, 1024, 24576], P(None, None, 'box'), may hold values from -6 to 6
- radiation: bfloat16 [2, 1024, 32, 64], P(None, None, None, 'samp'), may hold values from -0.125 to 0.125
- interp: float32 [7, 64], P(None, 'samp'), may hold values from -2 to 2
- anterp: float32 [7, 64], P(None, 'samp'), may hold values from -2 to 2
- weights: float32 [32], replicated, may hold values from 0.2 to 2
- operators: bfloat16 [2, 32, 64, 316], P(None, None, 'samp'), may hold values from -4 to 4
- pair_src: int32 [40960], P('box'), may hold values from 0 to 383
- pair_op: int32 [40960], P('box'), may hold values from 0 to 315
- pair_target: int32 [40960], P('box'), may hold values from 0 to 24575, as said below
Outputs:
- received: bfloat16 [2, 1024, 24576], P(None, 'samp', 'box')
Inputs may be any that keep to these rules, and one draw needn't show every extreme that they name: The box group that owns pair i's target, pair_target[i] // 384, lies at most 2 groups from the pair's own group i // 640. At most 128 of one group's pairs name targets of any one other group, and the pairs of every group but the last name exactly 128 targets of the next group.
All inputs are finite; a program needn't handle non-finite values.
Results may differ from a plain program's by a relative error of at most 0.0058.
Values may be sent and summed in bfloat16 or wider, within the bound.
No kernel may reach another device: no remote copies, remote signals or barrier semaphores. Data moves between devices by JAX's collectives and lax.ppermute only.
A program may use at most 64 MiB of HBM per device.

v0:
```python
import jax
import jax.numpy as jnp
from jax import lax
from jax.sharding import PartitionSpec as P

NT = 32
P_SIZE = 1024
WIDTH = 3
REACH = 2
CAP = 128


def extended(block, sides, width):
    for axis, dim in sides:
        count = lax.axis_size(axis)
        forward = [(i, i + 1) for i in range(count - 1)]
        forward.append((count - 1, 0))
        backward = [(target, source) for source, target in forward]
        low = lax.ppermute(
            lax.slice_in_dim(block, block.shape[dim] - width, None, axis=dim), axis, forward
        )
        high = lax.ppermute(lax.slice_in_dim(block, 0, width, axis=dim), axis, backward)
        block = jnp.concatenate([low, block, high], axis=dim)
    return block


def from_behind(value, axis, steps):
    count = lax.axis_size(axis)
    leading, last = (max(0, -steps), min(count, count - steps))
    return lax.ppermute(value, axis, [(source, source + steps) for source in range(leading, last)])


def contract_first(left, right):
    return lax.dot_general(
        left, right, (((0,), (0,)), ((), ())), preferred_element_type=jnp.float32
    )


def select_last(values, table, precision=None):
    return lax.dot_general(
        values,
        table,
        (((3,), (0,)), ((), ())),
        precision=precision,
        preferred_element_type=jnp.float32,
    )


def along_phi(coeffs, padded, width):
    total = jnp.zeros(padded.shape[:2] + (width, padded.shape[3]), jnp.float32)
    for k in range(2 * WIDTH + 1):
        total = total + coeffs[k][None, None, :, None] * padded[:, :, k : k + width, :]
    return total


def box_table(box_ids, local_boxes):
    columns = jnp.arange(local_boxes, dtype=jnp.int32)
    return (box_ids[:, None] == columns[None, :]).astype(jnp.bfloat16)


def on_device(
    currents, radiation, interp, anterp, weights, operators, pair_src, pair_op, pair_target
):
    local_boxes = currents.shape[2]
    phi_dev = radiation.shape[3]
    pair_count = pair_src.shape[0]
    count = NT * phi_dev
    rad_re = radiation[0].reshape(P_SIZE, count)
    rad_im = radiation[1].reshape(P_SIZE, count)
    field_re = contract_first(rad_re, currents[0]) - contract_first(rad_im, currents[1])
    field_im = contract_first(rad_re, currents[1]) + contract_first(rad_im, currents[0])
    field = jnp.stack([field_re, field_im]).reshape(2, NT, phi_dev, local_boxes)
    padded = extended(field, (("samp", 2),), WIDTH)
    inter = along_phi(interp, padded, phi_dev)
    box_cols = jnp.arange(local_boxes, dtype=jnp.int32)
    src_pick = jnp.transpose((box_cols[:, None] == pair_src[None, :]).astype(jnp.float32))
    src_pick = jnp.transpose(src_pick)
    src_field = select_last(inter, src_pick, lax.Precision.HIGHEST)
    op_cols = jnp.arange(operators.shape[3], dtype=jnp.int32)
    op_pick = (op_cols[:, None] == pair_op[None, :]).astype(jnp.bfloat16)
    oper_vals = select_last(operators, op_pick)
    part_re = oper_vals[0] * src_field[0] - oper_vals[1] * src_field[1]
    part_im = oper_vals[0] * src_field[1] + oper_vals[1] * src_field[0]
    contrib = jnp.stack([part_re, part_im]).astype(jnp.bfloat16)
    myself = lax.axis_index("box")
    owner = pair_target // local_boxes
    target_box = pair_target - owner * local_boxes
    offset = owner - myself
    local_index = jnp.where(offset == 0, target_box, local_boxes)
    incoming = select_last(contrib, box_table(local_index, local_boxes))
    reaches = jnp.arange(-REACH, REACH + 1, dtype=jnp.int32)
    onehot = (offset[:, None] == reaches[None, :]).astype(jnp.float32)
    pair_rows = jnp.arange(pair_count, dtype=jnp.int32)
    lower = (pair_rows[:, None] > pair_rows[None, :]).astype(jnp.float32)
    before = jnp.dot(
        lower, onehot, precision=lax.Precision.HIGHEST, preferred_element_type=jnp.float32
    )
    rank = jnp.sum(before * onehot, axis=1).astype(jnp.int32)
    slot_cols = jnp.arange(CAP, dtype=jnp.int32)
    for step in range(-REACH, REACH + 1):
        if step != 0:
            slot = jnp.where(offset == step, rank, CAP)
            chosen = slot[:, None] == slot_cols[None, :]
            buffer = select_last(contrib, chosen.astype(jnp.bfloat16)).astype(jnp.bfloat16)
            filled = jnp.sum(chosen.astype(jnp.int32), axis=0)
            named = jnp.sum(chosen.astype(jnp.int32) * target_box[:, None], axis=0)
            box_ids = jnp.where(filled > 0, named, local_boxes)
            buffer, box_ids = (buffer, box_ids.reshape(1, 1, 1, CAP))
            got, got_ids = from_behind((buffer, box_ids), "box", step)
            incoming = incoming + select_last(got, box_table(got_ids.reshape(-1), local_boxes))
    padded_in = extended(incoming, (("samp", 2),), WIDTH)
    outgoing = along_phi(anterp, padded_in, phi_dev) * weights[None, :, None, None]
    outgoing = outgoing.astype(jnp.bfloat16)
    flat_out = outgoing.reshape(2, count, local_boxes)
    recv_re = jnp.dot(rad_re, flat_out[0], preferred_element_type=jnp.float32) + jnp.dot(
        rad_im, flat_out[1], preferred_element_type=jnp.float32
    )
    recv_im = jnp.dot(rad_re, flat_out[1], preferred_element_type=jnp.float32) - jnp.dot(
        rad_im, flat_out[0], preferred_element_type=jnp.float32
    )
    terms = jnp.stack([recv_re, recv_im])
    return lax.psum_scatter(terms, "samp", scatter_dimension=1, tiled=True).astype(jnp.bfloat16)


def solution(mesh):
    return jax.shard_map(
        on_device,
        mesh=mesh,
        in_specs=(
            P(None, None, "box"),
            P(None, None, None, "samp"),
            P(None, "samp"),
            P(None, "samp"),
            P(),
            P(None, None, "samp", None),
            P("box"),
            P("box"),
            P("box"),
        ),
        out_specs=P(None, "samp", "box"),
        check_vma=False,
    )
```

profile of v0, /device:TPU:4, one launch (start us, length us, event | category | flops | bytes accessed | tf_op | source)
XLA Modules:
  0.0 147.0 jit_solution(15940590116033210800)
XLA Ops:
  6.6 0.8 compare_select_fusion
  7.7 0.6 convert_reduce_fusion.2
  8.4 2.4 %collective-permute-start.3 = (s32[1,1,1,128]{3,2,1,0:T(1,128)S(1)}, s32[1,1,1,128]{3,2,1,0:T(1,128)S(1)}, u32[]{:S(2)}, u32[]{:S(2)}) collective-permute-start(s32[1,1,1,128]{3,2,1,0:T(1,128)S(1)} %fusion.112), channel_id=1, source_target_pairs={{16,0},{24,8},{32,16},{40,24},{48,32},{56,40},{64,48},{72,56},{80,... | collective-permute-start | bytes 1544 | tf_op jit(solution)/shard_map/ppermute | solution.py:30
  10.9 3.4 %collective-permute-start.9 = (s32[1,1,1,128]{3,2,1,0:T(1,128)S(1)}, s32[1,1,1,128]{3,2,1,0:T(1,128)S(1)}, u32[]{:S(2)}, u32[]{:S(2)}) collective-permute-start(s32[1,1,1,128]{3,2,1,0:T(1,128)S(1)} %fusion.115), channel_id=1, source_target_pairs={{0,16},{8,24},{16,32},{24,40},{32,48},{40,56},{48,64},{56,72},{64,... | collective-permute-start | bytes 1544 | tf_op jit(solution)/shard_map/ppermute | solution.py:30
  14.3 2.1 %collective-permute-start.7 = (s32[1,1,1,128]{3,2,1,0:T(1,128)S(1)}, s32[1,1,1,128]{3,2,1,0:T(1,128)S(1)}, u32[]{:S(2)}, u32[]{:S(2)}) collective-permute-start(s32[1,1,1,128]{3,2,1,0:T(1,128)S(1)} %fusion.114), channel_id=1, source_target_pairs={{0,8},{8,16},{16,24},{24,32},{32,40},{40,48},{48,56},{56,64},{64,7... | collective-permute-start | bytes 1544 | tf_op jit(solution)/shard_map/ppermute | solution.py:30
  16.4 1.7 %fusion.42 = f32[256,384]{1,0:T(8,128)S(1)} fusion(bf16[2,1024,384]{2,1,0:T(8,128)(2,1)} %param.9, bf16[2,1024,32,8]{1,3,2,0:T(8,128)(2,1)} %param.10), kind=kOutput, calls=%fused_computation.78 | convolution fusion | flops 201326592 | bytes 1703936 | tf_op jit(solution)/shard_map/dot_general | solution.py:34
  18.1 1.5 %fusion.46 = f32[256,384]{1,0:T(8,128)S(1)} fusion(bf16[2,1024,384]{2,1,0:T(8,128)(2,1)S(1)} %copy-done.5, bf16[2,1024,32,8]{1,3,2,0:T(8,128)(2,1)} %param.10), kind=kOutput, calls=%fused_computation.82 | convolution fusion | flops 201326592 | bytes 1703936 | tf_op jit(solution)/shard_map/dot_general | solution.py:34
  19.6 0.4 fusion.5
  20.1 0.4 fusion.6
  20.6 4.3 %collective-permute-start = (f32[2,32,3,384]{3,2,1,0:T(4,128)S(1)}, f32[2,32,3,384]{3,2,1,0:T(4,128)S(1)}, u32[]{:S(2)}, u32[]{:S(2)}) collective-permute-start(f32[2,32,3,384]{3,2,1,0:T(4,128)S(1)} %get-tuple-element.21), channel_id=1, source_target_pairs={{0,1},{1,2},{2,3},{3,4},{4,5},{5,6},{6,7},{7,0},{8,9},{9,10},{10,1... | collective-permute-start | bytes 884744 | tf_op jit(solution)/shard_map/ppermute | solution.py:19
  24.9 8.6 %collective-permute-start.1 = (f32[2,32,3,384]{3,2,1,0:T(4,128)S(1)}, f32[2,32,3,384]{3,2,1,0:T(4,128)S(1)}, u32[]{:S(2)}, u32[]{:S(2)}) collective-permute-start(f32[2,32,3,384]{3,2,1,0:T(4,128)S(1)} %get-tuple-element.22), channel_id=1, source_target_pairs={{1,0},{2,1},{3,2},{4,3},{5,4},{6,5},{7,6},{0,7},{9,8},{10,9},{11,1... | collective-permute-start | bytes 884744 | tf_op jit(solution)/shard_map/ppermute | solution.py:22
  33.6 0.6 convolution_bitcast_fusion
  34.1 4.6 %collective-permute-done = f32[2,32,3,384]{3,2,1,0:T(4,128)S(1)} collective-permute-done((f32[2,32,3,384]{3,2,1,0:T(4,128)S(1)}, f32[2,32,3,384]{3,2,1,0:T(4,128)S(1)}, u32[]{:S(2)}, u32[]{:S(2)}) %collective-permute-start) | collective-permute-done | bytes 294944 | tf_op jit(solution)/shard_map/ppermute | solution.py:19
  38.7 4.6 %collective-permute-start.5 = (s32[1,1,1,128]{3,2,1,0:T(1,128)S(1)}, s32[1,1,1,128]{3,2,1,0:T(1,128)S(1)}, u32[]{:S(2)}, u32[]{:S(2)}) collective-permute-start(s32[1,1,1,128]{3,2,1,0:T(1,128)S(1)} %fusion.113), channel_id=1, source_target_pairs={{8,0},{16,8},{24,16},{32,24},{40,32},{48,40},{56,48},{64,56},{72,6... | collective-permute-start | bytes 1544 | tf_op jit(solution)/shard_map/ppermute | solution.py:30
  43.7 0.6 fusion.21
  44.4 1.4 fusion.10
  47.4 1.9 %collective-permute-start.2 = (bf16[2,32,8,128]{3,1,2,0:T(8,128)(2,1)S(1)}, bf16[2,32,8,128]{3,1,2,0:T(8,128)(2,1)S(1)}, u32[]{:S(2)}, u32[]{:S(2)}) collective-permute-start(bf16[2,32,8,128]{3,1,2,0:T(8,128)(2,1)S(1)} %convolution_convert_fusion.3), channel_id=1, source_target_pairs={{16,0},{24,8},{32,16},{40,24},{48,32},{56,40},{64,48},{72,56},{80,... | collective-permute-start | bytes 393224 | tf_op jit(solution)/shard_map/ppermute | solution.py:30
  49.3 0.7 fusion.13
  50.4 4.7 %collective-permute-start.8 = (bf16[2,32,8,128]{3,1,2,0:T(8,128)(2,1)S(1)}, bf16[2,32,8,128]{3,1,2,0:T(8,128)(2,1)S(1)}, u32[]{:S(2)}, u32[]{:S(2)}) collective-permute-start(bf16[2,32,8,128]{3,1,2,0:T(8,128)(2,1)S(1)} %convolution_convert_fusion), channel_id=1, source_target_pairs={{0,16},{8,24},{16,32},{24,40},{32,48},{40,56},{48,64},{56,72},{64,... | collective-permute-start | bytes 393224 | tf_op jit(solution)/shard_map/ppermute | solution.py:30
  55.1 1.1 collective-permute-done.2
  56.2 1.9 %collective-permute-start.6 = (bf16[2,32,8,128]{3,1,2,0:T(8,128)(2,1)S(1)}, bf16[2,32,8,128]{3,1,2,0:T(8,128)(2,1)S(1)}, u32[]{:S(2)}, u32[]{:S(2)}) collective-permute-start(bf16[2,32,8,128]{3,1,2,0:T(8,128)(2,1)S(1)} %convolution_convert_fusion.1), channel_id=1, source_target_pairs={{0,8},{8,16},{16,24},{24,32},{32,40},{40,48},{48,56},{56,64},{64,7... | collective-permute-start | bytes 393224 | tf_op jit(solution)/shard_map/ppermute | solution.py:30
  58.5 3.7 %collective-permute-start.4 = (bf16[2,32,8,128]{3,1,2,0:T(8,128)(2,1)S(1)}, bf16[2,32,8,128]{3,1,2,0:T(8,128)(2,1)S(1)}, u32[]{:S(2)}, u32[]{:S(2)}) collective-permute-start(bf16[2,32,8,128]{3,1,2,0:T(8,128)(2,1)S(1)} %convolution_convert_fusion.2), channel_id=1, source_target_pairs={{8,0},{16,8},{24,16},{32,24},{40,32},{48,40},{56,48},{64,56},{72,6... | collective-permute-start | bytes 393224 | tf_op jit(solution)/shard_map/ppermute | solution.py:30
  63.2 2.0 %collective-permute-done.4 = bf16[2,32,8,128]{3,1,2,0:T(8,128)(2,1)S(1)} collective-permute-done((bf16[2,32,8,128]{3,1,2,0:T(8,128)(2,1)S(1)}, bf16[2,32,8,128]{3,1,2,0:T(8,128)(2,1)S(1)}, u32[]{:S(2)}, u32[]{:S(2)}) %collective-permute-start.4) | collective-permute-done | bytes 131104 | tf_op jit(solution)/shard_map/ppermute | solution.py:30
  65.7 1.9 %collective-permute-start.10 = (f32[2,32,3,384]{3,2,1,0:T(4,128)S(1)}, f32[2,32,3,384]{3,2,1,0:T(4,128)S(1)}, u32[]{:S(2)}, u32[]{:S(2)}) collective-permute-start(f32[2,32,3,384]{3,2,1,0:T(4,128)S(1)} %get-tuple-element.17), channel_id=1, source_target_pairs={{0,1},{1,2},{2,3},{3,4},{4,5},{5,6},{6,7},{7,0},{8,9},{9,10},{10,1... | collective-permute-start | bytes 884744 | tf_op jit(solution)/shard_map/ppermute | solution.py:19
  67.6 5.3 %collective-permute-start.11 = (f32[2,32,3,384]{3,2,1,0:T(4,128)S(1)}, f32[2,32,3,384]{3,2,1,0:T(4,128)S(1)}, u32[]{:S(2)}, u32[]{:S(2)}) collective-permute-start(f32[2,32,3,384]{3,2,1,0:T(4,128)S(1)} %get-tuple-element.18), channel_id=1, source_target_pairs={{1,0},{2,1},{3,2},{4,3},{5,4},{6,5},{7,6},{0,7},{9,8},{10,9},{11,1... | collective-permute-start | bytes 884744 | tf_op jit(solution)/shard_map/ppermute | solution.py:22
  73.0 5.2 %collective-permute-done.10 = f32[2,32,3,384]{3,2,1,0:T(4,128)S(1)} collective-permute-done((f32[2,32,3,384]{3,2,1,0:T(4,128)S(1)}, f32[2,32,3,384]{3,2,1,0:T(4,128)S(1)}, u32[]{:S(2)}, u32[]{:S(2)}) %collective-permute-start.10) | collective-permute-done | bytes 294944 | tf_op jit(solution)/shard_map/ppermute | solution.py:19
  78.1 1.7 %collective-permute-done.11 = f32[2,32,3,384]{3,2,1,0:T(4,128)S(1)} collective-permute-done((f32[2,32,3,384]{3,2,1,0:T(4,128)S(1)}, f32[2,32,3,384]{3,2,1,0:T(4,128)S(1)}, u32[]{:S(2)}, u32[]{:S(2)}) %collective-permute-start.11) | collective-permute-done | bytes 294944 | tf_op jit(solution)/shard_map/ppermute | solution.py:22
  79.9 1.1 fusion.27
  82.7 1.9 %pad_maximum_fusion = f32[2,1024,384]{1,2,0:T(8,128)} fusion(f32[1,1024,384]{1,2,0:T(8,128)S(1)} %fusion.1, f32[1,1024,384]{1,2,0:T(8,128)S(1)} %fusion.2), kind=kLoop, calls=%fused_computation | loop fusion | flops 786432 | bytes 6291456 | tf_op jit(solution)/shard_map/stack | solution.py:121
  84.6 53.7 %reduce-scatter.2.cloned.1.call-done = f32[2,128,384]{1,2,0:T(8,128)} async-done(((f32[2,1024,384]{1,2,0:T(8,128)}), f32[2,128,384]{1,2,0:T(8,128)}) %reduce-scatter.2.cloned.1.call-update) | async-done | bytes 393232 | tf_op jit(solution)/shard_map/reduce_scatter | solution.py:122
  138.3 1.0 convert_element_type.61
  139.3 0.8 copy.42
  (51 shorter events, 6.3 us)
Async XLA Ops:
  6.5 27.0 %copy-start = (bf16[2,32,8,316]{3,2,1,0:T(8,128)(2,1)S(1)}, bf16[2,32,8,316]{3,2,1,0:T(8,128)(2,1)}, u32[]{:S(2)}) copy-start(bf16[2,32,8,316]{3,2,1,0:T(8,128)(2,1)} %param.14) | copy-start | bytes 970756
  6.5 11.6 %copy-start.5 = (bf16[2,1024,384]{2,1,0:T(8,128)(2,1)S(1)}, bf16[2,1024,384]{2,1,0:T(8,128)(2,1)}, u32[]{:S(2)}) copy-start(bf16[2,1024,384]{2,1,0:T(8,128)(2,1)} %param.9) | copy-start | bytes 4718596
  6.5 131.8 %reduce-scatter.2.cloned.1.call-start = ((), (), s32[]{:S(2)}) async-start(), calls=%async_computation.1 | async-start | bytes 3538944 | tf_op jit(solution)/shard_map/reduce_scatter | solution.py:122
  8.4 42.0 %collective-permute-start.3 = (s32[1,1,1,128]{3,2,1,0:T(1,128)S(1)}, s32[1,1,1,128]{3,2,1,0:T(1,128)S(1)}, u32[]{:S(2)}, u32[]{:S(2)}) collective-permute-start(s32[1,1,1,128]{3,2,1,0:T(1,128)S(1)} %fusion.112), channel_id=1, source_target_pairs={{16,0},{24,8},{32,16},{40,24},{48,32},{56,40},{64,48},{72,56},{80,... | collective-permute-start | bytes 1544 | tf_op jit(solution)/shard_map/ppermute | solution.py:30
  10.9 52.0 %collective-permute-start.9 = (s32[1,1,1,128]{3,2,1,0:T(1,128)S(1)}, s32[1,1,1,128]{3,2,1,0:T(1,128)S(1)}, u32[]{:S(2)}, u32[]{:S(2)}) collective-permute-start(s32[1,1,1,128]{3,2,1,0:T(1,128)S(1)} %fusion.115), channel_id=1, source_target_pairs={{0,16},{8,24},{16,32},{24,40},{32,48},{40,56},{48,64},{56,72},{64,... | collective-permute-start | bytes 1544 | tf_op jit(solution)/shard_map/ppermute | solution.py:30
  14.3 5.3 %copy-start.6 = (bf16[2,1024,32,8]{1,3,2,0:T(8,128)(2,1)S(1)}, bf16[2,1024,32,8]{1,3,2,0:T(8,128)(2,1)}, u32[]{:S(2)}) copy-start(bf16[2,1024,32,8]{1,3,2,0:T(8,128)(2,1)} %param.10) | copy-start | bytes 3145732
  14.3 44.2 %collective-permute-start.7 = (s32[1,1,1,128]{3,2,1,0:T(1,128)S(1)}, s32[1,1,1,128]{3,2,1,0:T(1,128)S(1)}, u32[]{:S(2)}, u32[]{:S(2)}) collective-permute-start(s32[1,1,1,128]{3,2,1,0:T(1,128)S(1)} %fusion.114), channel_id=1, source_target_pairs={{0,8},{8,16},{16,24},{24,32},{32,40},{40,48},{48,56},{56,64},{64,7... | collective-permute-start | bytes 1544 | tf_op jit(solution)/shard_map/ppermute | solution.py:30
  20.0 13.5 %copy-start.2 = (f32[7,8]{1,0:T(8,128)S(1)}, f32[7,8]{1,0:T(8,128)}, u32[]{:S(2)}) copy-start(f32[7,8]{1,0:T(8,128)} %param.11) | copy-start | bytes 676
  20.0 13.5 %copy-start.7 = (s32[640]{0:T(1024)S(1)}, s32[640]{0:T(1024)}, u32[]{:S(2)}) copy-start(s32[640]{0:T(1024)} %param.16) | copy-start | bytes 7684
  20.6 18.1 %collective-permute-start = (f32[2,32,3,384]{3,2,1,0:T(4,128)S(1)}, f32[2,32,3,384]{3,2,1,0:T(4,128)S(1)}, u32[]{:S(2)}, u32[]{:S(2)}) collective-permute-start(f32[2,32,3,384]{3,2,1,0:T(4,128)S(1)} %get-tuple-element.21), channel_id=1, source_target_pairs={{0,1},{1,2},{2,3},{3,4},{4,5},{5,6},{6,7},{7,0},{8,9},{9,10},{10,1... | collective-permute-start | bytes 884744 | tf_op jit(solution)/shard_map/ppermute | solution.py:19
  24.9 18.5 %collective-permute-start.1 = (f32[2,32,3,384]{3,2,1,0:T(4,128)S(1)}, f32[2,32,3,384]{3,2,1,0:T(4,128)S(1)}, u32[]{:S(2)}, u32[]{:S(2)}) collective-permute-start(f32[2,32,3,384]{3,2,1,0:T(4,128)S(1)} %get-tuple-element.22), channel_id=1, source_target_pairs={{1,0},{2,1},{3,2},{4,3},{5,4},{6,5},{7,6},{0,7},{9,8},{10,9},{11,1... | collective-permute-start | bytes 884744 | tf_op jit(solution)/shard_map/ppermute | solution.py:22
  38.7 24.5 %collective-permute-start.5 = (s32[1,1,1,128]{3,2,1,0:T(1,128)S(1)}, s32[1,1,1,128]{3,2,1,0:T(1,128)S(1)}, u32[]{:S(2)}, u32[]{:S(2)}) collective-permute-start(s32[1,1,1,128]{3,2,1,0:T(1,128)S(1)} %fusion.113), channel_id=1, source_target_pairs={{8,0},{16,8},{24,16},{32,24},{40,32},{48,40},{56,48},{64,56},{72,6... | collective-permute-start | bytes 1544 | tf_op jit(solution)/shard_map/ppermute | solution.py:30
  43.7 0.7 copy-start.1
  47.4 8.9 %collective-permute-start.2 = (bf16[2,32,8,128]{3,1,2,0:T(8,128)(2,1)S(1)}, bf16[2,32,8,128]{3,1,2,0:T(8,128)(2,1)S(1)}, u32[]{:S(2)}, u32[]{:S(2)}) collective-permute-start(bf16[2,32,8,128]{3,1,2,0:T(8,128)(2,1)S(1)} %convolution_convert_fusion.3), channel_id=1, source_target_pairs={{16,0},{24,8},{32,16},{40,24},{48,32},{56,40},{64,48},{72,56},{80,... | collective-permute-start | bytes 393224 | tf_op jit(solution)/shard_map/ppermute | solution.py:30
  50.4 12.4 %collective-permute-start.8 = (bf16[2,32,8,128]{3,1,2,0:T(8,128)(2,1)S(1)}, bf16[2,32,8,128]{3,1,2,0:T(8,128)(2,1)S(1)}, u32[]{:S(2)}, u32[]{:S(2)}) collective-permute-start(bf16[2,32,8,128]{3,1,2,0:T(8,128)(2,1)S(1)} %convolution_convert_fusion), channel_id=1, source_target_pairs={{0,16},{8,24},{16,32},{24,40},{32,48},{40,56},{48,64},{56,72},{64,... | collective-permute-start | bytes 393224 | tf_op jit(solution)/shard_map/ppermute | solution.py:30
  56.2 6.3 %collective-permute-start.6 = (bf16[2,32,8,128]{3,1,2,0:T(8,128)(2,1)S(1)}, bf16[2,32,8,128]{3,1,2,0:T(8,128)(2,1)S(1)}, u32[]{:S(2)}, u32[]{:S(2)}) collective-permute-start(bf16[2,32,8,128]{3,1,2,0:T(8,128)(2,1)S(1)} %convolution_convert_fusion.1), channel_id=1, source_target_pairs={{0,8},{8,16},{16,24},{24,32},{32,40},{40,48},{48,56},{56,64},{64,7... | collective-permute-start | bytes 393224 | tf_op jit(solution)/shard_map/ppermute | solution.py:30
  58.5 6.7 %collective-permute-start.4 = (bf16[2,32,8,128]{3,1,2,0:T(8,128)(2,1)S(1)}, bf16[2,32,8,128]{3,1,2,0:T(8,128)(2,1)S(1)}, u32[]{:S(2)}, u32[]{:S(2)}) collective-permute-start(bf16[2,32,8,128]{3,1,2,0:T(8,128)(2,1)S(1)} %convolution_convert_fusion.2), channel_id=1, source_target_pairs={{8,0},{16,8},{24,16},{32,24},{40,32},{48,40},{56,48},{64,56},{72,6... | collective-permute-start | bytes 393224 | tf_op jit(solution)/shard_map/ppermute | solution.py:30
  65.5 7.4 %copy-start.3 = (f32[7,8]{1,0:T(8,128)S(1)}, f32[7,8]{1,0:T(8,128)}, u32[]{:S(2)}) copy-start(f32[7,8]{1,0:T(8,128)} %param.12) | copy-start | bytes 676
  65.6 14.3 %copy-start.4 = (f32[32]{0:T(128)S(1)}, f32[32]{0:T(128)}, u32[]{:S(2)}) copy-start(f32[32]{0:T(128)} %param.13) | copy-start | bytes 388
  65.7 12.5 %collective-permute-start.10 = (f32[2,32,3,384]{3,2,1,0:T(4,128)S(1)}, f32[2,32,3,384]{3,2,1,0:T(4,128)S(1)}, u32[]{:S(2)}, u32[]{:S(2)}) collective-permute-start(f32[2,32,3,384]{3,2,1,0:T(4,128)S(1)} %get-tuple-element.17), channel_id=1, source_target_pairs={{0,1},{1,2},{2,3},{3,4},{4,5},{5,6},{6,7},{7,0},{8,9},{9,10},{10,1... | collective-permute-start | bytes 884744 | tf_op jit(solution)/shard_map/ppermute | solution.py:19
  67.6 12.3 %collective-permute-start.11 = (f32[2,32,3,384]{3,2,1,0:T(4,128)S(1)}, f32[2,32,3,384]{3,2,1,0:T(4,128)S(1)}, u32[]{:S(2)}, u32[]{:S(2)}) collective-permute-start(f32[2,32,3,384]{3,2,1,0:T(4,128)S(1)} %get-tuple-element.18), channel_id=1, source_target_pairs={{1,0},{2,1},{3,2},{4,3},{5,4},{6,5},{7,6},{0,7},{9,8},{10,9},{11,1... | collective-permute-start | bytes 884744 | tf_op jit(solution)/shard_map/ppermute | solution.py:22
Sparse Core Ops, SparseCore 0:
  84.7 53.5 reduce-scatter.1
where the time goes:
time: 148 us; the launch traced here: 147 us
  waiting for transfers between devices  68.7 us (46%)
  starting transfers between devices  44.8 us (30%)
  between operations  13.9 us (9%)
  matrix products  11.7 us (8%)
  other arithmetic  6.91 us (5%)
    reduce_scatter x1, waiting for transfers between devices, on_device(): lax.psum_scatter(terms, 'samp', scatter_dimension=1, tiled=True)  53.7 us
    ppermute x8, starting transfers between devices, from_behind(): lax.ppermute(value, axis, [(source, source + steps) for source in range(l...  24.7 us
    ppermute x2, starting transfers between devices, extended(): lax.ppermute(lax.slice_in_dim(block, 0, width, axis=dim), axis, backward)  13.9 us
    ppermute x2, waiting for transfers between devices, extended(): lax.ppermute(lax.slice_in_dim(block, block.shape[dim] - width, None, axis...  9.78 us
    ppermute x2, starting transfers between devices, extended(): lax.ppermute(lax.slice_in_dim(block, block.shape[dim] - width, None, axis...  6.2 us
    dot_general x11, matrix products, select_last(): lax.dot_general(values, table, (((3,), (0,)), ((), ())), precision=precis...  5.63 us
    dot_general x4, matrix products, contract_first(): lax.dot_general(left, right, (((0,), (0,)), ((), ())), preferred_element_...  4.07 us
    ppermute x8, waiting for transfers between devices, from_behind(): lax.ppermute(value, axis, [(source, source + steps) for source in range(l...  3.45 us
  transfers between devices with their start and end apart: 13, of which 7 were waited for; matrix products, arithmetic and copies ran while one was open for 7% of the time, Pallas kernels for 0%

commit v1 on v0

v1 whole, which is shorter than its diff:
```python
import functools

import jax
import jax.numpy as jnp
from jax import lax
from jax.experimental import pallas as pl
from jax.experimental.pallas import tpu as pltpu
from jax.sharding import PartitionSpec as P

NT = 32
FD = 8
NS = NT * FD
EDGE = 3 * NT
P_SIZE = 1024
NOPS = 316
WIDTH = 3
BOX = 384
PAIR = 640
CAP = 128
STEPS = (1, -1, 2, -2)
SLOTS = CAP * len(STEPS)
BUF = 2 * NS + 16
RANKS = 8
BF = jnp.bfloat16
F32 = jnp.float32

NN = (((1,), (0,)), ((), ()))
NTR = (((1,), (1,)), ((), ()))
TN = (((0,), (0,)), ((), ()))


def dot(a, b, dims=NN):
    return lax.dot_general(a, b, dims, preferred_element_type=F32)


def iota(shape, dim):
    return lax.broadcasted_iota(jnp.int32, shape, dim)


def split(value):
    high = value.astype(BF)
    return high, (value - high.astype(F32)).astype(BF)


def local_place(shape, dim):
    at = iota(shape, dim)
    return at >> 3, at & 7


def edge_place(shape, dim):
    at = iota(shape, dim)
    return at & 31, at >> 5


def band(columns, diff, same):
    total = jnp.zeros(diff.shape, F32)
    for k in range(2 * WIDTH + 1):
        total = jnp.where(diff == k, columns[:, k : k + 1], total)
    return jnp.where(same, total, 0.0)


def one_hot(rows, index):
    return (iota((rows, index.shape[1]), 0) == index).astype(BF)


def field_kernel(rad, cur, field, low, high, total):
    step = pl.program_id(0)
    re, im = cur[0], cur[1]
    part = dot(rad[0], jnp.concatenate([re, im], axis=1))
    part = part + dot(rad[1], jnp.concatenate([-im, re], axis=1))

    @pl.when(step == 0)
    def _():
        total[...] = part

    @pl.when(step > 0)
    def _():
        total[...] = total[...] + part

    @pl.when(step == pl.num_programs(0) - 1)
    def _():
        whole = total[...]
        field[...] = whole
        rounded = whole.astype(BF)
        t_row, j_row = edge_place((EDGE, NS), 0)
        t_col, f_col = local_place((EDGE, NS), 1)
        same = t_row == t_col
        low[...] = dot(jnp.logical_and(same, f_col == j_row).astype(BF), rounded).astype(BF)
        high[...] = dot(jnp.logical_and(same, f_col == j_row + FD - WIDTH).astype(BF), rounded).astype(BF)


def prepare_kernel(
    field, interp_cols, anterp_cols, rad, digits, offset, oper, op_row,
    inter, halo_mat, src_pick, oper_slot, slot_ids, oper_own, q_up, q_down,
):
    shape = (NS, NS)
    t_row, g_row = local_place(shape, 0)
    t_col, f_col = local_place(shape, 1)
    mat_hi, mat_lo = split(band(interp_cols[...], f_col - g_row + WIDTH, t_row == t_col))
    f_hi, f_lo = split(field[...])
    inter[...] = dot(mat_hi, f_hi) + dot(mat_lo, f_hi) + dot(mat_hi, f_lo)
    shape = (NS, EDGE)
    t_row, g_row = local_place(shape, 0)
    t_col, j_col = edge_place(shape, 1)
    same = t_row == t_col
    below = split(band(interp_cols[...], j_col - g_row, same))
    above = split(band(interp_cols[...], j_col - g_row + FD + WIDTH, same))
    for part in range(2):
        halo_mat[part, 0] = below[part]
        halo_mat[part, 1] = above[part]

    step_of = offset[...]
    at = iota((8, PAIR), 0)
    cls = jnp.full((1, PAIR), -1, jnp.int32)
    for k, step in enumerate(STEPS):
        cls = jnp.where(step_of == step, k, cls)
    member = (at == cls).astype(BF)
    earlier = (iota((PAIR, PAIR), 0) < iota((PAIR, PAIR), 1)).astype(BF)
    before = dot(member, earlier) * member.astype(F32)
    rank = jnp.sum(before, axis=0, keepdims=True).astype(jnp.int32)
    slot = jnp.where(cls >= 0, cls * CAP + rank, -1)
    chosen = (iota((SLOTS, PAIR), 0) == slot).astype(BF)
    named = dot(digits[...], chosen, NTR)
    src = (16.0 * named[0:1] + named[1:2]).astype(jnp.int32)
    opn = (16.0 * named[2:3] + named[3:4]).astype(jnp.int32)
    filled = named[6:7] > 0.5
    src_pick[...] = one_hot(BOX, src)
    oper_slot[...] = dot(oper[...], one_hot(NOPS, opn)).astype(BF)
    oper_own[...] = dot(oper[...], one_hot(NOPS, op_row[...])).astype(BF)
    row = iota((16, SLOTS), 0)
    t_hi = jnp.where(filled, named[4:5], float(BOX // 16))
    t_lo = jnp.where(filled, named[5:6], 0.0)
    slot_ids[...] = jnp.where(row == 0, t_hi, jnp.where(row == 1, t_lo, 0.0)).astype(BF)

    shape = (NS, EDGE)
    t_row, f_row = local_place(shape, 0)
    t_col, j_col = edge_place(shape, 1)
    same = t_row == t_col
    up = split(band(anterp_cols[...], FD + j_col - f_row + WIDTH, same))
    down = split(band(anterp_cols[...], j_col - f_row, same))
    for c in range(2):
        cols = pl.ds(c * P_SIZE, P_SIZE)
        q_up[:, cols] = (dot(up[0], rad[c], TN) + dot(up[1], rad[c], TN)).astype(BF)
        q_down[:, cols] = (dot(down[0], rad[c], TN) + dot(down[1], rad[c], TN)).astype(BF)


def multiply(oper, re, im):
    o_re, o_im = oper[:NS, :].astype(F32), oper[NS:, :].astype(F32)
    return (o_re * re - o_im * im).astype(BF), (o_re * im + o_im * re).astype(BF)


def send_kernel(inter, halo_mat, below, above, src_pick, oper_slot, slot_ids, out0, out1, out2, out3, parts):
    whole = inter[...]
    for part in range(2):
        whole = whole + dot(halo_mat[part, 0], below[...]) + dot(halo_mat[part, 1], above[...])
    hi, lo = split(whole)
    parts[0] = hi
    parts[1] = lo
    pick = src_pick[...]
    re = dot(hi[:, :BOX], pick) + dot(lo[:, :BOX], pick)
    im = dot(hi[:, BOX:], pick) + dot(lo[:, BOX:], pick)
    c_re, c_im = multiply(oper_slot[...], re, im)
    for k, out in enumerate((out0, out1, out2, out3)):
        cols = slice(k * CAP, (k + 1) * CAP)
        out[0:NS, :] = c_re[:, cols]
        out[NS : 2 * NS, :] = c_im[:, cols]
        out[2 * NS :, :] = slot_ids[:, cols]


def own_kernel(parts, src_row, oper_own, target_row, own):
    pick = one_hot(BOX, src_row[...])
    hi, lo = parts[0], parts[1]
    re = dot(hi[:, :BOX], pick) + dot(lo[:, :BOX], pick)
    im = dot(hi[:, BOX:], pick) + dot(lo[:, BOX:], pick)
    c_re, c_im = multiply(oper_own[...], re, im)
    table = one_hot(BOX, target_row[...])
    own[:, :BOX] = dot(c_re, table, NTR)
    own[:, BOX:] = dot(c_im, table, NTR)


def matrix_kernel(rad, anterp_cols, q_below, q_above, out):
    shape = (NS, NS)
    t_row, f_row = local_place(shape, 0)
    t_col, g_col = local_place(shape, 1)
    mat_hi, mat_lo = split(band(anterp_cols[...], g_col - f_row + WIDTH, t_row == t_col))
    shape = (EDGE, NS)
    t_row, j_row = edge_place(shape, 0)
    t_col, g_col = local_place(shape, 1)
    same = t_row == t_col
    first = jnp.logical_and(same, g_col == j_row).astype(BF)
    last = jnp.logical_and(same, g_col == j_row + FD - WIDTH).astype(BF)
    for c in range(2):
        r = rad[c]
        cols = pl.ds(c * P_SIZE, P_SIZE)
        q = dot(r, mat_hi, TN) + dot(r, mat_lo, TN)
        q = q + dot(q_below[:, cols], first, TN) + dot(q_above[:, cols], last, TN)
        out[:, c * NS : (c + 1) * NS] = q.astype(BF)


def receive_kernel(own, matrix, got0, got1, got2, got3, out, stack):
    gots = (got0, got1, got2, got3)
    ids = jnp.concatenate([g[2 * NS :, :].astype(F32) for g in gots], axis=1)
    index = (16.0 * ids[0:1] + ids[1:2]).astype(jnp.int32)
    table = one_hot(BOX, index)
    re = own[:, :BOX] + dot(jnp.concatenate([g[0:NS, :] for g in gots], axis=1), table, NTR)
    im = own[:, BOX:] + dot(jnp.concatenate([g[NS : 2 * NS, :] for g in gots], axis=1), table, NTR)
    re, im = re.astype(BF), im.astype(BF)
    stack[0:NS, :BOX] = re
    stack[0:NS, BOX:] = im
    stack[NS:, :BOX] = im
    stack[NS:, BOX:] = -re

    @pl.loop(0, RANKS)
    def _(d):
        rows = pl.ds(pl.multiple_of(d * CAP, CAP), CAP)
        out[d] = dot(matrix[rows, :], stack[...]).astype(BF)


def sum_kernel(parts, out):
    total = parts[0].astype(F32)
    for d in range(1, RANKS):
        total = total + parts[d].astype(F32)
    out[0] = total[:, :BOX].astype(BF)
    out[1] = total[:, BOX:].astype(BF)


def call(kernel, outs, *args, scratch=(), flops=10**8, name=None, **kw):
    shapes = [jax.ShapeDtypeStruct(s, d) for s, d in outs]
    moved = sum(a.size * a.dtype.itemsize for a in args) + sum(s.size * s.dtype.itemsize for s in shapes)
    return pl.pallas_call(
        kernel,
        out_shape=shapes,
        scratch_shapes=list(scratch),
        compiler_params=pltpu.CompilerParams(vmem_limit_bytes=48 * 2**20),
        cost_estimate=pl.CostEstimate(flops=flops, bytes_accessed=moved, transcendentals=0),
        name=name,
        **kw,
    )(*args)


def around(value, axis, steps):
    count = lax.axis_size(axis)
    return lax.ppermute(value, axis, [(i, (i + steps) % count) for i in range(count)])


def along(value, axis, steps):
    count = lax.axis_size(axis)
    pairs = [(i, i + steps) for i in range(count) if 0 <= i + steps < count]
    return lax.ppermute(value, axis, pairs)


def digit_rows(values):
    return [values // 16, values % 16]


def on_device(
    currents, radiation, interp, anterp, weights, operators, pair_src, pair_op, pair_target
):
    rad = jnp.transpose(radiation, (0, 2, 3, 1)).reshape(2, NS, P_SIZE)
    oper = operators.reshape(2 * NS, NOPS)
    interp_cols = jnp.tile(interp.T, (NT, 1))
    anterp_cols = (weights[:, None, None] * anterp.T[None]).reshape(NS, 2 * WIDTH + 1)
    owner = pair_target // BOX
    target = pair_target - owner * BOX
    offset = owner - lax.axis_index("box")
    digits = jnp.stack(
        digit_rows(pair_src) + digit_rows(pair_op) + digit_rows(target)
        + [jnp.ones_like(target), jnp.zeros_like(target)]
    ).astype(BF)
    own_target = jnp.where(offset == 0, target, -1).reshape(1, PAIR)

    blocks = 4
    depth = P_SIZE // blocks
    whole = lambda r, c: pl.BlockSpec((r, c), lambda i: (0, 0))
    field, low, high = call(
        field_kernel,
        [((NS, 2 * BOX), F32), ((EDGE, 2 * BOX), BF), ((EDGE, 2 * BOX), BF)],
        rad, currents,
        scratch=[pltpu.VMEM((NS, 2 * BOX), F32)],
        flops=10**9,
        name="field",
        grid=(blocks,),
        in_specs=[
            pl.BlockSpec((2, NS, depth), lambda i: (0, 0, i)),
            pl.BlockSpec((2, depth, BOX), lambda i: (0, i, 0)),
        ],
        out_specs=[whole(NS, 2 * BOX), whole(EDGE, 2 * BOX), whole(EDGE, 2 * BOX)],
    )
    below = around(high, "samp", 1)
    above = around(low, "samp", -1)
    inter, halo_mat, src_pick, oper_slot, slot_ids, oper_own, q_up, q_down = call(
        prepare_kernel,
        [
            ((NS, 2 * BOX), F32), ((2, 2, NS, EDGE), BF), ((BOX, SLOTS), BF),
            ((2 * NS, SLOTS), BF), ((16, SLOTS), BF), ((2 * NS, PAIR), BF),
            ((EDGE, 2 * P_SIZE), BF), ((EDGE, 2 * P_SIZE), BF),
        ],
        field, interp_cols, anterp_cols, rad, digits, offset.reshape(1, PAIR), oper,
        pair_op.reshape(1, PAIR),
        flops=2 * 10**9,
        name="prepare",
    )
    *buffers, parts = call(
        send_kernel,
        [((BUF, CAP), BF)] * 4 + [((2, NS, 2 * BOX), BF)],
        inter, halo_mat, below, above, src_pick, oper_slot, slot_ids,
        name="send",
    )
    gots = [along(b, "box", step) for b, step in zip(buffers, STEPS)]
    q_up, q_down = lax.optimization_barrier((q_up, q_down, parts))[:2]
    q_below = around(q_up, "samp", 1)
    q_above = around(q_down, "samp", -1)
    (own,) = call(
        own_kernel,
        [((NS, 2 * BOX), F32)],
        parts, pair_src.reshape(1, PAIR), oper_own, own_target,
        flops=10**9,
        name="own",
    )
    (matrix,) = call(
        matrix_kernel,
        [((P_SIZE, 2 * NS), BF)],
        rad, anterp_cols, q_below, q_above,
        flops=10**9,
        name="matrix",
    )
    (terms,) = call(
        receive_kernel,
        [((RANKS, CAP, 2 * BOX), BF)],
        own, matrix, *gots,
        scratch=[pltpu.VMEM((2 * NS, 2 * BOX), BF)],
        flops=10**9,
        name="receive",
    )
    terms = lax.all_to_all(terms, "samp", 0, 0)
    (out,) = call(sum_kernel, [((2, P_SIZE // RANKS, BOX), BF)], terms, name="total")
    return out


def solution(mesh):
    return jax.shard_map(
        on_device,
        mesh=mesh,
        in_specs=(
            P(None, None, "box"),
            P(None, None, None, "samp"),
            P(None, "samp"),
            P(None, "samp"),
            P(),
            P(None, None, "samp", None),
            P("box"),
            P("box"),
            P("box"),
        ),
        out_specs=P(None, "samp", "box"),
        check_vma=False,
    )
```

time: 148 us -> 97.3 us (0.66)
  the two profiles are of different devices: /device:TPU:4 before, /device:TPU:30 now
where the time goes in v1:
time: 97.3 us; the launch traced here: 97 us
  blocking collectives  39.5 us (41%)
  starting transfers between devices  35.3 us (36%)
  Pallas kernels  13.5 us (14%)
  waiting for transfers between devices  4.99 us (5%)
  local copies, waits for them, and re-layouts  3.1 us (3%)
    all_to_all x1, blocking collectives, on_device(): terms = lax.all_to_all(terms, 'samp', 0, 0)  39.5 us
    ppermute x4, starting transfers between devices, around(): lax.ppermute(value, axis, [(i, (i + steps) % count) for i in range(count)])  19.9 us
    ppermute x4, starting transfers between devices, along(): return lax.ppermute(value, axis, pairs)  15.4 us
    pallas_call x7, Pallas kernels, call(): pl.pallas_call(kernel, out_shape=shapes, scratch_shapes=list(scratch), co...  13.5 us
    ppermute x4, waiting for transfers between devices, along(): return lax.ppermute(value, axis, pairs)  4.98 us
    unnamed x20, local copies, waits for them, and re-layouts  2.66 us
  transfers between devices with their start and end apart: 8, of which 1 were waited for; matrix products, arithmetic and copies ran while one was open for 1% of the time, Pallas kernels for 6%

profile of v1, /device:TPU:30, one launch (start us, length us, event | category | flops | bytes accessed | tf_op | source)
XLA Modules:
  0.0 97.0 jit_solution(17464837671622404340)
XLA Ops:
  0.0 1.4 %copy-done = bf16[2,1024,384]{2,1,0:T(8,128)(2,1)S(1)} copy-done((bf16[2,1024,384]{2,1,0:T(8,128)(2,1)S(1)}, bf16[2,1024,384]{2,1,0:T(8,128)(2,1)}, u32[]{:S(2)}) %copy-start) | copy-done | bytes 1572888
  1.4 1.2 %copy-done.1 = bf16[2,1024,32,8]{1,3,2,0:T(8,128)(2,1)S(1)} copy-done((bf16[2,1024,32,8]{1,3,2,0:T(8,128)(2,1)S(1)}, bf16[2,1024,32,8]{1,3,2,0:T(8,128)(2,1)}, u32[]{:S(2)}) %copy-start.1) | copy-done | bytes 1048600
  2.7 2.4 %field.1 = (f32[256,768]{1,0:T(8,128)S(1)}, bf16[96,768]{1,0:T(8,128)(2,1)S(1)}, bf16[96,768]{1,0:T(8,128)(2,1)S(1)}) custom-call(bf16[2,256,1024]{2,1,0:T(8,128)(2,1)S(1)} %bitcast.10, bf16[2,1024,384]{2,1,0:T(8,128)(2,1)S(1)} %copy-done), custom_call_target="tpu_custom_call" | custom-call | flops 1000000000 | bytes 3702784 | tf_op jit(solution)/shard_map/field/pallas_call | solution.py:230
  5.1 4.3 %collective-permute-start = (bf16[96,768]{1,0:T(8,128)(2,1)S(1)}, bf16[96,768]{1,0:T(8,128)(2,1)S(1)}, u32[]{:S(2)}, u32[]{:S(2)}) collective-permute-start(bf16[96,768]{1,0:T(8,128)(2,1)S(1)} %get-tuple-element.26), channel_id=1, source_target_pairs={{0,1},{1,2},{2,3},{3,4},{4,5},{5,6},{6,7},{7,0},{8,9},{9,10},{10,1... | collective-permute-start | bytes 442376 | tf_op jit(solution)/shard_map/ppermute | solution.py:243
  9.4 8.6 %collective-permute-start.1 = (bf16[96,768]{1,0:T(8,128)(2,1)S(1)}, bf16[96,768]{1,0:T(8,128)(2,1)S(1)}, u32[]{:S(2)}, u32[]{:S(2)}) collective-permute-start(bf16[96,768]{1,0:T(8,128)(2,1)S(1)} %get-tuple-element.27), channel_id=1, source_target_pairs={{0,7},{1,0},{2,1},{3,2},{4,3},{5,4},{6,5},{7,6},{8,15},{9,8},{10,9... | collective-permute-start | bytes 442376 | tf_op jit(solution)/shard_map/ppermute | solution.py:243
  18.2 0.1 mul.24
  18.3 0.1 mul.25
  18.4 0.1 copy.13
  18.5 0.1 copy.12
  18.6 0.1 bitcast_multiply_fusion.anterp_cols
  18.7 0.1 stack.34.digits
  18.8 3.0 %prepare.1 = (f32[256,768]{1,0:T(8,128)S(1)}, bf16[2,2,256,96]{3,2,1,0:T(8,128)(2,1)S(1)}, bf16[384,512]{1,0:T(8,128)(2,1)S(1)}, bf16[512,512]{1,0:T(8,128)(2,1)...) custom-call(f32[256,768]{1,0:T(8,128)S(1)} %get-tuple-element.23.fie, ...), custom_call_target="tpu_custom_call" | custom-call | flops 2000000000 | bytes 5547008 | tf_op jit(solution)/shard_map/prepare/pallas_call | solution.py:230
  21.8 0.0 collective-permute-done.below
  21.8 0.0 collective-permute-done.1.above
  21.8 1.2 %send.1 = (bf16[528,128]{1,0:T(8,128)(2,1)S(1)}, bf16[528,128]{1,0:T(8,128)(2,1)S(1)}, bf16[528,128]{1,0:T(8,128)(2,1)S(1)}, bf16[528,128]{1,0:T(8,128)(2,1)S(1)}, bf16[2,256,768]{2,1,0:T(8,128)(2,1)S(1)}) custom-call(f32[256,768]{1,0:T(8,128)S(1)} %get-tuple-element.24.inter, bf16[2,2,256,96]{3,2,1,0:T(8,128)(2,1)S(1)} %get-tuple-element.25.halo_mat, ...), custom_call_target="tpu_custom_call" | custom-call | flops 100000000 | bytes 3538944 | tf_op jit(solution)/shard_map/send/pallas_call | solution.py:230
  23.0 1.9 %collective-permute-start.2 = (bf16[96,2048]{1,0:T(8,128)(2,1)S(1)}, bf16[96,2048]{1,0:T(8,128)(2,1)S(1)}, u32[]{:S(2)}, u32[]{:S(2)}) collective-permute-start(bf16[96,2048]{1,0:T(8,128)(2,1)S(1)} %get-tuple-element.35), channel_id=1, source_target_pairs={{0,1},{1,2},{2,3},{3,4},{4,5},{5,6},{6,7},{7,0},{8,9},{9,10},{10,1... | collective-permute-start | bytes 1179656 | tf_op jit(solution)/shard_map/ppermute | solution.py:243
  25.0 5.1 %collective-permute-start.3 = (bf16[96,2048]{1,0:T(8,128)(2,1)S(1)}, bf16[96,2048]{1,0:T(8,128)(2,1)S(1)}, u32[]{:S(2)}, u32[]{:S(2)}) collective-permute-start(bf16[96,2048]{1,0:T(8,128)(2,1)S(1)} %get-tuple-element.36), channel_id=1, source_target_pairs={{0,7},{1,0},{2,1},{3,2},{4,3},{5,4},{6,5},{7,6},{8,15},{9,8},{10,9... | collective-permute-start | bytes 1179656 | tf_op jit(solution)/shard_map/ppermute | solution.py:243
  30.1 1.9 %collective-permute-start.4 = (bf16[528,128]{1,0:T(8,128)(2,1)S(1)}, bf16[528,128]{1,0:T(8,128)(2,1)S(1)}, u32[]{:S(2)}, u32[]{:S(2)}) collective-permute-start(bf16[528,128]{1,0:T(8,128)(2,1)S(1)} %get-tuple-element.37), channel_id=1, source_target_pairs={{0,8},{8,16},{16,24},{24,32},{32,40},{40,48},{48,56},{56,64},{64,7... | collective-permute-start | bytes 405512 | tf_op jit(solution)/shard_map/ppermute | solution.py:249
  32.1 3.6 %collective-permute-start.5 = (bf16[528,128]{1,0:T(8,128)(2,1)S(1)}, bf16[528,128]{1,0:T(8,128)(2,1)S(1)}, u32[]{:S(2)}, u32[]{:S(2)}) collective-permute-start(bf16[528,128]{1,0:T(8,128)(2,1)S(1)} %get-tuple-element.38), channel_id=1, source_target_pairs={{8,0},{16,8},{24,16},{32,24},{40,32},{48,40},{56,48},{64,56},{72,6... | collective-permute-start | bytes 405512 | tf_op jit(solution)/shard_map/ppermute | solution.py:249
  35.7 7.9 %collective-permute-start.6 = (bf16[528,128]{1,0:T(8,128)(2,1)S(1)}, bf16[528,128]{1,0:T(8,128)(2,1)S(1)}, u32[]{:S(2)}, u32[]{:S(2)}) collective-permute-start(bf16[528,128]{1,0:T(8,128)(2,1)S(1)} %get-tuple-element.39), channel_id=1, source_target_pairs={{0,16},{8,24},{16,32},{24,40},{32,48},{40,56},{48,64},{56,72},{64,... | collective-permute-start | bytes 405512 | tf_op jit(solution)/shard_map/ppermute | solution.py:249
  43.7 0.0 collective-permute-done.2.q_below
  43.7 1.9 %collective-permute-start.7 = (bf16[528,128]{1,0:T(8,128)(2,1)S(1)}, bf16[528,128]{1,0:T(8,128)(2,1)S(1)}, u32[]{:S(2)}, u32[]{:S(2)}) collective-permute-start(bf16[528,128]{1,0:T(8,128)(2,1)S(1)} %get-tuple-element.40), channel_id=1, source_target_pairs={{16,0},{24,8},{32,16},{40,24},{48,32},{56,40},{64,48},{72,56},{80,... | collective-permute-start | bytes 405512 | tf_op jit(solution)/shard_map/ppermute | solution.py:249
  45.6 1.6 %own.1 = f32[256,768]{1,0:T(8,128)S(1)} custom-call(bf16[2,256,768]{2,1,0:T(8,128)(2,1)S(1)} %get-tuple-element.31.parts, s32[1,640]{1,0:T(1,128)S(1)} %reshape.31.src_row, bf16[512,640]{1,0:T(8,128)(2,1)S(1)} %get-tuple-element.32.oper_own, s32[1,640]{1,0:T(1,128)S(1)} %reshape.32.target_row), custom_call_target="tpu_custom_call" | custom-call | flops 1000000000 | bytes 2233344 | tf_op jit(solution)/shard_map/own/pallas_call | solution.py:230
  47.2 0.0 collective-permute-done.3.q_above
  47.2 1.7 %matrix.1 = bf16[1024,512]{1,0:T(8,128)(2,1)S(1)} custom-call(bf16[2,256,1024]{2,1,0:T(8,128)(2,1)S(1)} %bitcast.12, f32[256,7]{1,0:T(8,128)S(1)} %bitcast_multiply_fusion.anterp_cols, bf16[96,2048]{1,0:T(8,128)(2,1)S(1)} %collective-permute-done.2.q_below, bf16[96,2048]{1,0:T(8,128)(2,1)S(1)} %collective-permute-done.3.q_above), custom_call_target="tpu_custom_call" | custom-call | flops 1000000000 | bytes 2890752 | tf_op jit(solution)/shard_map/matrix/pallas_call | solution.py:230
  48.9 0.0 collective-permute-done.4.got0
  48.9 0.0 collective-permute-done.5.got1
  48.9 0.0 collective-permute-done.6.got2
  48.9 5.0 %collective-permute-done.7.got3 = bf16[528,128]{1,0:T(8,128)(2,1)S(1)} collective-permute-done((bf16[528,128]{1,0:T(8,128)(2,1)S(1)}, bf16[528,128]{1,0:T(8,128)(2,1)S(1)}, u32[]{:S(2)}, u32[]{:S(2)}) %collective-permute-start.7) | collective-permute-done | bytes 135200 | tf_op jit(solution)/shard_map/ppermute | solution.py:249
  53.9 2.7 %receive.1 = bf16[8,128,768]{2,1,0:T(8,128)(2,1)S(1)} custom-call(f32[256,768]{1,0:T(8,128)S(1)} %own.1, bf16[1024,512]{1,0:T(8,128)(2,1)S(1)} %matrix.1, bf16[528,128]{1,0:T(8,128)(2,1)S(1)} %collective-permute-done.4.got0, bf16[528,128]{1,0:T(8,128)(2,1)S(1)} %collective-permute-done.5.got1, bf16[528,128]{1,0:T(8,128)(2,1)S(1)} %collective-permute-done.6.got2, ...), custom_call_target="tpu_custom_call" | custom-call | flops 1000000000 | bytes 3948544 | tf_op jit(solution)/shard_map/receive/pallas_call | solution.py:230
  56.6 39.5 %all_to_all.5.parts = bf16[8,128,768]{2,1,0:T(8,128)(2,1)S(1)} all-to-all(bf16[8,128,768]{2,1,0:T(8,128)(2,1)S(1)} %receive.1), channel_id=1, replica_groups=mesh['box'=64,'samp'=8] {'samp'}, dimensions={0} | all-to-all | bytes 3145728 | tf_op jit(solution)/shard_map/all_to_all | solution.py:335
  96.1 0.9 total.1
  (34 shorter events, 0.2 us)
Async XLA Ops:
  0.0 1.4 %copy-start = (bf16[2,1024,384]{2,1,0:T(8,128)(2,1)S(1)}, bf16[2,1024,384]{2,1,0:T(8,128)(2,1)}, u32[]{:S(2)}) copy-start(bf16[2,1024,384]{2,1,0:T(8,128)(2,1)} %cur.1) | copy-start | bytes 4718596
  1.4 1.2 %copy-start.1 = (bf16[2,1024,32,8]{1,3,2,0:T(8,128)(2,1)S(1)}, bf16[2,1024,32,8]{1,3,2,0:T(8,128)(2,1)}, u32[]{:S(2)}) copy-start(bf16[2,1024,32,8]{1,3,2,0:T(8,128)(2,1)} %param.10) | copy-start | bytes 3145732
  2.6 15.4 %copy-start.4 = (s32[640]{0:T(1024)S(1)}, s32[640]{0:T(1024)}, u32[]{:S(2)}) copy-start(s32[640]{0:T(1024)} %param.16) | copy-start | bytes 7684
  2.6 15.4 %copy-start.8 = (s32[640]{0:T(1024)S(1)}, s32[640]{0:T(1024)}, u32[]{:S(2)}) copy-start(s32[640]{0:T(1024)} %param.17) | copy-start | bytes 7684
  2.6 15.5 %copy-start.5 = (s32[640]{0:T(1024)S(1)}, s32[640]{0:T(1024)}, u32[]{:S(2)}) copy-start(s32[640]{0:T(1024)} %param.15) | copy-start | bytes 7684
  2.6 15.6 %copy-start.9 = (f32[32]{0:T(128)S(1)}, f32[32]{0:T(128)}, u32[]{:S(2)}) copy-start(f32[32]{0:T(128)} %param.13) | copy-start | bytes 388
  2.6 15.7 %copy-start.6 = (f32[7,8]{1,0:T(8,128)S(1)}, f32[7,8]{1,0:T(8,128)}, u32[]{:S(2)}) copy-start(f32[7,8]{1,0:T(8,128)} %param.12) | copy-start | bytes 676
  2.7 15.8 %copy-start.7 = (f32[7,8]{1,0:T(8,128)S(1)}, f32[7,8]{1,0:T(8,128)}, u32[]{:S(2)}) copy-start(f32[7,8]{1,0:T(8,128)} %param.11) | copy-start | bytes 676
  2.7 16.1 %copy-start.2 = (bf16[2,1024,32,8]{1,3,2,0:T(8,128)(2,1)S(1)}, bf16[2,1024,32,8]{1,3,2,0:T(8,128)(2,1)}, u32[]{:S(2)}) copy-start(bf16[2,1024,32,8]{1,3,2,0:T(8,128)(2,1)} %param.10) | copy-start | bytes 3145732
  2.7 16.1 %copy-start.3 = (bf16[2,32,8,316]{3,2,1,0:T(8,128)(2,1)S(1)}, bf16[2,32,8,316]{3,2,1,0:T(8,128)(2,1)}, u32[]{:S(2)}) copy-start(bf16[2,32,8,316]{3,2,1,0:T(8,128)(2,1)} %param.14) | copy-start | bytes 970756
  5.1 16.7 %collective-permute-start = (bf16[96,768]{1,0:T(8,128)(2,1)S(1)}, bf16[96,768]{1,0:T(8,128)(2,1)S(1)}, u32[]{:S(2)}, u32[]{:S(2)}) collective-permute-start(bf16[96,768]{1,0:T(8,128)(2,1)S(1)} %get-tuple-element.26), channel_id=1, source_target_pairs={{0,1},{1,2},{2,3},{3,4},{4,5},{5,6},{6,7},{7,0},{8,9},{9,10},{10,1... | collective-permute-start | bytes 442376 | tf_op jit(solution)/shard_map/ppermute | solution.py:243
  9.4 12.4 %collective-permute-start.1 = (bf16[96,768]{1,0:T(8,128)(2,1)S(1)}, bf16[96,768]{1,0:T(8,128)(2,1)S(1)}, u32[]{:S(2)}, u32[]{:S(2)}) collective-permute-start(bf16[96,768]{1,0:T(8,128)(2,1)S(1)} %get-tuple-element.27), channel_id=1, source_target_pairs={{0,7},{1,0},{2,1},{3,2},{4,3},{5,4},{6,5},{7,6},{8,15},{9,8},{10,9... | collective-permute-start | bytes 442376 | tf_op jit(solution)/shard_map/ppermute | solution.py:243
  23.0 20.6 %collective-permute-start.2 = (bf16[96,2048]{1,0:T(8,128)(2,1)S(1)}, bf16[96,2048]{1,0:T(8,128)(2,1)S(1)}, u32[]{:S(2)}, u32[]{:S(2)}) collective-permute-start(bf16[96,2048]{1,0:T(8,128)(2,1)S(1)} %get-tuple-element.35), channel_id=1, source_target_pairs={{0,1},{1,2},{2,3},{3,4},{4,5},{5,6},{6,7},{7,0},{8,9},{9,10},{10,1... | collective-permute-start | bytes 1179656 | tf_op jit(solution)/shard_map/ppermute | solution.py:243
  25.0 22.2 %collective-permute-start.3 = (bf16[96,2048]{1,0:T(8,128)(2,1)S(1)}, bf16[96,2048]{1,0:T(8,128)(2,1)S(1)}, u32[]{:S(2)}, u32[]{:S(2)}) collective-permute-start(bf16[96,2048]{1,0:T(8,128)(2,1)S(1)} %get-tuple-element.36), channel_id=1, source_target_pairs={{0,7},{1,0},{2,1},{3,2},{4,3},{5,4},{6,5},{7,6},{8,15},{9,8},{10,9... | collective-permute-start | bytes 1179656 | tf_op jit(solution)/shard_map/ppermute | solution.py:243
  30.1 18.7 %collective-permute-start.4 = (bf16[528,128]{1,0:T(8,128)(2,1)S(1)}, bf16[528,128]{1,0:T(8,128)(2,1)S(1)}, u32[]{:S(2)}, u32[]{:S(2)}) collective-permute-start(bf16[528,128]{1,0:T(8,128)(2,1)S(1)} %get-tuple-element.37), channel_id=1, source_target_pairs={{0,8},{8,16},{16,24},{24,32},{32,40},{40,48},{48,56},{56,64},{64,7... | collective-permute-start | bytes 405512 | tf_op jit(solution)/shard_map/ppermute | solution.py:249
  32.1 16.8 %collective-permute-start.5 = (bf16[528,128]{1,0:T(8,128)(2,1)S(1)}, bf16[528,128]{1,0:T(8,128)(2,1)S(1)}, u32[]{:S(2)}, u32[]{:S(2)}) collective-permute-start(bf16[528,128]{1,0:T(8,128)(2,1)S(1)} %get-tuple-element.38), channel_id=1, source_target_pairs={{8,0},{16,8},{24,16},{32,24},{40,32},{48,40},{56,48},{64,56},{72,6... | collective-permute-start | bytes 405512 | tf_op jit(solution)/shard_map/ppermute | solution.py:249
  35.7 13.2 %collective-permute-start.6 = (bf16[528,128]{1,0:T(8,128)(2,1)S(1)}, bf16[528,128]{1,0:T(8,128)(2,1)S(1)}, u32[]{:S(2)}, u32[]{:S(2)}) collective-permute-start(bf16[528,128]{1,0:T(8,128)(2,1)S(1)} %get-tuple-element.39), channel_id=1, source_target_pairs={{0,16},{8,24},{16,32},{24,40},{32,48},{40,56},{48,64},{56,72},{64,... | collective-permute-start | bytes 405512 | tf_op jit(solution)/shard_map/ppermute | solution.py:249
  43.7 10.2 %collective-permute-start.7 = (bf16[528,128]{1,0:T(8,128)(2,1)S(1)}, bf16[528,128]{1,0:T(8,128)(2,1)S(1)}, u32[]{:S(2)}, u32[]{:S(2)}) collective-permute-start(bf16[528,128]{1,0:T(8,128)(2,1)S(1)} %get-tuple-element.40), channel_id=1, source_target_pairs={{16,0},{24,8},{32,16},{40,24},{48,32},{56,40},{64,48},{72,56},{80,... | collective-permute-start | bytes 405512 | tf_op jit(solution)/shard_map/ppermute | solution.py:249

commit v2 on v1

--- a/solution.py
+++ b/solution.py
@@ -22,6 +22,8 @@
 BUF = 2 * NS + 16
 RANKS = 8
 BF = jnp.bfloat16
+SMEM = pl.BlockSpec(memory_space=pltpu.SMEM)
+VMEM = pl.BlockSpec(memory_space=pltpu.VMEM)
 F32 = jnp.float32
 
 NN = (((1,), (0,)), ((), ()))
@@ -178,7 +180,7 @@
     own[:, BOX:] = dot(c_im, table, NTR)
 
 
-def matrix_kernel(rad, anterp_cols, q_below, q_above, out):
+def matrix_kernel(place, rad, anterp_cols, q_below, q_above, out):
     shape = (NS, NS)
     t_row, f_row = local_place(shape, 0)
     t_col, g_col = local_place(shape, 1)
@@ -189,15 +191,19 @@
     same = t_row == t_col
     first = jnp.logical_and(same, g_col == j_row).astype(BF)
     last = jnp.logical_and(same, g_col == j_row + FD - WIDTH).astype(BF)
+    me = place[0]
     for c in range(2):
         r = rad[c]
         cols = pl.ds(c * P_SIZE, P_SIZE)
         q = dot(r, mat_hi, TN) + dot(r, mat_lo, TN)
         q = q + dot(q_below[:, cols], first, TN) + dot(q_above[:, cols], last, TN)
-        out[:, c * NS : (c + 1) * NS] = q.astype(BF)
-
-
-def receive_kernel(own, matrix, got0, got1, got2, got3, out, stack):
+        q = q.astype(BF)
+        for d in range(RANKS):
+            rows = pl.ds(pl.multiple_of(((d - me) & (RANKS - 1)) * CAP, CAP), CAP)
+            out[rows, c * NS : (c + 1) * NS] = q[d * CAP : (d + 1) * CAP]
+
+
+def far_kernel(own, matrix, got0, got1, got2, got3, up3, far4, down3, stack):
     gots = (got0, got1, got2, got3)
     ids = jnp.concatenate([g[2 * NS :, :].astype(F32) for g in gots], axis=1)
     index = (16.0 * ids[0:1] + ids[1:2]).astype(jnp.int32)
@@ -209,17 +215,28 @@
     stack[0:NS, BOX:] = im
     stack[NS:, :BOX] = im
     stack[NS:, BOX:] = -re
-
-    @pl.loop(0, RANKS)
-    def _(d):
-        rows = pl.ds(pl.multiple_of(d * CAP, CAP), CAP)
-        out[d] = dot(matrix[rows, :], stack[...]).astype(BF)
-
-
-def sum_kernel(parts, out):
-    total = parts[0].astype(F32)
-    for d in range(1, RANKS):
-        total = total + parts[d].astype(F32)
+    for j, out in ((3, up3), (4, far4), (5, down3)):
+        out[...] = dot(matrix[j * CAP : (j + 1) * CAP, :], stack[...]).astype(BF)
+
+
+def near_kernel(matrix, stack, up1, down1, keep):
+    for j, out in ((1, up1), (7, down1)):
+        out[...] = dot(matrix[j * CAP : (j + 1) * CAP, :], stack[...]).astype(BF)
+    for i, j in enumerate((0, 2, 6)):
+        keep[i] = dot(matrix[j * CAP : (j + 1) * CAP, :], stack[...])
+
+
+def relay_kernel(place, keep, from_up3, from_far4, from_down3, up2, down2):
+    far = from_far4[...].astype(F32)
+    even = place[1] == 0
+    up2[...] = (keep[1] + from_up3[...].astype(F32) + jnp.where(even, far, 0.0)).astype(BF)
+    down2[...] = (keep[2] + from_down3[...].astype(F32) + jnp.where(even, 0.0, far)).astype(BF)
+
+
+def sum_kernel(keep, up1, down1, up2, down2, out):
+    total = keep[0]
+    for part in (up1, down1, up2, down2):
+        total = total + part[...].astype(F32)
     out[0] = total[:, :BOX].astype(BF)
     out[1] = total[:, BOX:].astype(BF)
 
@@ -241,6 +258,16 @@
 def around(value, axis, steps):
     count = lax.axis_size(axis)
     return lax.ppermute(value, axis, [(i, (i + steps) % count) for i in range(count)])
+
+
+def outward(value, steps):
+    groups, count = lax.axis_size("box"), lax.axis_size("samp")
+    pairs = []
+    for b in range(groups):
+        for i in range(count):
+            j = (i + (steps if b % 2 == 0 else -steps)) % count
+            pairs.append((b * count + i, b * count + j))
+    return lax.ppermute(value, ("box", "samp"), pairs)
 
 
 def along(value, axis, steps):
@@ -317,23 +344,50 @@
         flops=10**9,
         name="own",
     )
+    place = jnp.stack([lax.axis_index("samp"), lax.axis_index("box") % 2]).astype(jnp.int32)
     (matrix,) = call(
         matrix_kernel,
         [((P_SIZE, 2 * NS), BF)],
-        rad, anterp_cols, q_below, q_above,
+        place, rad, anterp_cols, q_below, q_above,
         flops=10**9,
         name="matrix",
-    )
-    (terms,) = call(
-        receive_kernel,
-        [((RANKS, CAP, 2 * BOX), BF)],
+        in_specs=[SMEM] + [VMEM] * 4,
+    )
+    block = (CAP, 2 * BOX)
+    up3, far4, down3, stack = call(
+        far_kernel,
+        [(block, BF)] * 3 + [((2 * NS, 2 * BOX), BF)],
         own, matrix, *gots,
-        scratch=[pltpu.VMEM((2 * NS, 2 * BOX), BF)],
-        flops=10**9,
-        name="receive",
-    )
-    terms = lax.all_to_all(terms, "samp", 0, 0)
-    (out,) = call(sum_kernel, [((2, P_SIZE // RANKS, BOX), BF)], terms, name="total")
+        flops=5 * 10**8,
+        name="far",
+    )
+    from_up3 = around(up3, "samp", 1)
+    from_far4 = outward(far4, 2)
+    from_down3 = around(down3, "samp", -1)
+    up1, down1, keep = call(
+        near_kernel,
+        [(block, BF)] * 2 + [((3,) + block, F32)],
+        matrix, stack,
+        flops=5 * 10**8,
+        name="near",
+    )
+    from_up1 = around(up1, "samp", 1)
+    from_down1 = around(down1, "samp", -1)
+    up2, down2 = call(
+        relay_kernel,
+        [(block, BF)] * 2,
+        place, keep, from_up3, from_far4, from_down3,
+        name="relay",
+        in_specs=[SMEM] + [VMEM] * 4,
+    )
+    from_up2 = around(up2, "samp", 2)
+    from_down2 = around(down2, "samp", -2)
+    (out,) = call(
+        sum_kernel,
+        [((2, P_SIZE // RANKS, BOX), BF)],
+        keep, from_up1, from_down1, from_up2, from_down2,
+        name="total",
+    )
     return out
 
 

time: 97.3 us -> 91.2 us (0.937)
  blocking collectives: 39.5 us -> 0 us
  starting transfers between devices: 35.3 us -> 59.3 us
  local copies, waits for them, and re-layouts: 3.1 us -> 7.7 us
  waiting for transfers between devices: 4.99 us -> 8.65 us
    all_to_all x1 -> x0, blocking collectives: 39.5 us -> none  [on_device(): terms = lax.all_to_all(terms, 'samp', 0, 0)]
    ppermute x4 -> x10, starting transfers between devices: 19.9 us -> 40.9 us  [around(): lax.ppermute(value, axis, [(i, (i + steps) % count) for i in range(count)])]
    ppermute x4 -> x10, waiting for transfers between devices: 0.01 us -> 5.89 us  [around(): lax.ppermute(value, axis, [(i, (i + steps) % count) for i in range(count)])]
    unnamed x20 -> x30, local copies, waits for them, and re-layouts: 2.66 us -> 7.26 us
    ppermute x0 -> x1, starting transfers between devices: none -> 3 us  [outward(): return lax.ppermute(value, ('box', 'samp'), pairs)]
    ppermute x4, waiting for transfers between devices: 4.98 us -> 2.76 us  [along(): return lax.ppermute(value, axis, pairs)]
    pallas_call x7 -> x9, Pallas kernels: 13.5 us -> 14.2 us  [call(): pl.pallas_call(kernel, out_shape=shapes, scratch_shapes=list(scratch), co...]
  transfers between devices with their start and end apart: 8 -> 15, of which waited for: 1 -> 3; matrix products, arithmetic and copies ran while one was open for 1% -> 1% of each run, Pallas kernels for 6% -> 10%
where the time goes in v2:
time: 91.2 us; the launch traced here: 90.6 us
  starting transfers between devices  59.3 us (65%)
  Pallas kernels  14.2 us (16%)
  waiting for transfers between devices  8.65 us (9%)
  local copies, waits for them, and re-layouts  7.7 us (8%)
    ppermute x10, starting transfers between devices, around(): lax.ppermute(value, axis, [(i, (i + steps) % count) for i in range(count)])  40.9 us
    ppermute x4, starting transfers between devices, along(): return lax.ppermute(value, axis, pairs)  15.4 us
    pallas_call x9, Pallas kernels, call(): pl.pallas_call(kernel, out_shape=shapes, scratch_shapes=list(scratch), co...  14.2 us
    unnamed x30, local copies, waits for them, and re-layouts  7.26 us
    ppermute x10, waiting for transfers between devices, around(): lax.ppermute(value, axis, [(i, (i + steps) % count) for i in range(count)])  5.89 us
    ppermute x1, starting transfers between devices, outward(): return lax.ppermute(value, ('box', 'samp'), pairs)  3 us
    ppermute x4, waiting for transfers between devices, along(): return lax.ppermute(value, axis, pairs)  2.76 us
  transfers between devices with their start and end apart: 15, of which 3 were waited for; matrix products, arithmetic and copies ran while one was open for 1% of the time, Pallas kernels for 10%

profile of v2, /device:TPU:30, one launch (start us, length us, event | category | flops | bytes accessed | tf_op | source)
XLA Modules:
  0.0 90.6 jit_solution(4978765127193816679)
XLA Ops:
  0.0 1.4 %copy-done = bf16[2,1024,384]{2,1,0:T(8,128)(2,1)S(1)} copy-done((bf16[2,1024,384]{2,1,0:T(8,128)(2,1)S(1)}, bf16[2,1024,384]{2,1,0:T(8,128)(2,1)}, u32[]{:S(2)}) %copy-start) | copy-done | bytes 1572888
  1.4 1.2 %copy-done.1 = bf16[2,1024,32,8]{1,3,2,0:T(8,128)(2,1)S(1)} copy-done((bf16[2,1024,32,8]{1,3,2,0:T(8,128)(2,1)S(1)}, bf16[2,1024,32,8]{1,3,2,0:T(8,128)(2,1)}, u32[]{:S(2)}) %copy-start.1) | copy-done | bytes 1048600
  2.7 2.4 %field.1 = (f32[256,768]{1,0:T(8,128)S(1)}, bf16[96,768]{1,0:T(8,128)(2,1)S(1)}, bf16[96,768]{1,0:T(8,128)(2,1)S(1)}) custom-call(bf16[2,256,1024]{2,1,0:T(8,128)(2,1)S(1)} %bitcast.12, bf16[2,1024,384]{2,1,0:T(8,128)(2,1)S(1)} %copy-done), custom_call_target="tpu_custom_call" | custom-call | flops 1000000000 | bytes 3702784 | tf_op jit(solution)/shard_map/field/pallas_call | solution.py:247
  5.1 0.9 copy-done.5
  6.0 4.3 %collective-permute-start = (bf16[96,768]{1,0:T(8,128)(2,1)S(1)}, bf16[96,768]{1,0:T(8,128)(2,1)S(1)}, u32[]{:S(2)}, u32[]{:S(2)}) collective-permute-start(bf16[96,768]{1,0:T(8,128)(2,1)S(1)} %get-tuple-element.37), channel_id=1, source_target_pairs={{0,1},{1,2},{2,3},{3,4},{4,5},{5,6},{6,7},{7,0},{8,9},{9,10},{10,1... | collective-permute-start | bytes 442376 | tf_op jit(solution)/shard_map/ppermute | solution.py:260
  10.3 8.6 %collective-permute-start.1 = (bf16[96,768]{1,0:T(8,128)(2,1)S(1)}, bf16[96,768]{1,0:T(8,128)(2,1)S(1)}, u32[]{:S(2)}, u32[]{:S(2)}) collective-permute-start(bf16[96,768]{1,0:T(8,128)(2,1)S(1)} %get-tuple-element.38), channel_id=1, source_target_pairs={{0,7},{1,0},{2,1},{3,2},{4,3},{5,4},{6,5},{7,6},{8,15},{9,8},{10,9... | collective-permute-start | bytes 442376 | tf_op jit(solution)/shard_map/ppermute | solution.py:260
  19.7 1.1 %copy-done.6 = f32[256,768]{1,0:T(8,128)S(1)} copy-done((f32[256,768]{1,0:T(8,128)S(1)}, f32[256,768]{1,0:T(8,128)}, u32[]{:S(2)}) %copy-start.6) | copy-done | bytes 786456
  20.8 3.0 %prepare.1 = (f32[256,768]{1,0:T(8,128)S(1)}, bf16[2,2,256,96]{3,2,1,0:T(8,128)(2,1)S(1)}, bf16[384,512]{1,0:T(8,128)(2,1)S(1)}, bf16[512,512]{1,0:T(8,128)(2,1)...) custom-call(f32[256,768]{1,0:T(8,128)S(1)} %copy-done.6, ...), custom_call_target="tpu_custom_call" | custom-call | flops 2000000000 | bytes 5547008 | tf_op jit(solution)/shard_map/prepare/pallas_call | solution.py:247
  23.8 0.9 copy-done.7
  24.7 1.2 %send.1 = (bf16[528,128]{1,0:T(8,128)(2,1)S(1)}, bf16[528,128]{1,0:T(8,128)(2,1)S(1)}, bf16[528,128]{1,0:T(8,128)(2,1)S(1)}, bf16[528,128]{1,0:T(8,128)(2,1)S(1)}, bf16[2,256,768]{2,1,0:T(8,128)(2,1)S(1)}) custom-call(f32[256,768]{1,0:T(8,128)S(1)} %get-tuple-element.35.inter, bf16[2,2,256,96]{3,2,1,0:T(8,128)(2,1)S(1)} %get-tuple-element.36.halo_mat, ...), custom_call_target="tpu_custom_call" | custom-call | flops 100000000 | bytes 3538944 | tf_op jit(solution)/shard_map/send/pallas_call | solution.py:247
  26.6 1.9 %collective-permute-start.2 = (bf16[96,2048]{1,0:T(8,128)(2,1)S(1)}, bf16[96,2048]{1,0:T(8,128)(2,1)}, u32[]{:S(2)}, u32[]{:S(2)}) collective-permute-start(bf16[96,2048]{1,0:T(8,128)(2,1)S(1)} %get-tuple-element.43), channel_id=1, source_target_pairs={{0,1},{1,2},{2,3},{3,4},{4,5},{5,6},{6,7},{7,0},{8,9},{9,10},{10,1... | collective-permute-start | bytes 1179656 | tf_op jit(solution)/shard_map/ppermute | solution.py:260
  28.5 5.1 %collective-permute-start.3 = (bf16[96,2048]{1,0:T(8,128)(2,1)S(1)}, bf16[96,2048]{1,0:T(8,128)(2,1)}, u32[]{:S(2)}, u32[]{:S(2)}) collective-permute-start(bf16[96,2048]{1,0:T(8,128)(2,1)S(1)} %get-tuple-element.44), channel_id=1, source_target_pairs={{0,7},{1,0},{2,1},{3,2},{4,3},{5,4},{6,5},{7,6},{8,15},{9,8},{10,9... | collective-permute-start | bytes 1179656 | tf_op jit(solution)/shard_map/ppermute | solution.py:260
  33.7 1.9 %collective-permute-start.4 = (bf16[528,128]{1,0:T(8,128)(2,1)}, bf16[528,128]{1,0:T(8,128)(2,1)S(1)}, u32[]{:S(2)}, u32[]{:S(2)}) collective-permute-start(bf16[528,128]{1,0:T(8,128)(2,1)} %copy-done.4), channel_id=1, source_target_pairs={{0,8},{8,16},{16,24},{24,32},{32,40},{40,48},{48,56},{56,64},{64,7... | collective-permute-start | bytes 405512 | tf_op jit(solution)/shard_map/ppermute | solution.py:276
  35.7 3.6 %collective-permute-start.5 = (bf16[528,128]{1,0:T(8,128)(2,1)S(1)}, bf16[528,128]{1,0:T(8,128)(2,1)S(1)}, u32[]{:S(2)}, u32[]{:S(2)}) collective-permute-start(bf16[528,128]{1,0:T(8,128)(2,1)S(1)} %get-tuple-element.47), channel_id=1, source_target_pairs={{8,0},{16,8},{24,16},{32,24},{40,32},{48,40},{56,48},{64,56},{72,6... | collective-permute-start | bytes 405512 | tf_op jit(solution)/shard_map/ppermute | solution.py:276
  39.3 7.9 %collective-permute-start.6 = (bf16[528,128]{1,0:T(8,128)(2,1)S(1)}, bf16[528,128]{1,0:T(8,128)(2,1)S(1)}, u32[]{:S(2)}, u32[]{:S(2)}) collective-permute-start(bf16[528,128]{1,0:T(8,128)(2,1)S(1)} %get-tuple-element.48), channel_id=1, source_target_pairs={{0,16},{8,24},{16,32},{24,40},{32,48},{40,56},{48,64},{56,72},{64,... | collective-permute-start | bytes 405512 | tf_op jit(solution)/shard_map/ppermute | solution.py:276
  47.3 1.9 %collective-permute-start.7 = (bf16[528,128]{1,0:T(8,128)(2,1)S(1)}, bf16[528,128]{1,0:T(8,128)(2,1)S(1)}, u32[]{:S(2)}, u32[]{:S(2)}) collective-permute-start(bf16[528,128]{1,0:T(8,128)(2,1)S(1)} %get-tuple-element.49), channel_id=1, source_target_pairs={{16,0},{24,8},{32,16},{40,24},{48,32},{56,40},{64,48},{72,56},{80,... | collective-permute-start | bytes 405512 | tf_op jit(solution)/shard_map/ppermute | solution.py:276
  49.2 1.1 %copy-done.8 = bf16[512,640]{1,0:T(8,128)(2,1)S(1)} copy-done((bf16[512,640]{1,0:T(8,128)(2,1)S(1)}, bf16[512,640]{1,0:T(8,128)(2,1)}, u32[]{:S(2)}) %copy-start.8) | copy-done | bytes 655384
  50.3 1.6 %own.1 = f32[256,768]{1,0:T(8,128)S(1)} custom-call(bf16[2,256,768]{2,1,0:T(8,128)(2,1)S(1)} %get-tuple-element.42.parts, s32[1,640]{1,0:T(1,128)S(1)} %reshape.31.src_row, bf16[512,640]{1,0:T(8,128)(2,1)S(1)} %copy-done.8, s32[1,640]{1,0:T(1,128)S(1)} %reshape.32.target_row), custom_call_target="tpu_custom_call" | custom-call | flops 1000000000 | bytes 2233344 | tf_op jit(solution)/shard_map/own/pallas_call | solution.py:247
  51.9 2.8 %matrix.1 = bf16[1024,512]{1,0:T(8,128)(2,1)S(1)} custom-call(s32[2]{0:T(128)S(1)} %pad_add_fusion.place, bf16[2,256,1024]{2,1,0:T(8,128)(2,1)S(1)} %bitcast.14, f32[256,7]{1,0:T(8,128)S(1)} %bitcast_multiply_fusion.anterp_cols, bf16[96,2048]{1,0:T(8,128)(2,1)} %collective-permute-done.2.q_below, bf16[96,2048]{1,0:T(8,128)(2,1)} %collective-permute-done.3.q_above), custom_call_target="tpu_custom_call" | custom-call | flops 1000000000 | bytes 2890760 | tf_op jit(solution)/shard_map/matrix/pallas_call | solution.py:247
  54.7 2.8 %collective-permute-done.7.got3 = bf16[528,128]{1,0:T(8,128)(2,1)S(1)} collective-permute-done((bf16[528,128]{1,0:T(8,128)(2,1)S(1)}, bf16[528,128]{1,0:T(8,128)(2,1)S(1)}, u32[]{:S(2)}, u32[]{:S(2)}) %collective-permute-start.7) | collective-permute-done | bytes 135200 | tf_op jit(solution)/shard_map/ppermute | solution.py:276
  57.5 0.9 %far.1 = (bf16[128,768]{1,0:T(8,128)(2,1)S(1)}, bf16[128,768]{1,0:T(8,128)(2,1)S(1)}, bf16[128,768]{1,0:T(8,128)(2,1)S(1)}, bf16[512,768]{1,0:T(8,128)(2,1)S(1)}) custom-call(f32[256,768]{1,0:T(8,128)S(1)} %own.1, bf16[1024,512]{1,0:T(8,128)(2,1)S(1)} %matrix.1, bf16[528,128]{1,0:T(8,128)(2,1)S(1)} %collective-permute-done.4.got0, ...), custom_call_target="tpu_custom_call" | custom-call | flops 500000000 | bytes 3751936 | tf_op jit(solution)/shard_map/far/pallas_call | solution.py:247
  58.4 1.9 %collective-permute-start.10 = (bf16[128,768]{1,0:T(8,128)(2,1)S(1)}, bf16[128,768]{1,0:T(8,128)(2,1)S(1)}, u32[]{:S(2)}, u32[]{:S(2)}) collective-permute-start(bf16[128,768]{1,0:T(8,128)(2,1)S(1)} %get-tuple-element.54), channel_id=1, source_target_pairs={{0,1},{1,2},{2,3},{3,4},{4,5},{5,6},{6,7},{7,0},{8,9},{9,10},{10,1... | collective-permute-start | bytes 589832 | tf_op jit(solution)/shard_map/ppermute | solution.py:260
  60.4 3.0 %collective-permute-start.11 = (bf16[128,768]{1,0:T(8,128)(2,1)S(1)}, bf16[128,768]{1,0:T(8,128)(2,1)S(1)}, u32[]{:S(2)}, u32[]{:S(2)}) collective-permute-start(bf16[128,768]{1,0:T(8,128)(2,1)S(1)} %get-tuple-element.55), channel_id=1, source_target_pairs={{0,2},{1,3},{2,4},{3,5},{4,6},{5,7},{6,0},{7,1},{8,14},{9,15},{10,... | collective-permute-start | bytes 589832 | tf_op jit(solution)/shard_map/ppermute | solution.py:270
  63.4 4.1 %collective-permute-start.12 = (bf16[128,768]{1,0:T(8,128)(2,1)S(1)}, bf16[128,768]{1,0:T(8,128)(2,1)S(1)}, u32[]{:S(2)}, u32[]{:S(2)}) collective-permute-start(bf16[128,768]{1,0:T(8,128)(2,1)S(1)} %get-tuple-element.56), channel_id=1, source_target_pairs={{0,7},{1,0},{2,1},{3,2},{4,3},{5,4},{6,5},{7,6},{8,15},{9,8},{10,9... | collective-permute-start | bytes 589832 | tf_op jit(solution)/shard_map/ppermute | solution.py:260
  68.1 3.0 %collective-permute-start.8 = (bf16[128,768]{1,0:T(8,128)(2,1)S(1)}, bf16[128,768]{1,0:T(8,128)(2,1)S(1)}, u32[]{:S(2)}, u32[]{:S(2)}) collective-permute-start(bf16[128,768]{1,0:T(8,128)(2,1)S(1)} %get-tuple-element.52), channel_id=1, source_target_pairs={{0,1},{1,2},{2,3},{3,4},{4,5},{5,6},{6,7},{7,0},{8,9},{9,10},{10,1... | collective-permute-start | bytes 589832 | tf_op jit(solution)/shard_map/ppermute | solution.py:260
  71.1 4.1 %collective-permute-start.9 = (bf16[128,768]{1,0:T(8,128)(2,1)S(1)}, bf16[128,768]{1,0:T(8,128)(2,1)S(1)}, u32[]{:S(2)}, u32[]{:S(2)}) collective-permute-start(bf16[128,768]{1,0:T(8,128)(2,1)S(1)} %get-tuple-element.53), channel_id=1, source_target_pairs={{0,7},{1,0},{2,1},{3,2},{4,3},{5,4},{6,5},{7,6},{8,15},{9,8},{10,9... | collective-permute-start | bytes 589832 | tf_op jit(solution)/shard_map/ppermute | solution.py:260
  75.2 0.7 relay.1
  75.9 3.2 %collective-permute-start.13 = (bf16[128,768]{1,0:T(8,128)(2,1)S(1)}, bf16[128,768]{1,0:T(8,128)(2,1)S(1)}, u32[]{:S(2)}, u32[]{:S(2)}) collective-permute-start(bf16[128,768]{1,0:T(8,128)(2,1)S(1)} %get-tuple-element.57), channel_id=1, source_target_pairs={{0,2},{1,3},{2,4},{3,5},{4,6},{5,7},{6,0},{7,1},{8,10},{9,11},{10,... | collective-permute-start | bytes 589832 | tf_op jit(solution)/shard_map/ppermute | solution.py:260
  79.2 4.7 %collective-permute-start.14 = (bf16[128,768]{1,0:T(8,128)(2,1)S(1)}, bf16[128,768]{1,0:T(8,128)(2,1)S(1)}, u32[]{:S(2)}, u32[]{:S(2)}) collective-permute-start(bf16[128,768]{1,0:T(8,128)(2,1)S(1)} %get-tuple-element.58), channel_id=1, source_target_pairs={{0,6},{1,7},{2,0},{3,1},{4,2},{5,3},{6,4},{7,5},{8,14},{9,15},{10,... | collective-permute-start | bytes 589832 | tf_op jit(solution)/shard_map/ppermute | solution.py:260
  83.9 2.5 %collective-permute-done.13.up2 = bf16[128,768]{1,0:T(8,128)(2,1)S(1)} collective-permute-done((bf16[128,768]{1,0:T(8,128)(2,1)S(1)}, bf16[128,768]{1,0:T(8,128)(2,1)S(1)}, u32[]{:S(2)}, u32[]{:S(2)}) %collective-permute-start.13) | collective-permute-done | bytes 196640 | tf_op jit(solution)/shard_map/ppermute | solution.py:260
  86.4 3.4 %collective-permute-done.14.down2 = bf16[128,768]{1,0:T(8,128)(2,1)S(1)} collective-permute-done((bf16[128,768]{1,0:T(8,128)(2,1)S(1)}, bf16[128,768]{1,0:T(8,128)(2,1)S(1)}, u32[]{:S(2)}, u32[]{:S(2)}) %collective-permute-start.14) | collective-permute-done | bytes 196640 | tf_op jit(solution)/shard_map/ppermute | solution.py:260
  89.8 0.8 total.1
  (60 shorter events, 2.1 us)
Async XLA Ops:
  0.0 1.4 %copy-start = (bf16[2,1024,384]{2,1,0:T(8,128)(2,1)S(1)}, bf16[2,1024,384]{2,1,0:T(8,128)(2,1)}, u32[]{:S(2)}) copy-start(bf16[2,1024,384]{2,1,0:T(8,128)(2,1)} %cur.1) | copy-start | bytes 4718596
  1.4 1.2 %copy-start.1 = (bf16[2,1024,32,8]{1,3,2,0:T(8,128)(2,1)S(1)}, bf16[2,1024,32,8]{1,3,2,0:T(8,128)(2,1)}, u32[]{:S(2)}) copy-start(bf16[2,1024,32,8]{1,3,2,0:T(8,128)(2,1)} %param.10) | copy-start | bytes 3145732
  2.6 16.3 %copy-start.9 = (s32[640]{0:T(1024)S(1)}, s32[640]{0:T(1024)}, u32[]{:S(2)}) copy-start(s32[640]{0:T(1024)} %param.16) | copy-start | bytes 7684
  2.6 16.3 %copy-start.11 = (f32[7,8]{1,0:T(8,128)S(1)}, f32[7,8]{1,0:T(8,128)}, u32[]{:S(2)}) copy-start(f32[7,8]{1,0:T(8,128)} %param.12) | copy-start | bytes 676
  2.6 16.4 %copy-start.14 = (f32[32]{0:T(128)S(1)}, f32[32]{0:T(128)}, u32[]{:S(2)}) copy-start(f32[32]{0:T(128)} %param.13) | copy-start | bytes 388
  2.6 16.6 %copy-start.12 = (f32[7,8]{1,0:T(8,128)S(1)}, f32[7,8]{1,0:T(8,128)}, u32[]{:S(2)}) copy-start(f32[7,8]{1,0:T(8,128)} %param.11) | copy-start | bytes 676
  2.6 16.7 %copy-start.10 = (s32[640]{0:T(1024)S(1)}, s32[640]{0:T(1024)}, u32[]{:S(2)}) copy-start(s32[640]{0:T(1024)} %param.15) | copy-start | bytes 7684
  2.7 16.7 %copy-start.13 = (s32[640]{0:T(1024)S(1)}, s32[640]{0:T(1024)}, u32[]{:S(2)}) copy-start(s32[640]{0:T(1024)} %param.17) | copy-start | bytes 7684
  2.7 17.0 %copy-start.2 = (bf16[2,1024,32,8]{1,3,2,0:T(8,128)(2,1)S(1)}, bf16[2,1024,32,8]{1,3,2,0:T(8,128)(2,1)}, u32[]{:S(2)}) copy-start(bf16[2,1024,32,8]{1,3,2,0:T(8,128)(2,1)} %param.10) | copy-start | bytes 3145732
  2.7 17.0 %copy-start.3 = (bf16[2,32,8,316]{3,2,1,0:T(8,128)(2,1)S(1)}, bf16[2,32,8,316]{3,2,1,0:T(8,128)(2,1)}, u32[]{:S(2)}) copy-start(bf16[2,32,8,316]{3,2,1,0:T(8,128)(2,1)} %param.14) | copy-start | bytes 970756
  5.1 0.9 copy-start.5
  6.0 18.6 %collective-permute-start = (bf16[96,768]{1,0:T(8,128)(2,1)S(1)}, bf16[96,768]{1,0:T(8,128)(2,1)S(1)}, u32[]{:S(2)}, u32[]{:S(2)}) collective-permute-start(bf16[96,768]{1,0:T(8,128)(2,1)S(1)} %get-tuple-element.37), channel_id=1, source_target_pairs={{0,1},{1,2},{2,3},{3,4},{4,5},{5,6},{6,7},{7,0},{8,9},{9,10},{10,1... | collective-permute-start | bytes 442376 | tf_op jit(solution)/shard_map/ppermute | solution.py:260
  10.3 14.4 %collective-permute-start.1 = (bf16[96,768]{1,0:T(8,128)(2,1)S(1)}, bf16[96,768]{1,0:T(8,128)(2,1)S(1)}, u32[]{:S(2)}, u32[]{:S(2)}) collective-permute-start(bf16[96,768]{1,0:T(8,128)(2,1)S(1)} %get-tuple-element.38), channel_id=1, source_target_pairs={{0,7},{1,0},{2,1},{3,2},{4,3},{5,4},{6,5},{7,6},{8,15},{9,8},{10,9... | collective-permute-start | bytes 442376 | tf_op jit(solution)/shard_map/ppermute | solution.py:260
  19.6 1.1 %copy-start.6 = (f32[256,768]{1,0:T(8,128)S(1)}, f32[256,768]{1,0:T(8,128)}, u32[]{:S(2)}) copy-start(f32[256,768]{1,0:T(8,128)} %copy-done.5) | copy-start | bytes 2359300
  23.8 0.9 copy-start.7
  25.9 0.7 copy-start.4
  26.6 20.7 %collective-permute-start.2 = (bf16[96,2048]{1,0:T(8,128)(2,1)S(1)}, bf16[96,2048]{1,0:T(8,128)(2,1)}, u32[]{:S(2)}, u32[]{:S(2)}) collective-permute-start(bf16[96,2048]{1,0:T(8,128)(2,1)S(1)} %get-tuple-element.43), channel_id=1, source_target_pairs={{0,1},{1,2},{2,3},{3,4},{4,5},{5,6},{6,7},{7,0},{8,9},{9,10},{10,1... | collective-permute-start | bytes 1179656 | tf_op jit(solution)/shard_map/ppermute | solution.py:260
  28.5 23.4 %collective-permute-start.3 = (bf16[96,2048]{1,0:T(8,128)(2,1)S(1)}, bf16[96,2048]{1,0:T(8,128)(2,1)}, u32[]{:S(2)}, u32[]{:S(2)}) collective-permute-start(bf16[96,2048]{1,0:T(8,128)(2,1)S(1)} %get-tuple-element.44), channel_id=1, source_target_pairs={{0,7},{1,0},{2,1},{3,2},{4,3},{5,4},{6,5},{7,6},{8,15},{9,8},{10,9... | collective-permute-start | bytes 1179656 | tf_op jit(solution)/shard_map/ppermute | solution.py:260
  33.7 21.0 %collective-permute-start.4 = (bf16[528,128]{1,0:T(8,128)(2,1)}, bf16[528,128]{1,0:T(8,128)(2,1)S(1)}, u32[]{:S(2)}, u32[]{:S(2)}) collective-permute-start(bf16[528,128]{1,0:T(8,128)(2,1)} %copy-done.4), channel_id=1, source_target_pairs={{0,8},{8,16},{16,24},{24,32},{32,40},{40,48},{48,56},{56,64},{64,7... | collective-permute-start | bytes 405512 | tf_op jit(solution)/shard_map/ppermute | solution.py:276
  35.7 19.1 %collective-permute-start.5 = (bf16[528,128]{1,0:T(8,128)(2,1)S(1)}, bf16[528,128]{1,0:T(8,128)(2,1)S(1)}, u32[]{:S(2)}, u32[]{:S(2)}) collective-permute-start(bf16[528,128]{1,0:T(8,128)(2,1)S(1)} %get-tuple-element.47), channel_id=1, source_target_pairs={{8,0},{16,8},{24,16},{32,24},{40,32},{48,40},{56,48},{64,56},{72,6... | collective-permute-start | bytes 405512 | tf_op jit(solution)/shard_map/ppermute | solution.py:276
  39.3 15.4 %collective-permute-start.6 = (bf16[528,128]{1,0:T(8,128)(2,1)S(1)}, bf16[528,128]{1,0:T(8,128)(2,1)S(1)}, u32[]{:S(2)}, u32[]{:S(2)}) collective-permute-start(bf16[528,128]{1,0:T(8,128)(2,1)S(1)} %get-tuple-element.48), channel_id=1, source_target_pairs={{0,16},{8,24},{16,32},{24,40},{32,48},{40,56},{48,64},{56,72},{64,... | collective-permute-start | bytes 405512 | tf_op jit(solution)/shard_map/ppermute | solution.py:276
  47.3 10.2 %collective-permute-start.7 = (bf16[528,128]{1,0:T(8,128)(2,1)S(1)}, bf16[528,128]{1,0:T(8,128)(2,1)S(1)}, u32[]{:S(2)}, u32[]{:S(2)}) collective-permute-start(bf16[528,128]{1,0:T(8,128)(2,1)S(1)} %get-tuple-element.49), channel_id=1, source_target_pairs={{16,0},{24,8},{32,16},{40,24},{48,32},{56,40},{64,48},{72,56},{80,... | collective-permute-start | bytes 405512 | tf_op jit(solution)/shard_map/ppermute | solution.py:276
  49.2 1.1 %copy-start.8 = (bf16[512,640]{1,0:T(8,128)(2,1)S(1)}, bf16[512,640]{1,0:T(8,128)(2,1)}, u32[]{:S(2)}) copy-start(bf16[512,640]{1,0:T(8,128)(2,1)} %copy-done.7) | copy-start | bytes 1966084
  58.4 16.8 %collective-permute-start.10 = (bf16[128,768]{1,0:T(8,128)(2,1)S(1)}, bf16[128,768]{1,0:T(8,128)(2,1)S(1)}, u32[]{:S(2)}, u32[]{:S(2)}) collective-permute-start(bf16[128,768]{1,0:T(8,128)(2,1)S(1)} %get-tuple-element.54), channel_id=1, source_target_pairs={{0,1},{1,2},{2,3},{3,4},{4,5},{5,6},{6,7},{7,0},{8,9},{9,10},{10,1... | collective-permute-start | bytes 589832 | tf_op jit(solution)/shard_map/ppermute | solution.py:260
  60.4 14.8 %collective-permute-start.11 = (bf16[128,768]{1,0:T(8,128)(2,1)S(1)}, bf16[128,768]{1,0:T(8,128)(2,1)S(1)}, u32[]{:S(2)}, u32[]{:S(2)}) collective-permute-start(bf16[128,768]{1,0:T(8,128)(2,1)S(1)} %get-tuple-element.55), channel_id=1, source_target_pairs={{0,2},{1,3},{2,4},{3,5},{4,6},{5,7},{6,0},{7,1},{8,14},{9,15},{10,... | collective-permute-start | bytes 589832 | tf_op jit(solution)/shard_map/ppermute | solution.py:270
  63.4 11.8 %collective-permute-start.12 = (bf16[128,768]{1,0:T(8,128)(2,1)S(1)}, bf16[128,768]{1,0:T(8,128)(2,1)S(1)}, u32[]{:S(2)}, u32[]{:S(2)}) collective-permute-start(bf16[128,768]{1,0:T(8,128)(2,1)S(1)} %get-tuple-element.56), channel_id=1, source_target_pairs={{0,7},{1,0},{2,1},{3,2},{4,3},{5,4},{6,5},{7,6},{8,15},{9,8},{10,9... | collective-permute-start | bytes 589832 | tf_op jit(solution)/shard_map/ppermute | solution.py:260
  68.1 15.8 %collective-permute-start.8 = (bf16[128,768]{1,0:T(8,128)(2,1)S(1)}, bf16[128,768]{1,0:T(8,128)(2,1)S(1)}, u32[]{:S(2)}, u32[]{:S(2)}) collective-permute-start(bf16[128,768]{1,0:T(8,128)(2,1)S(1)} %get-tuple-element.52), channel_id=1, source_target_pairs={{0,1},{1,2},{2,3},{3,4},{4,5},{5,6},{6,7},{7,0},{8,9},{9,10},{10,1... | collective-permute-start | bytes 589832 | tf_op jit(solution)/shard_map/ppermute | solution.py:260
  71.1 12.8 %collective-permute-start.9 = (bf16[128,768]{1,0:T(8,128)(2,1)S(1)}, bf16[128,768]{1,0:T(8,128)(2,1)S(1)}, u32[]{:S(2)}, u32[]{:S(2)}) collective-permute-start(bf16[128,768]{1,0:T(8,128)(2,1)S(1)} %get-tuple-element.53), channel_id=1, source_target_pairs={{0,7},{1,0},{2,1},{3,2},{4,3},{5,4},{6,5},{7,6},{8,15},{9,8},{10,9... | collective-permute-start | bytes 589832 | tf_op jit(solution)/shard_map/ppermute | solution.py:260
  75.9 10.4 %collective-permute-start.13 = (bf16[128,768]{1,0:T(8,128)(2,1)S(1)}, bf16[128,768]{1,0:T(8,128)(2,1)S(1)}, u32[]{:S(2)}, u32[]{:S(2)}) collective-permute-start(bf16[128,768]{1,0:T(8,128)(2,1)S(1)} %get-tuple-element.57), channel_id=1, source_target_pairs={{0,2},{1,3},{2,4},{3,5},{4,6},{5,7},{6,0},{7,1},{8,10},{9,11},{10,... | collective-permute-start | bytes 589832 | tf_op jit(solution)/shard_map/ppermute | solution.py:260
  79.2 10.6 %collective-permute-start.14 = (bf16[128,768]{1,0:T(8,128)(2,1)S(1)}, bf16[128,768]{1,0:T(8,128)(2,1)S(1)}, u32[]{:S(2)}, u32[]{:S(2)}) collective-permute-start(bf16[128,768]{1,0:T(8,128)(2,1)S(1)} %get-tuple-element.58), channel_id=1, source_target_pairs={{0,6},{1,7},{2,0},{3,1},{4,2},{5,3},{6,4},{7,5},{8,14},{9,15},{10,... | collective-permute-start | bytes 589832 | tf_op jit(solution)/shard_map/ppermute | solution.py:260

commit v3 on v2

v3 whole, which is shorter than its diff:
```python
import functools

import jax
import jax.numpy as jnp
from jax import lax
from jax.experimental import pallas as pl
from jax.experimental.pallas import tpu as pltpu
from jax.sharding import PartitionSpec as P

NT = 32
FD = 8
NS = NT * FD
EDGE = 3 * NT
P_SIZE = 1024
NOPS = 316
WIDTH = 3
REACH = 2
BOX = 384
PAIR = 640
CAP = 128
STEPS = (2, -2, 1, -1)
SLOTS = CAP * len(STEPS)
BUF = 2 * NS + 16
RANKS = 8
BF = jnp.bfloat16
SMEM = pl.BlockSpec(memory_space=pltpu.SMEM)
VMEM = pl.BlockSpec(memory_space=pltpu.VMEM)
HBM = pl.BlockSpec(memory_space=pltpu.HBM)
EDGE_PARTS = 4
F32 = jnp.float32

NN = (((1,), (0,)), ((), ()))
NTR = (((1,), (1,)), ((), ()))
TN = (((0,), (0,)), ((), ()))


def dot(a, b, dims=NN):
    return lax.dot_general(a, b, dims, preferred_element_type=F32)


def iota(shape, dim):
    return lax.broadcasted_iota(jnp.int32, shape, dim)


def split(value):
    high = value.astype(BF)
    return high, (value - high.astype(F32)).astype(BF)


def local_place(shape, dim):
    at = iota(shape, dim)
    return at >> 3, at & 7


def edge_place(shape, dim):
    at = iota(shape, dim)
    return at & 31, at >> 5


def band(columns, diff, same):
    total = jnp.zeros(diff.shape, F32)
    for k in range(2 * WIDTH + 1):
        total = jnp.where(diff == k, columns[:, k : k + 1], total)
    return jnp.where(same, total, 0.0)


def exact(a, b, dims=NN):
    return lax.dot_general(a, b, dims, precision=lax.Precision.HIGHEST, preferred_element_type=F32)


def own_columns(coeffs):
    _, f_row = local_place((NS, FD), 0)
    return exact((f_row == iota((NS, FD), 1)).astype(F32), coeffs, NTR)


def sample_weights(weights):
    t_row, _ = local_place((NS, NT), 0)
    same = t_row == iota((NS, NT), 1)
    return jnp.sum(jnp.where(same, weights, 0.0), axis=1, keepdims=True)


def one_hot(rows, index):
    return (iota((rows, index.shape[1]), 0) == index).astype(BF)


def edge_kernel(place, rad_all, anterp_all, weights_all, out, rad, anterp, weights, sems):
    parts = EDGE_PARTS
    depth = P_SIZE // parts
    copies = [
        pltpu.make_async_copy(anterp_all, anterp, sems.at[parts]),
        pltpu.make_async_copy(weights_all, weights, sems.at[parts + 1]),
    ]
    for i in range(parts):
        cols = pl.ds(i * depth, depth)
        copies.append(pltpu.make_async_copy(rad_all.at[:, cols], rad.at[:, cols], sems.at[i]))
    for copy in copies:
        copy.start()
    t_row, j_row = edge_place((EDGE, NS), 0)
    t_col, f_col = local_place((EDGE, NS), 1)
    first = jnp.where(place[1] == 0, FD - WIDTH, 0)
    pick = jnp.logical_and(t_row == t_col, f_col == j_row + first).astype(BF)
    t_lane, _ = edge_place((NT, CAP), 1)
    _, j_lane = edge_place((FD, CAP), 1)
    copies[0].wait()
    copies[1].wait()
    spread = exact(weights[...], (iota((NT, CAP), 0) == t_lane).astype(F32))
    coeffs = exact(anterp[...], (iota((FD, CAP), 0) == j_lane + first).astype(F32)) * spread
    high, low = split(jnp.concatenate([coeffs, jnp.zeros((1, CAP), F32)], axis=0))
    out[2 * EDGE :, :] = jnp.zeros((16, P_SIZE), BF)
    out[2 * EDGE :, 0:CAP] = jnp.concatenate([high.astype(F32), low.astype(F32)], axis=0).astype(BF)
    for i in range(parts):
        copies[2 + i].wait()
        cols = slice(i * depth, (i + 1) * depth)
        for c in range(2):
            out[c * EDGE : (c + 1) * EDGE, cols] = dot(pick, rad[c * NS : (c + 1) * NS, cols]).astype(BF)


def radiate(rad, cur, rows):
    with_re = dot(rad, cur[0])
    with_im = dot(rad, cur[1])
    return with_re[:rows] - with_im[rows:], with_im[:rows] + with_re[rows:]


def field_kernel(rad, cur, field):
    re, im = radiate(rad[...], cur, NS)
    field[:, :BOX] = re
    field[:, BOX:] = im


def prepare_kernel(
    place, field, interp, pair_src, pair_op, pair_target, oper,
    inter, halo_mat, src_pick, oper_slot, slot_ids, oper_own, own_rows,
):
    columns = own_columns(interp[...])
    shape = (NS, NS)
    t_row, g_row = local_place(shape, 0)
    t_col, f_col = local_place(shape, 1)
    mat_hi, mat_lo = split(band(columns, f_col - g_row + WIDTH, t_row == t_col))
    f_hi, f_lo = split(field[...])
    inter[...] = dot(mat_hi, f_hi) + dot(mat_lo, f_hi) + dot(mat_hi, f_lo)
    shape = (NS, EDGE)
    t_row, g_row = local_place(shape, 0)
    t_col, j_col = edge_place(shape, 1)
    for side in range(2):
        base = jnp.where(place[1] == side, 0, FD + WIDTH)
        mats = split(band(columns, j_col - g_row + base, t_row == t_col))
        for part in range(2):
            halo_mat[side, part] = mats[part]

    src_row, op_row = pair_src[...].reshape(1, PAIR), pair_op[...].reshape(1, PAIR)
    ahead = pair_target[...].reshape(1, PAIR) - place[2] * BOX
    step_of = jnp.full((1, PAIR), -REACH, jnp.int32)
    for k in range(1 - REACH, REACH + 1):
        step_of = step_of + (ahead >= k * BOX).astype(jnp.int32)
    target = ahead - step_of * BOX
    row = iota((8, PAIR), 0)
    own_rows[...] = jnp.where(row == 0, src_row, jnp.where(step_of == 0, target, -1))
    step_of = step_of * (2 * place[1] - 1)
    digits = jnp.ones((8, PAIR), jnp.int32)
    for k, value in enumerate((src_row, op_row, target)):
        digits = jnp.where(row == 2 * k, value >> 4, digits)
        digits = jnp.where(row == 2 * k + 1, value & 15, digits)
    digits = digits.astype(F32).astype(BF)

    at = iota((8, PAIR), 0)
    cls = jnp.full((1, PAIR), -1, jnp.int32)
    for k, step in enumerate(STEPS):
        cls = jnp.where(step_of == step, k, cls)
    member = (at == cls).astype(BF)
    earlier = (iota((PAIR, PAIR), 0) < iota((PAIR, PAIR), 1)).astype(BF)
    before = dot(member, earlier) * member.astype(F32)
    rank = jnp.sum(before, axis=0, keepdims=True).astype(jnp.int32)
    slot = jnp.where(cls >= 0, cls * CAP + rank, -1)
    chosen = (iota((SLOTS, PAIR), 0) == slot).astype(BF)
    named = dot(digits, chosen, NTR)
    src = (16.0 * named[0:1] + named[1:2]).astype(jnp.int32)
    opn = (16.0 * named[2:3] + named[3:4]).astype(jnp.int32)
    filled = named[6:7] > 0.5
    src_pick[...] = one_hot(BOX, src)
    oper_slot[...] = dot(oper[...], one_hot(NOPS, opn)).astype(BF)
    oper_own[...] = dot(oper[...], one_hot(NOPS, op_row)).astype(BF)
    row = iota((16, SLOTS), 0)
    t_hi = jnp.where(filled, named[4:5], float(BOX // 16))
    t_lo = jnp.where(filled, named[5:6], 0.0)
    slot_ids[...] = jnp.where(row == 0, t_hi, jnp.where(row == 1, t_lo, 0.0)).astype(BF)


def with_edge(inter, mats, edge, cur):
    re, im = radiate(edge[: 2 * EDGE, :], cur, EDGE)
    halo = jnp.concatenate([re, im], axis=1).astype(BF)
    return inter[...] + dot(mats[0], halo) + dot(mats[1], halo)


def first_edge_kernel(inter, halo_mat, edge, cur, out):
    out[...] = with_edge(inter, (halo_mat[0, 0], halo_mat[0, 1]), edge, cur)


def multiply(oper, re, im):
    o_re, o_im = oper[:NS, :].astype(F32), oper[NS:, :].astype(F32)
    return (o_re * re - o_im * im).astype(BF), (o_re * im + o_im * re).astype(BF)


def send_kernel(inter, halo_mat, edge, cur, src_pick, oper_slot, slot_ids, out0, out1, out2, out3, parts):
    whole = with_edge(inter, (halo_mat[1, 0], halo_mat[1, 1]), edge, cur)
    hi, lo = split(whole)
    parts[0] = hi
    parts[1] = lo
    pick = src_pick[...]
    re = dot(hi[:, :BOX], pick) + dot(lo[:, :BOX], pick)
    im = dot(hi[:, BOX:], pick) + dot(lo[:, BOX:], pick)
    c_re, c_im = multiply(oper_slot[...], re, im)
    for k, out in enumerate((out0, out1, out2, out3)):
        cols = slice(k * CAP, (k + 1) * CAP)
        out[0:NS, :] = c_re[:, cols]
        out[NS : 2 * NS, :] = c_im[:, cols]
        out[2 * NS :, :] = slot_ids[:, cols]


def own_kernel(parts, own_rows, oper_own, own):
    pick = one_hot(BOX, own_rows[0:1, :])
    hi, lo = parts[0], parts[1]
    re = dot(hi[:, :BOX], pick) + dot(lo[:, :BOX], pick)
    im = dot(hi[:, BOX:], pick) + dot(lo[:, BOX:], pick)
    c_re, c_im = multiply(oper_own[...], re, im)
    table = one_hot(BOX, own_rows[1:2, :])
    own[:, :BOX] = dot(c_re, table, NTR)
    own[:, BOX:] = dot(c_im, table, NTR)


def own_matrix_kernel(rad, anterp, weights, out):
    columns = own_columns(anterp[...]) * sample_weights(weights[...])
    shape = (NS, NS)
    t_row, f_row = local_place(shape, 0)
    t_col, g_col = local_place(shape, 1)
    mat_hi, mat_lo = split(band(columns, g_col - f_row + WIDTH, t_row == t_col))
    for c in range(2):
        r = rad[c * NS : (c + 1) * NS, :]
        out[:, c * NS : (c + 1) * NS] = dot(r, mat_hi, TN) + dot(r, mat_lo, TN)


def matrix_kernel(place, own, edge0, edge1, out):
    shape = (EDGE, NS)
    t_row, j_row = edge_place(shape, 0)
    t_col, g_col = local_place(shape, 1)
    mats = []
    for side, edge in enumerate((edge0, edge1)):
        tail = edge[2 * EDGE :, 0:CAP].astype(F32)
        cols = (tail[0:8] + tail[8:16]).T[:EDGE]
        base = jnp.where(place[1] == side, 2 * WIDTH, WIDTH - FD)
        mats.append(band(cols, g_col - j_row + base, t_row == t_col))
    high, low = split(jnp.concatenate(mats, axis=0))
    me = place[0]
    for c in range(2):
        rows = slice(c * EDGE, (c + 1) * EDGE)
        edges = jnp.concatenate([edge0[rows, :], edge1[rows, :]], axis=0)
        cols = slice(c * NS, (c + 1) * NS)
        q = (own[:, cols] + dot(edges, high, TN) + dot(edges, low, TN)).astype(BF)
        for d in range(RANKS):
            rows = pl.ds(pl.multiple_of(((d - me) & (RANKS - 1)) * CAP, CAP), CAP)
            out[rows, cols] = q[d * CAP : (d + 1) * CAP]


def far_kernel(own, matrix, got0, got1, got2, got3, up3, far4, down3, stack):
    gots = (got0, got1, got2, got3)
    ids = jnp.concatenate([g[2 * NS :, :].astype(F32) for g in gots], axis=1)
    index = (16.0 * ids[0:1] + ids[1:2]).astype(jnp.int32)
    table = one_hot(BOX, index)
    re = own[:, :BOX] + dot(jnp.concatenate([g[0:NS, :] for g in gots], axis=1), table, NTR)
    im = own[:, BOX:] + dot(jnp.concatenate([g[NS : 2 * NS, :] for g in gots], axis=1), table, NTR)
    re, im = re.astype(BF), im.astype(BF)
    stack[0:NS, :BOX] = re
    stack[0:NS, BOX:] = im
    stack[NS:, :BOX] = im
    stack[NS:, BOX:] = -re
    for j, out in ((3, up3), (4, far4), (5, down3)):
        out[...] = dot(matrix[j * CAP : (j + 1) * CAP, :], stack[...]).astype(BF)


def near_kernel(matrix, stack, up1, down1, keep):
    for j, out in ((1, up1), (7, down1)):
        out[...] = dot(matrix[j * CAP : (j + 1) * CAP, :], stack[...]).astype(BF)
    for i, j in enumerate((0, 2, 6)):
        keep[i] = dot(matrix[j * CAP : (j + 1) * CAP, :], stack[...])


def relay_kernel(place, keep, from_up3, from_far4, from_down3, up2, down2):
    far = from_far4[...].astype(F32)
    even = place[1] == 0
    up2[...] = (keep[1] + from_up3[...].astype(F32) + jnp.where(even, far, 0.0)).astype(BF)
    down2[...] = (keep[2] + from_down3[...].astype(F32) + jnp.where(even, 0.0, far)).astype(BF)


def sum_kernel(keep, up1, down1, up2, down2, out):
    total = keep[0]
    for part in (up1, down1, up2, down2):
        total = total + part[...].astype(F32)
    out[0] = total[:, :BOX].astype(BF)
    out[1] = total[:, BOX:].astype(BF)


def call(kernel, outs, *args, scratch=(), flops=10**8, name=None, vmem=24, **kw):
    shapes = [jax.ShapeDtypeStruct(s, d) for s, d in outs]
    moved = sum(a.size * a.dtype.itemsize for a in args) + sum(s.size * s.dtype.itemsize for s in shapes)
    return pl.pallas_call(
        kernel,
        out_shape=shapes,
        scratch_shapes=list(scratch),
        compiler_params=pltpu.CompilerParams(vmem_limit_bytes=vmem * 2**20),
        cost_estimate=pl.CostEstimate(flops=flops, bytes_accessed=moved, transcendentals=0),
        name=name,
        **kw,
    )(*args)


def around(value, axis, steps):
    count = lax.axis_size(axis)
    return lax.ppermute(value, axis, [(i, (i + steps) % count) for i in range(count)])


def outward(value, steps):
    groups, count = lax.axis_size("box"), lax.axis_size("samp")
    pairs = []
    for b in range(groups):
        for i in range(count):
            j = (i + (steps if b % 2 == 0 else -steps)) % count
            pairs.append((b * count + i, b * count + j))
    return lax.ppermute(value, ("box", "samp"), pairs)


def across(value):
    groups = lax.axis_size("box")
    return lax.ppermute(value, "box", [(b, b ^ 1) for b in range(groups)])


def sideways(value, steps):
    groups = lax.axis_size("box")
    pairs = [(b, b + steps * (1 if b % 2 else -1)) for b in range(groups)]
    return lax.ppermute(value, "box", [(b, to) for b, to in pairs if 0 <= to < groups])


def on_device(
    currents, radiation, interp, anterp, weights, operators, pair_src, pair_op, pair_target
):
    rad = jnp.transpose(radiation, (0, 2, 3, 1)).reshape(2 * NS, P_SIZE)
    oper = operators.reshape(2 * NS, NOPS)
    weights = weights.reshape(1, NT)
    group = lax.axis_index("box")
    place = jnp.stack([lax.axis_index("samp"), group % 2, group]).astype(jnp.int32)
    (edge,) = call(
        edge_kernel,
        [((2 * EDGE + 16, P_SIZE), BF)],
        place, rad, anterp, weights,
        scratch=[
            pltpu.VMEM((2 * NS, P_SIZE), BF),
            pltpu.VMEM((2 * WIDTH + 1, FD), F32),
            pltpu.VMEM((1, NT), F32),
            pltpu.SemaphoreType.DMA((EDGE_PARTS + 2,)),
        ],
        vmem=60,
        name="edge",
        in_specs=[SMEM] + [HBM] * 3,
    )
    edge0 = outward(edge, 1)

    (field,) = call(field_kernel, [((NS, 2 * BOX), F32)], rad, currents, flops=10**9, name="field")
    inter, halo_mat, src_pick, oper_slot, slot_ids, oper_own, own_rows = call(
        prepare_kernel,
        [
            ((NS, 2 * BOX), F32), ((2, 2, NS, EDGE), BF), ((BOX, SLOTS), BF),
            ((2 * NS, SLOTS), BF), ((16, SLOTS), BF), ((2 * NS, PAIR), BF), ((8, PAIR), jnp.int32),
        ],
        place, field, interp, pair_src, pair_op, pair_target, oper,
        flops=10**9,
        name="prepare",
        in_specs=[SMEM] + [VMEM] * 6,
    )
    (own_matrix,) = call(
        own_matrix_kernel, [((P_SIZE, 2 * NS), F32)], rad, anterp, weights, flops=10**9, name="own_matrix"
    )
    edge0, inter, own_matrix = lax.optimization_barrier((edge0, inter, own_matrix))
    edge1 = across(edge0)
    (inter,) = call(
        first_edge_kernel, [((NS, 2 * BOX), F32)], inter, halo_mat, edge0, currents,
        flops=4 * 10**8, name="first_edge",
    )
    *buffers, parts = call(
        send_kernel,
        [((BUF, CAP), BF)] * 4 + [((2, NS, 2 * BOX), BF)],
        inter, halo_mat, edge1, currents, src_pick, oper_slot, slot_ids,
        flops=4 * 10**8,
        name="send",
    )
    gots = [sideways(b, step) for b, step in zip(buffers, STEPS)]
    (own,) = call(
        own_kernel,
        [((NS, 2 * BOX), F32)],
        parts, own_rows, oper_own,
        flops=10**9,
        name="own",
    )
    (matrix,) = call(
        matrix_kernel,
        [((P_SIZE, 2 * NS), BF)],
        place, own_matrix, edge0, edge1,
        flops=10**9,
        name="matrix",
        in_specs=[SMEM] + [VMEM] * 3,
    )
    block = (CAP, 2 * BOX)
    up3, far4, down3, stack = call(
        far_kernel,
        [(block, BF)] * 3 + [((2 * NS, 2 * BOX), BF)],
        own, matrix, *gots,
        flops=5 * 10**8,
        name="far",
    )
    from_up3 = around(up3, "samp", 1)
    from_far4 = outward(far4, 2)
    from_down3 = around(down3, "samp", -1)
    up1, down1, keep = call(
        near_kernel,
        [(block, BF)] * 2 + [((3,) + block, F32)],
        matrix, stack,
        flops=5 * 10**8,
        name="near",
    )
    from_up1 = around(up1, "samp", 1)
    from_down1 = around(down1, "samp", -1)
    up2, down2 = call(
        relay_kernel,
        [(block, BF)] * 2,
        place, keep, from_up3, from_far4, from_down3,
        name="relay",
        in_specs=[SMEM] + [VMEM] * 4,
    )
    from_up2 = around(up2, "samp", 2)
    from_down2 = around(down2, "samp", -2)
    (out,) = call(
        sum_kernel,
        [((2, P_SIZE // RANKS, BOX), BF)],
        keep, from_up1, from_down1, from_up2, from_down2,
        name="total",
    )
    return out


def solution(mesh):
    return jax.shard_map(
        on_device,
        mesh=mesh,
        in_specs=(
            P(None, None, "box"),
            P(None, None, None, "samp"),
            P(None, "samp"),
            P(None, "samp"),
            P(),
            P(None, None, "samp", None),
            P("box"),
            P("box"),
            P("box"),
        ),
        out_specs=P(None, "samp", "box"),
        check_vma=False,
    )
```

time: 91.2 us -> 81.2 us (0.89)
  the two profiles are of different devices: /device:TPU:30 before, /device:TPU:28 now
where the time goes in v3:
time: 81.2 us; the launch traced here: 80.7 us
  starting transfers between devices  46.2 us (57%)
  Pallas kernels  17.8 us (22%)
  waiting for transfers between devices  13.1 us (16%)
  local copies, waits for them, and re-layouts  2.6 us (3%)
    ppermute x6, starting transfers between devices, around(): lax.ppermute(value, axis, [(i, (i + steps) % count) for i in range(count)])  20.2 us
    pallas_call x12, Pallas kernels, call(): pl.pallas_call(kernel, out_shape=shapes, scratch_shapes=list(scratch), co...  17.8 us
    ppermute x4, starting transfers between devices, sideways(): lax.ppermute(value, 'box', [(b, to) for b, to in pairs if 0 <= to < groups])  14.3 us
    ppermute x2, starting transfers between devices, outward(): return lax.ppermute(value, ('box', 'samp'), pairs)  8.22 us
    ppermute x6, waiting for transfers between devices, around(): lax.ppermute(value, axis, [(i, (i + steps) % count) for i in range(count)])  8.08 us
    ppermute x2, waiting for transfers between devices, outward(): return lax.ppermute(value, ('box', 'samp'), pairs)  4.6 us
    ppermute x1, starting transfers between devices, across(): return lax.ppermute(value, 'box', [(b, b ^ 1) for b in range(groups)])  3.54 us
    unnamed x20, local copies, waits for them, and re-layouts  2.6 us
  transfers between devices with their start and end apart: 13, of which 4 were waited for; matrix products, arithmetic and copies ran while one was open for 0% of the time, Pallas kernels for 14%

profile of v3, /device:TPU:28, one launch (start us, length us, event | category | flops | bytes accessed | tf_op | source)
XLA Modules:
  0.0 80.7 jit_solution(1379740677545592539)
XLA Ops:
  0.0 0.6 pad_add_fusion.place
  0.6 3.2 %edge.1 = bf16[208,1024]{1,0:T(8,128)(2,1)} custom-call(s32[3]{0:T(128)} %pad_add_fusion.place, bf16[512,1024]{1,0:T(8,128)(2,1)} %bitcast.8, f32[7,8]{1,0:T(8,128)} %anterp.1, f32[1,32]{1,0:T(1,128)} %bitcast.11), custom_call_target="tpu_custom_call" | custom-call | flops 100000000 | bytes 1474924 | tf_op jit(solution)/shard_map/edge/pallas_call | solution.py:304
  3.8 4.4 %collective-permute-start = (bf16[208,1024]{1,0:T(8,128)(2,1)}, bf16[208,1024]{1,0:T(8,128)(2,1)S(1)}, u32[]{:S(2)}, u32[]{:S(2)}) collective-permute-start(bf16[208,1024]{1,0:T(8,128)(2,1)} %edge.1), channel_id=1, source_target_pairs={{0,1},{1,2},{2,3},{3,4},{4,5},{5,6},{6,7},{7,0},{8,15},{9,8},{10,9... | collective-permute-start | bytes 1277960 | tf_op jit(solution)/shard_map/ppermute | solution.py:327
  8.2 1.2 %copy-done.1 = bf16[2,1024,32,8]{1,3,2,0:T(8,128)(2,1)S(1)} copy-done((bf16[2,1024,32,8]{1,3,2,0:T(8,128)(2,1)S(1)}, bf16[2,1024,32,8]{1,3,2,0:T(8,128)(2,1)}, u32[]{:S(2)}) %copy-start.1) | copy-done | bytes 1048600
  9.5 0.7 copy-done.3
  10.1 0.7 copy-done.4
  10.8 1.5 %own_matrix.1.own = f32[1024,512]{1,0:T(8,128)S(1)} custom-call(bf16[512,1024]{1,0:T(8,128)(2,1)S(1)} %bitcast.9, f32[7,8]{1,0:T(8,128)S(1)} %copy-done.3, f32[1,32]{1,0:T(1,128)S(1)} %bitcast.12), custom_call_target="tpu_custom_call" | custom-call | flops 1000000000 | bytes 3146080 | tf_op jit(solution)/shard_map/own_matrix/pallas_call | solution.py:304
  12.4 1.3 %field.1 = f32[256,768]{1,0:T(8,128)S(1)} custom-call(bf16[512,1024]{1,0:T(8,128)(2,1)S(1)} %bitcast.10, bf16[2,1024,384]{2,1,0:T(8,128)(2,1)S(1)} %copy-done), custom_call_target="tpu_custom_call" | custom-call | flops 1000000000 | bytes 3407872 | tf_op jit(solution)/shard_map/field/pallas_call | solution.py:304
  13.7 2.9 %prepare.1 = (f32[256,768]{1,0:T(8,128)S(1)}, bf16[2,2,256,96]{3,2,1,0:T(8,128)(2,1)S(1)}, bf16[384,512]{1,0:T(8,128)(2,1)S(1)}, bf16[512,512]{1,0:T(8,128)(2,1)...) custom-call(s32[3]{0:T(128)S(1)} %copy-done.2, f32[256,768]{1,0:T(8,128)S(1)} %field.1, ...), custom_call_target="tpu_custom_call" | custom-call | flops 1000000000 | bytes 3710700 | tf_op jit(solution)/shard_map/prepare/pallas_call | solution.py:304
  16.6 4.6 %collective-permute-done.edge0.edge = bf16[208,1024]{1,0:T(8,128)(2,1)S(1)} collective-permute-done((bf16[208,1024]{1,0:T(8,128)(2,1)}, bf16[208,1024]{1,0:T(8,128)(2,1)S(1)}, u32[]{:S(2)}, u32[]{:S(2)}) %collective-permute-start) | collective-permute-done | bytes 426016 | tf_op jit(solution)/shard_map/ppermute | solution.py:327
  21.2 3.5 %collective-permute-start.1 = (bf16[208,1024]{1,0:T(8,128)(2,1)S(1)}, bf16[208,1024]{1,0:T(8,128)(2,1)S(1)}, u32[]{:S(2)}, u32[]{:S(2)}) collective-permute-start(bf16[208,1024]{1,0:T(8,128)(2,1)S(1)} %collective-permute-done.edge0.edge), channel_id=1, source_target_pairs={{0,8},{8,0},{16,24},{24,16},{32,40},{40,32},{48,56},{56,48},{64,72... | collective-permute-start | bytes 1277960 | tf_op jit(solution)/shard_map/ppermute | solution.py:332
  24.7 0.9 %first_edge.1.inter = f32[256,768]{1,0:T(8,128)S(1)} custom-call(f32[256,768]{1,0:T(8,128)S(1)} %get-tuple-element.32.inter, bf16[2,2,256,96]{3,2,1,0:T(8,128)(2,1)S(1)} %get-tuple-element.33.halo_mat, bf16[208,1024]{1,0:T(8,128)(2,1)S(1)} %collective-permute-done.edge0.edge, bf16[2,1024,384]{2,1,0:T(8,128)(2,1)S(1)} %copy-done), custom_call_target="tpu_custom_call" | custom-call | flops 400000000 | bytes 3768320 | tf_op jit(solution)/shard_map/first_edge/pallas_call | solution.py:304
  26.1 1.6 %send.1 = (bf16[528,128]{1,0:T(8,128)(2,1)S(1)}, bf16[528,128]{1,0:T(8,128)(2,1)S(1)}, bf16[528,128]{1,0:T(8,128)(2,1)S(1)}, bf16[528,128]{1,0:T(8,128)(2,1)S(1)}, bf16[2,256,768]{2,1,0:T(8,128)(2,1)S(1)}) custom-call(f32[256,768]{1,0:T(8,128)S(1)} %first_edge.1.inter, bf16[2,2,256,96]{3,2,1,0:T(8,128)(2,1)S(1)} %get-tuple-element.33.halo_mat, ...), custom_call_target="tpu_custom_call" | custom-call | flops 400000000 | bytes 5242880 | tf_op jit(solution)/shard_map/send/pallas_call | solution.py:304
  27.7 2.4 %collective-permute-start.2 = (bf16[528,128]{1,0:T(8,128)(2,1)S(1)}, bf16[528,128]{1,0:T(8,128)(2,1)S(1)}, u32[]{:S(2)}, u32[]{:S(2)}) collective-permute-start(bf16[528,128]{1,0:T(8,128)(2,1)S(1)} %get-tuple-element.40), channel_id=1, source_target_pairs={{8,24},{16,0},{24,40},{32,16},{40,56},{48,32},{56,72},{64,48},{72,... | collective-permute-start | bytes 405512 | tf_op jit(solution)/shard_map/ppermute | solution.py:338
  30.2 3.4 %collective-permute-start.3 = (bf16[528,128]{1,0:T(8,128)(2,1)S(1)}, bf16[528,128]{1,0:T(8,128)(2,1)S(1)}, u32[]{:S(2)}, u32[]{:S(2)}) collective-permute-start(bf16[528,128]{1,0:T(8,128)(2,1)S(1)} %get-tuple-element.41), channel_id=1, source_target_pairs={{0,16},{16,32},{24,8},{32,48},{40,24},{48,64},{56,40},{64,80},{72,... | collective-permute-start | bytes 405512 | tf_op jit(solution)/shard_map/ppermute | solution.py:338
  33.6 1.9 %collective-permute-start.4 = (bf16[528,128]{1,0:T(8,128)(2,1)S(1)}, bf16[528,128]{1,0:T(8,128)(2,1)S(1)}, u32[]{:S(2)}, u32[]{:S(2)}) collective-permute-start(bf16[528,128]{1,0:T(8,128)(2,1)S(1)} %get-tuple-element.42), channel_id=1, source_target_pairs={{8,16},{16,8},{24,32},{32,24},{40,48},{48,40},{56,64},{64,56},{72,... | collective-permute-start | bytes 405512 | tf_op jit(solution)/shard_map/ppermute | solution.py:338
  35.5 6.5 %collective-permute-start.5 = (bf16[528,128]{1,0:T(8,128)(2,1)S(1)}, bf16[528,128]{1,0:T(8,128)(2,1)S(1)}, u32[]{:S(2)}, u32[]{:S(2)}) collective-permute-start(bf16[528,128]{1,0:T(8,128)(2,1)S(1)} %get-tuple-element.43), channel_id=1, source_target_pairs={{0,8},{8,0},{16,24},{24,16},{32,40},{40,32},{48,56},{56,48},{64,72... | collective-permute-start | bytes 405512 | tf_op jit(solution)/shard_map/ppermute | solution.py:338
  42.1 1.6 %own.1 = f32[256,768]{1,0:T(8,128)S(1)} custom-call(bf16[2,256,768]{2,1,0:T(8,128)(2,1)S(1)} %get-tuple-element.37.parts, s32[8,640]{1,0:T(8,128)S(1)} %get-tuple-element.38.own_rows, bf16[512,640]{1,0:T(8,128)(2,1)S(1)} %get-tuple-element.39.oper_own), custom_call_target="tpu_custom_call" | custom-call | flops 1000000000 | bytes 2248704 | tf_op jit(solution)/shard_map/own/pallas_call | solution.py:304
  43.7 1.7 %matrix.1 = bf16[1024,512]{1,0:T(8,128)(2,1)S(1)} custom-call(s32[3]{0:T(128)S(1)} %copy-done.2, f32[1024,512]{1,0:T(8,128)S(1)} %own_matrix.1.own, bf16[208,1024]{1,0:T(8,128)(2,1)S(1)} %collective-permute-done.edge0.edge, bf16[208,1024]{1,0:T(8,128)(2,1)S(1)} %collective-permute-done.1.edge1.edge), custom_call_target="tpu_custom_call" | custom-call | flops 1000000000 | bytes 3997708 | tf_op jit(solution)/shard_map/matrix/pallas_call | solution.py:304
  45.4 0.9 %far.1 = (bf16[128,768]{1,0:T(8,128)(2,1)S(1)}, bf16[128,768]{1,0:T(8,128)(2,1)S(1)}, bf16[128,768]{1,0:T(8,128)(2,1)S(1)}, bf16[512,768]{1,0:T(8,128)(2,1)S(1)}) custom-call(f32[256,768]{1,0:T(8,128)S(1)} %own.1, bf16[1024,512]{1,0:T(8,128)(2,1)S(1)} %matrix.1, bf16[528,128]{1,0:T(8,128)(2,1)S(1)} %collective-permute-done.2.got0, ...), custom_call_target="tpu_custom_call" | custom-call | flops 500000000 | bytes 3751936 | tf_op jit(solution)/shard_map/far/pallas_call | solution.py:304
  46.4 1.9 %collective-permute-start.8 = (bf16[128,768]{1,0:T(8,128)(2,1)S(1)}, bf16[128,768]{1,0:T(8,128)(2,1)S(1)}, u32[]{:S(2)}, u32[]{:S(2)}) collective-permute-start(bf16[128,768]{1,0:T(8,128)(2,1)S(1)} %get-tuple-element.48), channel_id=1, source_target_pairs={{0,1},{1,2},{2,3},{3,4},{4,5},{5,6},{6,7},{7,0},{8,9},{9,10},{10,1... | collective-permute-start | bytes 589832 | tf_op jit(solution)/shard_map/ppermute | solution.py:317
  48.3 3.8 %collective-permute-start.9 = (bf16[128,768]{1,0:T(8,128)(2,1)S(1)}, bf16[128,768]{1,0:T(8,128)(2,1)S(1)}, u32[]{:S(2)}, u32[]{:S(2)}) collective-permute-start(bf16[128,768]{1,0:T(8,128)(2,1)S(1)} %get-tuple-element.49), channel_id=1, source_target_pairs={{0,2},{1,3},{2,4},{3,5},{4,6},{5,7},{6,0},{7,1},{8,14},{9,15},{10,... | collective-permute-start | bytes 589832 | tf_op jit(solution)/shard_map/ppermute | solution.py:327
  52.1 3.2 %collective-permute-start.10 = (bf16[128,768]{1,0:T(8,128)(2,1)S(1)}, bf16[128,768]{1,0:T(8,128)(2,1)S(1)}, u32[]{:S(2)}, u32[]{:S(2)}) collective-permute-start(bf16[128,768]{1,0:T(8,128)(2,1)S(1)} %get-tuple-element.50), channel_id=1, source_target_pairs={{0,7},{1,0},{2,1},{3,2},{4,3},{5,4},{6,5},{7,6},{8,15},{9,8},{10,9... | collective-permute-start | bytes 589832 | tf_op jit(solution)/shard_map/ppermute | solution.py:317
  55.4 0.7 near.1
  56.0 2.6 %collective-permute-start.6 = (bf16[128,768]{1,0:T(8,128)(2,1)S(1)}, bf16[128,768]{1,0:T(8,128)(2,1)S(1)}, u32[]{:S(2)}, u32[]{:S(2)}) collective-permute-start(bf16[128,768]{1,0:T(8,128)(2,1)S(1)} %get-tuple-element.46), channel_id=1, source_target_pairs={{0,1},{1,2},{2,3},{3,4},{4,5},{5,6},{6,7},{7,0},{8,9},{9,10},{10,1... | collective-permute-start | bytes 589832 | tf_op jit(solution)/shard_map/ppermute | solution.py:317
  58.7 4.5 %collective-permute-start.7 = (bf16[128,768]{1,0:T(8,128)(2,1)S(1)}, bf16[128,768]{1,0:T(8,128)(2,1)S(1)}, u32[]{:S(2)}, u32[]{:S(2)}) collective-permute-start(bf16[128,768]{1,0:T(8,128)(2,1)S(1)} %get-tuple-element.47), channel_id=1, source_target_pairs={{0,7},{1,0},{2,1},{3,2},{4,3},{5,4},{6,5},{7,6},{8,15},{9,8},{10,9... | collective-permute-start | bytes 589832 | tf_op jit(solution)/shard_map/ppermute | solution.py:317
  63.1 0.7 relay.1
  63.8 2.3 %collective-permute-start.11 = (bf16[128,768]{1,0:T(8,128)(2,1)S(1)}, bf16[128,768]{1,0:T(8,128)(2,1)S(1)}, u32[]{:S(2)}, u32[]{:S(2)}) collective-permute-start(bf16[128,768]{1,0:T(8,128)(2,1)S(1)} %get-tuple-element.51), channel_id=1, source_target_pairs={{0,2},{1,3},{2,4},{3,5},{4,6},{5,7},{6,0},{7,1},{8,10},{9,11},{10,... | collective-permute-start | bytes 589832 | tf_op jit(solution)/shard_map/ppermute | solution.py:317
  66.1 5.7 %collective-permute-start.12 = (bf16[128,768]{1,0:T(8,128)(2,1)S(1)}, bf16[128,768]{1,0:T(8,128)(2,1)S(1)}, u32[]{:S(2)}, u32[]{:S(2)}) collective-permute-start(bf16[128,768]{1,0:T(8,128)(2,1)S(1)} %get-tuple-element.52), channel_id=1, source_target_pairs={{0,6},{1,7},{2,0},{3,1},{4,2},{5,3},{6,4},{7,5},{8,14},{9,15},{10,... | collective-permute-start | bytes 589832 | tf_op jit(solution)/shard_map/ppermute | solution.py:317
  71.8 7.5 %collective-permute-done.11.up2 = bf16[128,768]{1,0:T(8,128)(2,1)S(1)} collective-permute-done((bf16[128,768]{1,0:T(8,128)(2,1)S(1)}, bf16[128,768]{1,0:T(8,128)(2,1)S(1)}, u32[]{:S(2)}, u32[]{:S(2)}) %collective-permute-start.11) | collective-permute-done | bytes 196640 | tf_op jit(solution)/shard_map/ppermute | solution.py:317
  79.3 0.6 collective-permute-done.12.down2
  79.9 0.8 total.1
  (27 shorter events, 0.5 us)
Async XLA Ops:
  3.8 8.5 %copy-start = (bf16[2,1024,384]{2,1,0:T(8,128)(2,1)S(1)}, bf16[2,1024,384]{2,1,0:T(8,128)(2,1)}, u32[]{:S(2)}) copy-start(bf16[2,1024,384]{2,1,0:T(8,128)(2,1)} %cur.5) | copy-start | bytes 4718596
  3.8 17.4 %collective-permute-start = (bf16[208,1024]{1,0:T(8,128)(2,1)}, bf16[208,1024]{1,0:T(8,128)(2,1)S(1)}, u32[]{:S(2)}, u32[]{:S(2)}) collective-permute-start(bf16[208,1024]{1,0:T(8,128)(2,1)} %edge.1), channel_id=1, source_target_pairs={{0,1},{1,2},{2,3},{3,4},{4,5},{5,6},{6,7},{7,0},{8,15},{9,8},{10,9... | collective-permute-start | bytes 1277960 | tf_op jit(solution)/shard_map/ppermute | solution.py:327
  8.2 1.2 %copy-start.1 = (bf16[2,1024,32,8]{1,3,2,0:T(8,128)(2,1)S(1)}, bf16[2,1024,32,8]{1,3,2,0:T(8,128)(2,1)}, u32[]{:S(2)}) copy-start(bf16[2,1024,32,8]{1,3,2,0:T(8,128)(2,1)} %param.10) | copy-start | bytes 3145732
  9.5 0.7 copy-start.3
  10.1 0.7 copy-start.4
  12.3 1.3 %copy-start.2 = (s32[3]{0:T(128)S(1)}, s32[3]{0:T(128)}, u32[]{:S(2)}) copy-start(s32[3]{0:T(128)} %pad_add_fusion.place) | copy-start | bytes 40
  12.4 1.3 %copy-start.5 = (bf16[2,32,8,316]{3,2,1,0:T(8,128)(2,1)S(1)}, bf16[2,32,8,316]{3,2,1,0:T(8,128)(2,1)}, u32[]{:S(2)}) copy-start(bf16[2,32,8,316]{3,2,1,0:T(8,128)(2,1)} %param.14) | copy-start | bytes 970756
  12.4 1.3 %copy-start.6 = (f32[7,8]{1,0:T(8,128)S(1)}, f32[7,8]{1,0:T(8,128)}, u32[]{:S(2)}) copy-start(f32[7,8]{1,0:T(8,128)} %interp.1) | copy-start | bytes 676
  12.4 1.3 %copy-start.7 = (s32[640]{0:T(1024)S(1)}, s32[640]{0:T(1024)}, u32[]{:S(2)}) copy-start(s32[640]{0:T(1024)} %pair_src.1) | copy-start | bytes 7684
  12.4 1.3 %copy-start.8 = (s32[640]{0:T(1024)S(1)}, s32[640]{0:T(1024)}, u32[]{:S(2)}) copy-start(s32[640]{0:T(1024)} %pair_op.1) | copy-start | bytes 7684
  12.4 1.3 %copy-start.9 = (s32[640]{0:T(1024)S(1)}, s32[640]{0:T(1024)}, u32[]{:S(2)}) copy-start(s32[640]{0:T(1024)} %pair_target.1) | copy-start | bytes 7684
  21.2 4.9 %collective-permute-start.1 = (bf16[208,1024]{1,0:T(8,128)(2,1)S(1)}, bf16[208,1024]{1,0:T(8,128)(2,1)S(1)}, u32[]{:S(2)}, u32[]{:S(2)}) collective-permute-start(bf16[208,1024]{1,0:T(8,128)(2,1)S(1)} %collective-permute-done.edge0.edge), channel_id=1, source_target_pairs={{0,8},{8,0},{16,24},{24,16},{32,40},{40,32},{48,56},{56,48},{64,72... | collective-permute-start | bytes 1277960 | tf_op jit(solution)/shard_map/ppermute | solution.py:332
  27.7 17.6 %collective-permute-start.2 = (bf16[528,128]{1,0:T(8,128)(2,1)S(1)}, bf16[528,128]{1,0:T(8,128)(2,1)S(1)}, u32[]{:S(2)}, u32[]{:S(2)}) collective-permute-start(bf16[528,128]{1,0:T(8,128)(2,1)S(1)} %get-tuple-element.40), channel_id=1, source_target_pairs={{8,24},{16,0},{24,40},{32,16},{40,56},{48,32},{56,72},{64,48},{72,... | collective-permute-start | bytes 405512 | tf_op jit(solution)/shard_map/ppermute | solution.py:338
  30.2 15.2 %collective-permute-start.3 = (bf16[528,128]{1,0:T(8,128)(2,1)S(1)}, bf16[528,128]{1,0:T(8,128)(2,1)S(1)}, u32[]{:S(2)}, u32[]{:S(2)}) collective-permute-start(bf16[528,128]{1,0:T(8,128)(2,1)S(1)} %get-tuple-element.41), channel_id=1, source_target_pairs={{0,16},{16,32},{24,8},{32,48},{40,24},{48,64},{56,40},{64,80},{72,... | collective-permute-start | bytes 405512 | tf_op jit(solution)/shard_map/ppermute | solution.py:338
  33.6 11.8 %collective-permute-start.4 = (bf16[528,128]{1,0:T(8,128)(2,1)S(1)}, bf16[528,128]{1,0:T(8,128)(2,1)S(1)}, u32[]{:S(2)}, u32[]{:S(2)}) collective-permute-start(bf16[528,128]{1,0:T(8,128)(2,1)S(1)} %get-tuple-element.42), channel_id=1, source_target_pairs={{8,16},{16,8},{24,32},{32,24},{40,48},{48,40},{56,64},{64,56},{72,... | collective-permute-start | bytes 405512 | tf_op jit(solution)/shard_map/ppermute | solution.py:338
  35.5 9.9 %collective-permute-start.5 = (bf16[528,128]{1,0:T(8,128)(2,1)S(1)}, bf16[528,128]{1,0:T(8,128)(2,1)S(1)}, u32[]{:S(2)}, u32[]{:S(2)}) collective-permute-start(bf16[528,128]{1,0:T(8,128)(2,1)S(1)} %get-tuple-element.43), channel_id=1, source_target_pairs={{0,8},{8,0},{16,24},{24,16},{32,40},{40,32},{48,56},{56,48},{64,72... | collective-permute-start | bytes 405512 | tf_op jit(solution)/shard_map/ppermute | solution.py:338
  46.4 16.8 %collective-permute-start.8 = (bf16[128,768]{1,0:T(8,128)(2,1)S(1)}, bf16[128,768]{1,0:T(8,128)(2,1)S(1)}, u32[]{:S(2)}, u32[]{:S(2)}) collective-permute-start(bf16[128,768]{1,0:T(8,128)(2,1)S(1)} %get-tuple-element.48), channel_id=1, source_target_pairs={{0,1},{1,2},{2,3},{3,4},{4,5},{5,6},{6,7},{7,0},{8,9},{9,10},{10,1... | collective-permute-start | bytes 589832 | tf_op jit(solution)/shard_map/ppermute | solution.py:317
  48.3 14.8 %collective-permute-start.9 = (bf16[128,768]{1,0:T(8,128)(2,1)S(1)}, bf16[128,768]{1,0:T(8,128)(2,1)S(1)}, u32[]{:S(2)}, u32[]{:S(2)}) collective-permute-start(bf16[128,768]{1,0:T(8,128)(2,1)S(1)} %get-tuple-element.49), channel_id=1, source_target_pairs={{0,2},{1,3},{2,4},{3,5},{4,6},{5,7},{6,0},{7,1},{8,14},{9,15},{10,... | collective-permute-start | bytes 589832 | tf_op jit(solution)/shard_map/ppermute | solution.py:327
  52.1 11.0 %collective-permute-start.10 = (bf16[128,768]{1,0:T(8,128)(2,1)S(1)}, bf16[128,768]{1,0:T(8,128)(2,1)S(1)}, u32[]{:S(2)}, u32[]{:S(2)}) collective-permute-start(bf16[128,768]{1,0:T(8,128)(2,1)S(1)} %get-tuple-element.50), channel_id=1, source_target_pairs={{0,7},{1,0},{2,1},{3,2},{4,3},{5,4},{6,5},{7,6},{8,15},{9,8},{10,9... | collective-permute-start | bytes 589832 | tf_op jit(solution)/shard_map/ppermute | solution.py:317
  56.0 15.8 %collective-permute-start.6 = (bf16[128,768]{1,0:T(8,128)(2,1)S(1)}, bf16[128,768]{1,0:T(8,128)(2,1)S(1)}, u32[]{:S(2)}, u32[]{:S(2)}) collective-permute-start(bf16[128,768]{1,0:T(8,128)(2,1)S(1)} %get-tuple-element.46), channel_id=1, source_target_pairs={{0,1},{1,2},{2,3},{3,4},{4,5},{5,6},{6,7},{7,0},{8,9},{9,10},{10,1... | collective-permute-start | bytes 589832 | tf_op jit(solution)/shard_map/ppermute | solution.py:317
  58.7 13.2 %collective-permute-start.7 = (bf16[128,768]{1,0:T(8,128)(2,1)S(1)}, bf16[128,768]{1,0:T(8,128)(2,1)S(1)}, u32[]{:S(2)}, u32[]{:S(2)}) collective-permute-start(bf16[128,768]{1,0:T(8,128)(2,1)S(1)} %get-tuple-element.47), channel_id=1, source_target_pairs={{0,7},{1,0},{2,1},{3,2},{4,3},{5,4},{6,5},{7,6},{8,15},{9,8},{10,9... | collective-permute-start | bytes 589832 | tf_op jit(solution)/shard_map/ppermute | solution.py:317
  63.8 15.5 %collective-permute-start.11 = (bf16[128,768]{1,0:T(8,128)(2,1)S(1)}, bf16[128,768]{1,0:T(8,128)(2,1)S(1)}, u32[]{:S(2)}, u32[]{:S(2)}) collective-permute-start(bf16[128,768]{1,0:T(8,128)(2,1)S(1)} %get-tuple-element.51), channel_id=1, source_target_pairs={{0,2},{1,3},{2,4},{3,5},{4,6},{5,7},{6,0},{7,1},{8,10},{9,11},{10,... | collective-permute-start | bytes 589832 | tf_op jit(solution)/shard_map/ppermute | solution.py:317
  66.1 13.8 %collective-permute-start.12 = (bf16[128,768]{1,0:T(8,128)(2,1)S(1)}, bf16[128,768]{1,0:T(8,128)(2,1)S(1)}, u32[]{:S(2)}, u32[]{:S(2)}) collective-permute-start(bf16[128,768]{1,0:T(8,128)(2,1)S(1)} %get-tuple-element.52), channel_id=1, source_target_pairs={{0,6},{1,7},{2,0},{3,1},{4,2},{5,3},{6,4},{7,5},{8,14},{9,15},{10,... | collective-permute-start | bytes 589832 | tf_op jit(solution)/shard_map/ppermute | solution.py:317

commit v4 on v3

--- a/solution.py
+++ b/solution.py
@@ -22,9 +22,10 @@
 SLOTS = CAP * len(STEPS)
 BUF = 2 * NS + 16
 RANKS = 8
+OUTWARD = (1, 3, 6)
+INWARD = (7, 4)
+KEPT = (0, 2, 5)
 BF = jnp.bfloat16
-SMEM = pl.BlockSpec(memory_space=pltpu.SMEM)
-VMEM = pl.BlockSpec(memory_space=pltpu.VMEM)
 HBM = pl.BlockSpec(memory_space=pltpu.HBM)
 EDGE_PARTS = 4
 F32 = jnp.float32
@@ -79,11 +80,15 @@
     return jnp.sum(jnp.where(same, weights, 0.0), axis=1, keepdims=True)
 
 
+def parity():
+    return lax.rem(lax.axis_index("box"), 2)
+
+
 def one_hot(rows, index):
     return (iota((rows, index.shape[1]), 0) == index).astype(BF)
 
 
-def edge_kernel(place, rad_all, anterp_all, weights_all, out, rad, anterp, weights, sems):
+def edge_kernel(rad_all, anterp_all, weights_all, out, rad, anterp, weights, sems):
     parts = EDGE_PARTS
     depth = P_SIZE // parts
     copies = [
@@ -97,8 +102,13 @@
         copy.start()
     t_row, j_row = edge_place((EDGE, NS), 0)
     t_col, f_col = local_place((EDGE, NS), 1)
-    first = jnp.where(place[1] == 0, FD - WIDTH, 0)
+    first = jnp.where(parity() == 0, FD - WIDTH, 0)
     pick = jnp.logical_and(t_row == t_col, f_col == j_row + first).astype(BF)
+    for i in range(parts):
+        copies[2 + i].wait()
+        cols = slice(i * depth, (i + 1) * depth)
+        for c in range(2):
+            out[c * EDGE : (c + 1) * EDGE, cols] = dot(pick, rad[c * NS : (c + 1) * NS, cols]).astype(BF)
     t_lane, _ = edge_place((NT, CAP), 1)
     _, j_lane = edge_place((FD, CAP), 1)
     copies[0].wait()
@@ -106,13 +116,8 @@
     spread = exact(weights[...], (iota((NT, CAP), 0) == t_lane).astype(F32))
     coeffs = exact(anterp[...], (iota((FD, CAP), 0) == j_lane + first).astype(F32)) * spread
     high, low = split(jnp.concatenate([coeffs, jnp.zeros((1, CAP), F32)], axis=0))
-    out[2 * EDGE :, :] = jnp.zeros((16, P_SIZE), BF)
     out[2 * EDGE :, 0:CAP] = jnp.concatenate([high.astype(F32), low.astype(F32)], axis=0).astype(BF)
-    for i in range(parts):
-        copies[2 + i].wait()
-        cols = slice(i * depth, (i + 1) * depth)
-        for c in range(2):
-            out[c * EDGE : (c + 1) * EDGE, cols] = dot(pick, rad[c * NS : (c + 1) * NS, cols]).astype(BF)
+    out[2 * EDGE :, CAP:] = jnp.zeros((16, P_SIZE - CAP), BF)
 
 
 def radiate(rad, cur, rows):
@@ -128,7 +133,7 @@
 
 
 def prepare_kernel(
-    place, field, interp, pair_src, pair_op, pair_target, oper,
+    field, interp, pair_src, pair_op, pair_target, oper,
     inter, halo_mat, src_pick, oper_slot, slot_ids, oper_own, own_rows,
 ):
     columns = own_columns(interp[...])
@@ -141,21 +146,22 @@
     shape = (NS, EDGE)
     t_row, g_row = local_place(shape, 0)
     t_col, j_col = edge_place(shape, 1)
+    odd = parity()
     for side in range(2):
-        base = jnp.where(place[1] == side, 0, FD + WIDTH)
+        base = jnp.where(odd == side, 0, FD + WIDTH)
         mats = split(band(columns, j_col - g_row + base, t_row == t_col))
         for part in range(2):
             halo_mat[side, part] = mats[part]
 
     src_row, op_row = pair_src[...].reshape(1, PAIR), pair_op[...].reshape(1, PAIR)
-    ahead = pair_target[...].reshape(1, PAIR) - place[2] * BOX
+    ahead = pair_target[...].reshape(1, PAIR) - lax.axis_index("box") * BOX
     step_of = jnp.full((1, PAIR), -REACH, jnp.int32)
     for k in range(1 - REACH, REACH + 1):
         step_of = step_of + (ahead >= k * BOX).astype(jnp.int32)
     target = ahead - step_of * BOX
     row = iota((8, PAIR), 0)
     own_rows[...] = jnp.where(row == 0, src_row, jnp.where(step_of == 0, target, -1))
-    step_of = step_of * (2 * place[1] - 1)
+    step_of = step_of * (2 * odd - 1)
     digits = jnp.ones((8, PAIR), jnp.int32)
     for k, value in enumerate((src_row, op_row, target)):
         digits = jnp.where(row == 2 * k, value >> 4, digits)
@@ -227,40 +233,42 @@
     own[:, BOX:] = dot(c_im, table, NTR)
 
 
-def own_matrix_kernel(rad, anterp, weights, out):
-    columns = own_columns(anterp[...]) * sample_weights(weights[...])
+def matrix_rows(rad, edge0, edge1, mats, steps, out):
+    me = lax.axis_index("samp")
+    side = 1 - 2 * parity()
+    for c in range(2):
+        blocks = []
+        for j in steps:
+            cols = pl.ds(pl.multiple_of(((me + side * j) & (RANKS - 1)) * CAP, CAP), CAP)
+            mine = rad[c * NS : (c + 1) * NS, cols]
+            rows = slice(c * EDGE, (c + 1) * EDGE)
+            blocks.append(jnp.concatenate([mine, edge0[rows, cols], edge1[rows, cols]], axis=0))
+        both = dot(jnp.concatenate(blocks, axis=1), mats[...], TN)
+        out[:, c * NS : (c + 1) * NS] = (both[:, :NS] + both[:, NS:]).astype(BF)
+
+
+def matrix_kernel(rad, edge0, edge1, anterp, weights, mats, out):
     shape = (NS, NS)
     t_row, f_row = local_place(shape, 0)
     t_col, g_col = local_place(shape, 1)
-    mat_hi, mat_lo = split(band(columns, g_col - f_row + WIDTH, t_row == t_col))
-    for c in range(2):
-        r = rad[c * NS : (c + 1) * NS, :]
-        out[:, c * NS : (c + 1) * NS] = dot(r, mat_hi, TN) + dot(r, mat_lo, TN)
-
-
-def matrix_kernel(place, own, edge0, edge1, out):
+    columns = own_columns(anterp[...]) * sample_weights(weights[...])
+    bands = [band(columns, g_col - f_row + WIDTH, t_row == t_col)]
     shape = (EDGE, NS)
     t_row, j_row = edge_place(shape, 0)
     t_col, g_col = local_place(shape, 1)
-    mats = []
+    odd = parity()
     for side, edge in enumerate((edge0, edge1)):
         tail = edge[2 * EDGE :, 0:CAP].astype(F32)
         cols = (tail[0:8] + tail[8:16]).T[:EDGE]
-        base = jnp.where(place[1] == side, 2 * WIDTH, WIDTH - FD)
-        mats.append(band(cols, g_col - j_row + base, t_row == t_col))
-    high, low = split(jnp.concatenate(mats, axis=0))
-    me = place[0]
-    for c in range(2):
-        rows = slice(c * EDGE, (c + 1) * EDGE)
-        edges = jnp.concatenate([edge0[rows, :], edge1[rows, :]], axis=0)
-        cols = slice(c * NS, (c + 1) * NS)
-        q = (own[:, cols] + dot(edges, high, TN) + dot(edges, low, TN)).astype(BF)
-        for d in range(RANKS):
-            rows = pl.ds(pl.multiple_of(((d - me) & (RANKS - 1)) * CAP, CAP), CAP)
-            out[rows, cols] = q[d * CAP : (d + 1) * CAP]
-
-
-def far_kernel(own, matrix, got0, got1, got2, got3, up3, far4, down3, stack):
+        base = jnp.where(odd == side, 2 * WIDTH, WIDTH - FD)
+        bands.append(band(cols, g_col - j_row + base, t_row == t_col))
+    high, low = split(jnp.concatenate(bands, axis=0))
+    mats[:, :NS] = high
+    mats[:, NS:] = low
+    matrix_rows(rad, edge0, edge1, mats, OUTWARD, out)
+
+
+def far_kernel(own, matrix, got0, got1, got2, got3, out, stack):
     gots = (got0, got1, got2, got3)
     ids = jnp.concatenate([g[2 * NS :, :].astype(F32) for g in gots], axis=1)
     index = (16.0 * ids[0:1] + ids[1:2]).astype(jnp.int32)
@@ -272,28 +280,29 @@
     stack[0:NS, BOX:] = im
     stack[NS:, :BOX] = im
     stack[NS:, BOX:] = -re
-    for j, out in ((3, up3), (4, far4), (5, down3)):
-        out[...] = dot(matrix[j * CAP : (j + 1) * CAP, :], stack[...]).astype(BF)
-
-
-def near_kernel(matrix, stack, up1, down1, keep):
-    for j, out in ((1, up1), (7, down1)):
-        out[...] = dot(matrix[j * CAP : (j + 1) * CAP, :], stack[...]).astype(BF)
-    for i, j in enumerate((0, 2, 6)):
-        keep[i] = dot(matrix[j * CAP : (j + 1) * CAP, :], stack[...])
-
-
-def relay_kernel(place, keep, from_up3, from_far4, from_down3, up2, down2):
-    far = from_far4[...].astype(F32)
-    even = place[1] == 0
-    up2[...] = (keep[1] + from_up3[...].astype(F32) + jnp.where(even, far, 0.0)).astype(BF)
-    down2[...] = (keep[2] + from_down3[...].astype(F32) + jnp.where(even, 0.0, far)).astype(BF)
-
-
-def sum_kernel(keep, up1, down1, up2, down2, out):
-    total = keep[0]
-    for part in (up1, down1, up2, down2):
-        total = total + part[...].astype(F32)
+    out[...] = dot(matrix[...], stack[...]).astype(BF)
+
+
+def near_kernel(rad, edge0, edge1, mats, stack, inward, keep, matrix):
+    matrix_rows(rad, edge0, edge1, mats, INWARD + KEPT, matrix)
+    cut = len(INWARD) * CAP
+    inward[...] = dot(matrix[0:cut, :], stack[...]).astype(BF)
+    keep[...] = dot(matrix[cut:, :], stack[...])
+
+
+def relay_out_kernel(keep, from_inner, out2):
+    out2[...] = (keep[CAP : 2 * CAP, :] + from_inner[CAP : 2 * CAP, :].astype(F32)).astype(BF)
+
+
+def relay_in_kernel(keep, from_inner, from_outer, in3):
+    far = from_inner[2 * CAP :, :].astype(F32) + from_outer[CAP:, :].astype(F32)
+    in3[...] = (keep[2 * CAP :, :] + far).astype(BF)
+
+
+def sum_kernel(keep, from_inner, from_outer, out2, in3, out):
+    total = keep[0:CAP, :]
+    for part in (from_inner[0:CAP, :], from_outer[0:CAP, :], out2[...], in3[...]):
+        total = total + part.astype(F32)
     out[0] = total[:, :BOX].astype(BF)
     out[1] = total[:, BOX:].astype(BF)
 
@@ -312,11 +321,6 @@
     )(*args)
 
 
-def around(value, axis, steps):
-    count = lax.axis_size(axis)
-    return lax.ppermute(value, axis, [(i, (i + steps) % count) for i in range(count)])
-
-
 def outward(value, steps):
     groups, count = lax.axis_size("box"), lax.axis_size("samp")
     pairs = []
@@ -344,21 +348,19 @@
     rad = jnp.transpose(radiation, (0, 2, 3, 1)).reshape(2 * NS, P_SIZE)
     oper = operators.reshape(2 * NS, NOPS)
     weights = weights.reshape(1, NT)
-    group = lax.axis_index("box")
-    place = jnp.stack([lax.axis_index("samp"), group % 2, group]).astype(jnp.int32)
     (edge,) = call(
         edge_kernel,
         [((2 * EDGE + 16, P_SIZE), BF)],
-        place, rad, anterp, weights,
+        rad, anterp, weights,
         scratch=[
             pltpu.VMEM((2 * NS, P_SIZE), BF),
             pltpu.VMEM((2 * WIDTH + 1, FD), F32),
             pltpu.VMEM((1, NT), F32),
             pltpu.SemaphoreType.DMA((EDGE_PARTS + 2,)),
         ],
-        vmem=60,
+        vmem=58,
         name="edge",
-        in_specs=[SMEM] + [HBM] * 3,
+        in_specs=[HBM] * 3,
     )
     edge0 = outward(edge, 1)
 
@@ -369,15 +371,11 @@
             ((NS, 2 * BOX), F32), ((2, 2, NS, EDGE), BF), ((BOX, SLOTS), BF),
             ((2 * NS, SLOTS), BF), ((16, SLOTS), BF), ((2 * NS, PAIR), BF), ((8, PAIR), jnp.int32),
         ],
-        place, field, interp, pair_src, pair_op, pair_target, oper,
+        field, interp, pair_src, pair_op, pair_target, oper,
         flops=10**9,
         name="prepare",
-        in_specs=[SMEM] + [VMEM] * 6,
-    )
-    (own_matrix,) = call(
-        own_matrix_kernel, [((P_SIZE, 2 * NS), F32)], rad, anterp, weights, flops=10**9, name="own_matrix"
-    )
-    edge0, inter, own_matrix = lax.optimization_barrier((edge0, inter, own_matrix))
+    )
+    edge0, inter = lax.optimization_barrier((edge0, inter))
     edge1 = across(edge0)
     (inter,) = call(
         first_edge_kernel, [((NS, 2 * BOX), F32)], inter, halo_mat, edge0, currents,
@@ -398,47 +396,39 @@
         flops=10**9,
         name="own",
     )
-    (matrix,) = call(
+    mats, matrix = call(
         matrix_kernel,
-        [((P_SIZE, 2 * NS), BF)],
-        place, own_matrix, edge0, edge1,
+        [((NS + 2 * EDGE, 2 * NS), BF), ((len(OUTWARD) * CAP, 2 * NS), BF)],
+        rad, edge0, edge1, anterp, weights,
         flops=10**9,
         name="matrix",
-        in_specs=[SMEM] + [VMEM] * 3,
-    )
-    block = (CAP, 2 * BOX)
-    up3, far4, down3, stack = call(
+    )
+    blocks = lambda steps: (steps * CAP, 2 * BOX)
+    leaving, stack = call(
         far_kernel,
-        [(block, BF)] * 3 + [((2 * NS, 2 * BOX), BF)],
+        [(blocks(len(OUTWARD)), BF), ((2 * NS, 2 * BOX), BF)],
         own, matrix, *gots,
         flops=5 * 10**8,
         name="far",
     )
-    from_up3 = around(up3, "samp", 1)
-    from_far4 = outward(far4, 2)
-    from_down3 = around(down3, "samp", -1)
-    up1, down1, keep = call(
+    from_inner = outward(leaving, 1)
+    inward, keep = call(
         near_kernel,
-        [(block, BF)] * 2 + [((3,) + block, F32)],
-        matrix, stack,
-        flops=5 * 10**8,
+        [(blocks(len(INWARD)), BF), (blocks(len(KEPT)), F32)],
+        rad, edge0, edge1, mats, stack,
+        scratch=[pltpu.VMEM(((len(INWARD) + len(KEPT)) * CAP, 2 * NS), BF)],
+        flops=10**9,
         name="near",
     )
-    from_up1 = around(up1, "samp", 1)
-    from_down1 = around(down1, "samp", -1)
-    up2, down2 = call(
-        relay_kernel,
-        [(block, BF)] * 2,
-        place, keep, from_up3, from_far4, from_down3,
-        name="relay",
-        in_specs=[SMEM] + [VMEM] * 4,
-    )
-    from_up2 = around(up2, "samp", 2)
-    from_down2 = around(down2, "samp", -2)
+    from_outer = outward(inward, -1)
+    (out2,) = call(relay_out_kernel, [(blocks(1), BF)], keep, from_inner, name="relay_out")
+    from_inner2 = outward(out2, 2)
+    (in3,) = call(relay_in_kernel, [(blocks(1), BF)], keep, from_inner, from_outer, name="relay_in")
+    from_outer3 = outward(in3, -3)
     (out,) = call(
         sum_kernel,
         [((2, P_SIZE // RANKS, BOX), BF)],
-        keep, from_up1, from_down1, from_up2, from_down2,
+        keep, from_inner, from_outer, from_inner2, from_outer3,
         name="total",
     )
     return out

time: 81.2 us -> 77 us (0.948)
  the two profiles are of different devices: /device:TPU:28 before, /device:TPU:57 now
where the time goes in v4:
time: 77 us; the launch traced here: 76.3 us
  starting transfers between devices  36 us (47%)
  waiting for transfers between devices  22.2 us (29%)
  Pallas kernels  15.2 us (20%)
  local copies, waits for them, and re-layouts  2.67 us (3%)
    ppermute x5, waiting for transfers between devices, outward(): return lax.ppermute(value, ('box', 'samp'), pairs)  21.7 us
    ppermute x5, starting transfers between devices, outward(): return lax.ppermute(value, ('box', 'samp'), pairs)  20.4 us
    pallas_call x12, Pallas kernels, call(): pl.pallas_call(kernel, out_shape=shapes, scratch_shapes=list(scratch), co...  15.2 us
    ppermute x4, starting transfers between devices, sideways(): lax.ppermute(value, 'box', [(b, to) for b, to in pairs if 0 <= to < groups])  12.8 us
    ppermute x1, starting transfers between devices, across(): return lax.ppermute(value, 'box', [(b, b ^ 1) for b in range(groups)])  2.86 us
    unnamed x22, local copies, waits for them, and re-layouts  2.67 us
  transfers between devices with their start and end apart: 10, of which 5 were waited for; matrix products, arithmetic and copies ran while one was open for 0% of the time, Pallas kernels for 12%

profile of v4, /device:TPU:57, one launch (start us, length us, event | category | flops | bytes accessed | tf_op | source)
XLA Modules:
  0.0 76.3 jit_solution(16068964058992167077)
XLA Ops:
  0.0 2.7 %edge.1 = bf16[208,1024]{1,0:T(8,128)(2,1)} custom-call(bf16[512,1024]{1,0:T(8,128)(2,1)} %bitcast.5, f32[7,8]{1,0:T(8,128)} %anterp.1, f32[1,32]{1,0:T(1,128)} %bitcast.9), custom_call_target="tpu_custom_call" | custom-call | flops 100000000 | bytes 1474912 | tf_op jit(solution)/shard_map/edge/pallas_call | solution.py:313
  2.7 10.7 %collective-permute-start = (bf16[208,1024]{1,0:T(8,128)(2,1)}, bf16[208,1024]{1,0:T(8,128)(2,1)S(1)}, u32[]{:S(2)}, u32[]{:S(2)}) collective-permute-start(bf16[208,1024]{1,0:T(8,128)(2,1)} %edge.1), channel_id=1, source_target_pairs={{0,1},{1,2},{2,3},{3,4},{4,5},{5,6},{6,7},{7,0},{8,15},{9,8},{10,9... | collective-permute-start | bytes 1277960 | tf_op jit(solution)/shard_map/ppermute | solution.py:331
  13.4 0.0 copy-start
  13.4 1.4 %copy-done = bf16[2,1024,384]{2,1,0:T(8,128)(2,1)S(1)} copy-done((bf16[2,1024,384]{2,1,0:T(8,128)(2,1)S(1)}, bf16[2,1024,384]{2,1,0:T(8,128)(2,1)}, u32[]{:S(2)}) %copy-start) | copy-done | bytes 1572888
  14.8 1.2 %copy-done.2 = bf16[2,1024,32,8]{1,3,2,0:T(8,128)(2,1)S(1)} copy-done((bf16[2,1024,32,8]{1,3,2,0:T(8,128)(2,1)S(1)}, bf16[2,1024,32,8]{1,3,2,0:T(8,128)(2,1)}, u32[]{:S(2)}) %copy-start.2) | copy-done | bytes 1048600
  16.0 1.2 %field.1 = f32[256,768]{1,0:T(8,128)S(1)} custom-call(bf16[512,1024]{1,0:T(8,128)(2,1)S(1)} %bitcast.6, bf16[2,1024,384]{2,1,0:T(8,128)(2,1)S(1)} %copy-done), custom_call_target="tpu_custom_call" | custom-call | flops 1000000000 | bytes 3407872 | tf_op jit(solution)/shard_map/field/pallas_call | solution.py:313
  17.3 0.0 copy-start.1
  17.4 2.3 %prepare.1 = (f32[256,768]{1,0:T(8,128)S(1)}, bf16[2,2,256,96]{3,2,1,0:T(8,128)(2,1)S(1)}, bf16[384,512]{1,0:T(8,128)(2,1)S(1)}, bf16[512,512]{1,0:T(8,128)(2,1)...) custom-call(f32[256,768]{1,0:T(8,128)S(1)} %field.1, f32[7,8]{1,0:T(8,128)S(1)} %copy-done.7, ...), custom_call_target="tpu_custom_call" | custom-call | flops 1000000000 | bytes 3710688 | tf_op jit(solution)/shard_map/prepare/pallas_call | solution.py:313
  19.7 2.9 %collective-permute-start.1 = (bf16[208,1024]{1,0:T(8,128)(2,1)S(1)}, bf16[208,1024]{1,0:T(8,128)(2,1)S(1)}, u32[]{:S(2)}, u32[]{:S(2)}) collective-permute-start(bf16[208,1024]{1,0:T(8,128)(2,1)S(1)} %collective-permute-done.edge0.edge), channel_id=1, source_target_pairs={{0,8},{8,0},{16,24},{24,16},{32,40},{40,32},{48,56},{56,48},{64,72... | collective-permute-start | bytes 1277960 | tf_op jit(solution)/shard_map/ppermute | solution.py:336
  22.5 0.9 %first_edge.1.inter = f32[256,768]{1,0:T(8,128)S(1)} custom-call(f32[256,768]{1,0:T(8,128)S(1)} %get-tuple-element.28.inter, bf16[2,2,256,96]{3,2,1,0:T(8,128)(2,1)S(1)} %get-tuple-element.29.halo_mat, bf16[208,1024]{1,0:T(8,128)(2,1)S(1)} %collective-permute-done.edge0.edge, bf16[2,1024,384]{2,1,0:T(8,128)(2,1)S(1)} %copy-done.1), custom_call_target="tpu_custom_call" | custom-call | flops 400000000 | bytes 3768320 | tf_op jit(solution)/shard_map/first_edge/pallas_call | solution.py:313
  23.5 0.5 collective-permute-done.1.edge1.edge
  23.9 1.6 %send.1 = (bf16[528,128]{1,0:T(8,128)(2,1)S(1)}, bf16[528,128]{1,0:T(8,128)(2,1)S(1)}, bf16[528,128]{1,0:T(8,128)(2,1)S(1)}, bf16[528,128]{1,0:T(8,128)(2,1)S(1)}, bf16[2,256,768]{2,1,0:T(8,128)(2,1)S(1)}) custom-call(f32[256,768]{1,0:T(8,128)S(1)} %first_edge.1.inter, bf16[2,2,256,96]{3,2,1,0:T(8,128)(2,1)S(1)} %get-tuple-element.29.halo_mat, ...), custom_call_target="tpu_custom_call" | custom-call | flops 400000000 | bytes 5242880 | tf_op jit(solution)/shard_map/send/pallas_call | solution.py:313
  25.6 3.1 %collective-permute-start.2 = (bf16[528,128]{1,0:T(8,128)(2,1)S(1)}, bf16[528,128]{1,0:T(8,128)(2,1)S(1)}, u32[]{:S(2)}, u32[]{:S(2)}) collective-permute-start(bf16[528,128]{1,0:T(8,128)(2,1)S(1)} %get-tuple-element.37), channel_id=1, source_target_pairs={{8,24},{16,0},{24,40},{32,16},{40,56},{48,32},{56,72},{64,48},{72,... | collective-permute-start | bytes 405512 | tf_op jit(solution)/shard_map/ppermute | solution.py:342
  28.7 4.3 %collective-permute-start.3 = (bf16[528,128]{1,0:T(8,128)(2,1)S(1)}, bf16[528,128]{1,0:T(8,128)(2,1)S(1)}, u32[]{:S(2)}, u32[]{:S(2)}) collective-permute-start(bf16[528,128]{1,0:T(8,128)(2,1)S(1)} %get-tuple-element.38), channel_id=1, source_target_pairs={{0,16},{16,32},{24,8},{32,48},{40,24},{48,64},{56,40},{64,80},{72,... | collective-permute-start | bytes 405512 | tf_op jit(solution)/shard_map/ppermute | solution.py:342
  33.0 1.9 %collective-permute-start.4 = (bf16[528,128]{1,0:T(8,128)(2,1)S(1)}, bf16[528,128]{1,0:T(8,128)(2,1)S(1)}, u32[]{:S(2)}, u32[]{:S(2)}) collective-permute-start(bf16[528,128]{1,0:T(8,128)(2,1)S(1)} %get-tuple-element.39), channel_id=1, source_target_pairs={{8,16},{16,8},{24,32},{32,24},{40,48},{48,40},{56,64},{64,56},{72,... | collective-permute-start | bytes 405512 | tf_op jit(solution)/shard_map/ppermute | solution.py:342
  34.9 3.4 %collective-permute-start.5 = (bf16[528,128]{1,0:T(8,128)(2,1)S(1)}, bf16[528,128]{1,0:T(8,128)(2,1)S(1)}, u32[]{:S(2)}, u32[]{:S(2)}) collective-permute-start(bf16[528,128]{1,0:T(8,128)(2,1)S(1)} %get-tuple-element.40), channel_id=1, source_target_pairs={{0,8},{8,0},{16,24},{24,16},{32,40},{40,32},{48,56},{56,48},{64,72... | collective-permute-start | bytes 405512 | tf_op jit(solution)/shard_map/ppermute | solution.py:342
  38.3 0.0 copy-start.3
  38.4 0.0 copy-start.4
  38.4 1.6 %own.1 = f32[256,768]{1,0:T(8,128)S(1)} custom-call(bf16[2,256,768]{2,1,0:T(8,128)(2,1)S(1)} %get-tuple-element.33.parts, s32[8,640]{1,0:T(8,128)S(1)} %get-tuple-element.34.own_rows, bf16[512,640]{1,0:T(8,128)(2,1)S(1)} %get-tuple-element.35.oper_own), custom_call_target="tpu_custom_call" | custom-call | flops 1000000000 | bytes 2248704 | tf_op jit(solution)/shard_map/own/pallas_call | solution.py:313
  40.0 1.5 %matrix.1 = (bf16[448,512]{1,0:T(8,128)(2,1)S(1)}, bf16[384,512]{1,0:T(8,128)(2,1)S(1)}) custom-call(bf16[512,1024]{1,0:T(8,128)(2,1)S(1)} %bitcast.7, bf16[208,1024]{1,0:T(8,128)(2,1)S(1)} %collective-permute-done.edge0.edge, bf16[208,1024]{1,0:T(8,128)(2,1)S(1)} %collective-permute-done.1.edge1.edge, f32[7,8]{1,0:T(8,128)S(1)} %copy-done.4, ...), custom_call_target="tpu_custom_call" | custom-call | flops 1000000000 | bytes 2752864 | tf_op jit(solution)/shard_map/matrix/pallas_call | solution.py:313
  41.6 0.9 %far.1 = (bf16[384,768]{1,0:T(8,128)(2,1)S(1)}, bf16[512,768]{1,0:T(8,128)(2,1)S(1)}) custom-call(f32[256,768]{1,0:T(8,128)S(1)} %own.1, bf16[384,512]{1,0:T(8,128)(2,1)S(1)} %get-tuple-element.36.matrix, bf16[528,128]{1,0:T(8,128)(2,1)S(1)} %collective-permute-done.2.got0, bf16[528,128]{1,0:T(8,128)(2,1)S(1)} %collective-permute-done.3.got1, ...), custom_call_target="tpu_custom_call" | custom-call | flops 500000000 | bytes 3096576 | tf_op jit(solution)/shard_map/far/pallas_call | solution.py:313
  42.5 3.6 %collective-permute-start.6 = (bf16[384,768]{1,0:T(8,128)(2,1)S(1)}, bf16[384,768]{1,0:T(8,128)(2,1)S(1)}, u32[]{:S(2)}, u32[]{:S(2)}) collective-permute-start(bf16[384,768]{1,0:T(8,128)(2,1)S(1)} %get-tuple-element.43), channel_id=1, source_target_pairs={{0,1},{1,2},{2,3},{3,4},{4,5},{5,6},{6,7},{7,0},{8,15},{9,8},{10,9... | collective-permute-start | bytes 1769480 | tf_op jit(solution)/shard_map/ppermute | solution.py:331
  46.1 1.5 %near.1 = (bf16[256,768]{1,0:T(8,128)(2,1)S(1)}, f32[384,768]{1,0:T(8,128)S(1)}) custom-call(bf16[512,1024]{1,0:T(8,128)(2,1)S(1)} %bitcast.8, bf16[208,1024]{1,0:T(8,128)(2,1)S(1)} %collective-permute-done.edge0.edge, bf16[208,1024]{1,0:T(8,128)(2,1)S(1)} %collective-permute-done.1.edge1.edge, bf16[448,512]{1,0:T(8,128)(2,1)S(1)} %get-tuple-element.27.mats, ...), custom_call_target="tpu_custom_call" | custom-call | flops 1000000000 | bytes 4718592 | tf_op jit(solution)/shard_map/near/pallas_call | solution.py:313
  47.6 1.9 %collective-permute-start.7 = (bf16[256,768]{1,0:T(8,128)(2,1)S(1)}, bf16[256,768]{1,0:T(8,128)(2,1)S(1)}, u32[]{:S(2)}, u32[]{:S(2)}) collective-permute-start(bf16[256,768]{1,0:T(8,128)(2,1)S(1)} %get-tuple-element.44), channel_id=1, source_target_pairs={{0,7},{1,0},{2,1},{3,2},{4,3},{5,4},{6,5},{7,6},{8,9},{9,10},{10,1... | collective-permute-start | bytes 1179656 | tf_op jit(solution)/shard_map/ppermute | solution.py:331
  49.5 5.9 %collective-permute-done.6.from_inner = bf16[384,768]{1,0:T(8,128)(2,1)S(1)} collective-permute-done((bf16[384,768]{1,0:T(8,128)(2,1)S(1)}, bf16[384,768]{1,0:T(8,128)(2,1)S(1)}, u32[]{:S(2)}, u32[]{:S(2)}) %collective-permute-start.6) | collective-permute-done | bytes 589856 | tf_op jit(solution)/shard_map/ppermute | solution.py:331
  55.5 2.2 %collective-permute-start.8 = (bf16[128,768]{1,0:T(8,128)(2,1)S(1)}, bf16[128,768]{1,0:T(8,128)(2,1)S(1)}, u32[]{:S(2)}, u32[]{:S(2)}) collective-permute-start(bf16[128,768]{1,0:T(8,128)(2,1)S(1)} %relay_out.1), channel_id=1, source_target_pairs={{0,2},{1,3},{2,4},{3,5},{4,6},{5,7},{6,0},{7,1},{8,14},{9,15},{10,... | collective-permute-start | bytes 589832 | tf_op jit(solution)/shard_map/ppermute | solution.py:331
  57.7 1.6 %collective-permute-done.7.from_outer = bf16[256,768]{1,0:T(8,128)(2,1)S(1)} collective-permute-done((bf16[256,768]{1,0:T(8,128)(2,1)S(1)}, bf16[256,768]{1,0:T(8,128)(2,1)S(1)}, u32[]{:S(2)}, u32[]{:S(2)}) %collective-permute-start.7) | collective-permute-done | bytes 393248 | tf_op jit(solution)/shard_map/ppermute | solution.py:331
  59.3 0.1 relay_in.1
  59.3 2.0 %collective-permute-start.9 = (bf16[128,768]{1,0:T(8,128)(2,1)S(1)}, bf16[128,768]{1,0:T(8,128)(2,1)S(1)}, u32[]{:S(2)}, u32[]{:S(2)}) collective-permute-start(bf16[128,768]{1,0:T(8,128)(2,1)S(1)} %relay_in.1), channel_id=1, source_target_pairs={{0,5},{1,6},{2,7},{3,0},{4,1},{5,2},{6,3},{7,4},{8,11},{9,12},{10,... | collective-permute-start | bytes 589832 | tf_op jit(solution)/shard_map/ppermute | solution.py:331
  61.3 2.7 %collective-permute-done.8.out2 = bf16[128,768]{1,0:T(8,128)(2,1)S(1)} collective-permute-done((bf16[128,768]{1,0:T(8,128)(2,1)S(1)}, bf16[128,768]{1,0:T(8,128)(2,1)S(1)}, u32[]{:S(2)}, u32[]{:S(2)}) %collective-permute-start.8) | collective-permute-done | bytes 196640 | tf_op jit(solution)/shard_map/ppermute | solution.py:331
  64.0 11.6 %collective-permute-done.9.in3 = bf16[128,768]{1,0:T(8,128)(2,1)S(1)} collective-permute-done((bf16[128,768]{1,0:T(8,128)(2,1)S(1)}, bf16[128,768]{1,0:T(8,128)(2,1)S(1)}, u32[]{:S(2)}, u32[]{:S(2)}) %collective-permute-start.9) | collective-permute-done | bytes 196640 | tf_op jit(solution)/shard_map/ppermute | solution.py:331
  75.6 0.8 %total.1 = bf16[2,128,384]{2,1,0:T(8,128)(2,1)} custom-call(f32[384,768]{1,0:T(8,128)S(1)} %get-tuple-element.42.keep, bf16[384,768]{1,0:T(8,128)(2,1)S(1)} %collective-permute-done.6.from_inner, bf16[256,768]{1,0:T(8,128)(2,1)S(1)} %collective-permute-done.7.from_outer, bf16[128,768]{1,0:T(8,128)(2,1)S(1)} %collective-permute-done.8.out2, ...), custom_call_target="tpu_custom_call" | custom-call | flops 100000000 | bytes 2752512 | tf_op jit(solution)/shard_map/total/pallas_call | solution.py:313
  (22 shorter events, 0.1 us)
Async XLA Ops:
  2.7 17.0 %collective-permute-start = (bf16[208,1024]{1,0:T(8,128)(2,1)}, bf16[208,1024]{1,0:T(8,128)(2,1)S(1)}, u32[]{:S(2)}, u32[]{:S(2)}) collective-permute-start(bf16[208,1024]{1,0:T(8,128)(2,1)} %edge.1), channel_id=1, source_target_pairs={{0,1},{1,2},{2,3},{3,4},{4,5},{5,6},{6,7},{7,0},{8,15},{9,8},{10,9... | collective-permute-start | bytes 1277960 | tf_op jit(solution)/shard_map/ppermute | solution.py:331
  13.4 1.4 %copy-start = (bf16[2,1024,384]{2,1,0:T(8,128)(2,1)S(1)}, bf16[2,1024,384]{2,1,0:T(8,128)(2,1)}, u32[]{:S(2)}) copy-start(bf16[2,1024,384]{2,1,0:T(8,128)(2,1)} %cur.5) | copy-start | bytes 4718596
  14.8 1.2 %copy-start.2 = (bf16[2,1024,32,8]{1,3,2,0:T(8,128)(2,1)S(1)}, bf16[2,1024,32,8]{1,3,2,0:T(8,128)(2,1)}, u32[]{:S(2)}) copy-start(bf16[2,1024,32,8]{1,3,2,0:T(8,128)(2,1)} %param.10) | copy-start | bytes 3145732
  16.0 1.3 %copy-start.6 = (bf16[2,32,8,316]{3,2,1,0:T(8,128)(2,1)S(1)}, bf16[2,32,8,316]{3,2,1,0:T(8,128)(2,1)}, u32[]{:S(2)}) copy-start(bf16[2,32,8,316]{3,2,1,0:T(8,128)(2,1)} %param.14) | copy-start | bytes 970756
  16.0 1.3 %copy-start.7 = (f32[7,8]{1,0:T(8,128)S(1)}, f32[7,8]{1,0:T(8,128)}, u32[]{:S(2)}) copy-start(f32[7,8]{1,0:T(8,128)} %interp.1) | copy-start | bytes 676
  16.0 1.3 %copy-start.8 = (s32[640]{0:T(1024)S(1)}, s32[640]{0:T(1024)}, u32[]{:S(2)}) copy-start(s32[640]{0:T(1024)} %pair_src.1) | copy-start | bytes 7684
  16.0 1.3 %copy-start.9 = (s32[640]{0:T(1024)S(1)}, s32[640]{0:T(1024)}, u32[]{:S(2)}) copy-start(s32[640]{0:T(1024)} %pair_op.1) | copy-start | bytes 7684
  16.0 1.3 %copy-start.10 = (s32[640]{0:T(1024)S(1)}, s32[640]{0:T(1024)}, u32[]{:S(2)}) copy-start(s32[640]{0:T(1024)} %pair_target.1) | copy-start | bytes 7684
  17.3 5.2 %copy-start.1 = (bf16[2,1024,384]{2,1,0:T(8,128)(2,1)S(1)}, bf16[2,1024,384]{2,1,0:T(8,128)(2,1)}, u32[]{:S(2)}) copy-start(bf16[2,1024,384]{2,1,0:T(8,128)(2,1)} %cur.5) | copy-start | bytes 4718596
  19.7 4.2 %collective-permute-start.1 = (bf16[208,1024]{1,0:T(8,128)(2,1)S(1)}, bf16[208,1024]{1,0:T(8,128)(2,1)S(1)}, u32[]{:S(2)}, u32[]{:S(2)}) collective-permute-start(bf16[208,1024]{1,0:T(8,128)(2,1)S(1)} %collective-permute-done.edge0.edge), channel_id=1, source_target_pairs={{0,8},{8,0},{16,24},{24,16},{32,40},{40,32},{48,56},{56,48},{64,72... | collective-permute-start | bytes 1277960 | tf_op jit(solution)/shard_map/ppermute | solution.py:336
  25.6 16.0 %collective-permute-start.2 = (bf16[528,128]{1,0:T(8,128)(2,1)S(1)}, bf16[528,128]{1,0:T(8,128)(2,1)S(1)}, u32[]{:S(2)}, u32[]{:S(2)}) collective-permute-start(bf16[528,128]{1,0:T(8,128)(2,1)S(1)} %get-tuple-element.37), channel_id=1, source_target_pairs={{8,24},{16,0},{24,40},{32,16},{40,56},{48,32},{56,72},{64,48},{72,... | collective-permute-start | bytes 405512 | tf_op jit(solution)/shard_map/ppermute | solution.py:342
  28.7 12.9 %collective-permute-start.3 = (bf16[528,128]{1,0:T(8,128)(2,1)S(1)}, bf16[528,128]{1,0:T(8,128)(2,1)S(1)}, u32[]{:S(2)}, u32[]{:S(2)}) collective-permute-start(bf16[528,128]{1,0:T(8,128)(2,1)S(1)} %get-tuple-element.38), channel_id=1, source_target_pairs={{0,16},{16,32},{24,8},{32,48},{40,24},{48,64},{56,40},{64,80},{72,... | collective-permute-start | bytes 405512 | tf_op jit(solution)/shard_map/ppermute | solution.py:342
  33.0 8.6 %collective-permute-start.4 = (bf16[528,128]{1,0:T(8,128)(2,1)S(1)}, bf16[528,128]{1,0:T(8,128)(2,1)S(1)}, u32[]{:S(2)}, u32[]{:S(2)}) collective-permute-start(bf16[528,128]{1,0:T(8,128)(2,1)S(1)} %get-tuple-element.39), channel_id=1, source_target_pairs={{8,16},{16,8},{24,32},{32,24},{40,48},{48,40},{56,64},{64,56},{72,... | collective-permute-start | bytes 405512 | tf_op jit(solution)/shard_map/ppermute | solution.py:342
  34.9 6.7 %collective-permute-start.5 = (bf16[528,128]{1,0:T(8,128)(2,1)S(1)}, bf16[528,128]{1,0:T(8,128)(2,1)S(1)}, u32[]{:S(2)}, u32[]{:S(2)}) collective-permute-start(bf16[528,128]{1,0:T(8,128)(2,1)S(1)} %get-tuple-element.40), channel_id=1, source_target_pairs={{0,8},{8,0},{16,24},{24,16},{32,40},{40,32},{48,56},{56,48},{64,72... | collective-permute-start | bytes 405512 | tf_op jit(solution)/shard_map/ppermute | solution.py:342
  38.3 1.6 %copy-start.3 = (bf16[2,1024,32,8]{1,3,2,0:T(8,128)(2,1)S(1)}, bf16[2,1024,32,8]{1,3,2,0:T(8,128)(2,1)}, u32[]{:S(2)}) copy-start(bf16[2,1024,32,8]{1,3,2,0:T(8,128)(2,1)} %param.10) | copy-start | bytes 3145732
  38.4 1.6 %copy-start.4 = (f32[7,8]{1,0:T(8,128)S(1)}, f32[7,8]{1,0:T(8,128)}, u32[]{:S(2)}) copy-start(f32[7,8]{1,0:T(8,128)} %anterp.1) | copy-start | bytes 676
  38.4 1.6 %copy-start.5 = (f32[32]{0:T(128)S(1)}, f32[32]{0:T(128)}, u32[]{:S(2)}) copy-start(f32[32]{0:T(128)} %param.13) | copy-start | bytes 388
  42.5 13.0 %collective-permute-start.6 = (bf16[384,768]{1,0:T(8,128)(2,1)S(1)}, bf16[384,768]{1,0:T(8,128)(2,1)S(1)}, u32[]{:S(2)}, u32[]{:S(2)}) collective-permute-start(bf16[384,768]{1,0:T(8,128)(2,1)S(1)} %get-tuple-element.43), channel_id=1, source_target_pairs={{0,1},{1,2},{2,3},{3,4},{4,5},{5,6},{6,7},{7,0},{8,15},{9,8},{10,9... | collective-permute-start | bytes 1769480 | tf_op jit(solution)/shard_map/ppermute | solution.py:331
  47.6 11.7 %collective-permute-start.7 = (bf16[256,768]{1,0:T(8,128)(2,1)S(1)}, bf16[256,768]{1,0:T(8,128)(2,1)S(1)}, u32[]{:S(2)}, u32[]{:S(2)}) collective-permute-start(bf16[256,768]{1,0:T(8,128)(2,1)S(1)} %get-tuple-element.44), channel_id=1, source_target_pairs={{0,7},{1,0},{2,1},{3,2},{4,3},{5,4},{6,5},{7,6},{8,9},{9,10},{10,1... | collective-permute-start | bytes 1179656 | tf_op jit(solution)/shard_map/ppermute | solution.py:331
  55.5 8.5 %collective-permute-start.8 = (bf16[128,768]{1,0:T(8,128)(2,1)S(1)}, bf16[128,768]{1,0:T(8,128)(2,1)S(1)}, u32[]{:S(2)}, u32[]{:S(2)}) collective-permute-start(bf16[128,768]{1,0:T(8,128)(2,1)S(1)} %relay_out.1), channel_id=1, source_target_pairs={{0,2},{1,3},{2,4},{3,5},{4,6},{5,7},{6,0},{7,1},{8,14},{9,15},{10,... | collective-permute-start | bytes 589832 | tf_op jit(solution)/shard_map/ppermute | solution.py:331
  59.3 16.2 %collective-permute-start.9 = (bf16[128,768]{1,0:T(8,128)(2,1)S(1)}, bf16[128,768]{1,0:T(8,128)(2,1)S(1)}, u32[]{:S(2)}, u32[]{:S(2)}) collective-permute-start(bf16[128,768]{1,0:T(8,128)(2,1)S(1)} %relay_in.1), channel_id=1, source_target_pairs={{0,5},{1,6},{2,7},{3,0},{4,1},{5,2},{6,3},{7,4},{8,11},{9,12},{10,... | collective-permute-start | bytes 589832 | tf_op jit(solution)/shard_map/ppermute | solution.py:331

commit v5 on v4

--- a/solution.py
+++ b/solution.py
@@ -22,6 +22,7 @@
 SLOTS = CAP * len(STEPS)
 BUF = 2 * NS + 16
 RANKS = 8
+TAIL = RANKS * 2 * EDGE
 OUTWARD = (1, 3, 6)
 INWARD = (7, 4)
 KEPT = (0, 2, 5)
@@ -108,7 +109,10 @@
         copies[2 + i].wait()
         cols = slice(i * depth, (i + 1) * depth)
         for c in range(2):
-            out[c * EDGE : (c + 1) * EDGE, cols] = dot(pick, rad[c * NS : (c + 1) * NS, cols]).astype(BF)
+            picked = dot(pick, rad[c * NS : (c + 1) * NS, cols]).astype(BF)
+            for k in range(depth // CAP):
+                row = (i * (depth // CAP) + k) * 2 * EDGE + c * EDGE
+                out[row : row + EDGE, :] = picked[:, k * CAP : (k + 1) * CAP]
     t_lane, _ = edge_place((NT, CAP), 1)
     _, j_lane = edge_place((FD, CAP), 1)
     copies[0].wait()
@@ -116,8 +120,7 @@
     spread = exact(weights[...], (iota((NT, CAP), 0) == t_lane).astype(F32))
     coeffs = exact(anterp[...], (iota((FD, CAP), 0) == j_lane + first).astype(F32)) * spread
     high, low = split(jnp.concatenate([coeffs, jnp.zeros((1, CAP), F32)], axis=0))
-    out[2 * EDGE :, 0:CAP] = jnp.concatenate([high.astype(F32), low.astype(F32)], axis=0).astype(BF)
-    out[2 * EDGE :, CAP:] = jnp.zeros((16, P_SIZE - CAP), BF)
+    out[TAIL:, :] = jnp.concatenate([high.astype(F32), low.astype(F32)], axis=0).astype(BF)
 
 
 def radiate(rad, cur, rows):
@@ -133,8 +136,8 @@
 
 
 def prepare_kernel(
-    field, interp, pair_src, pair_op, pair_target, oper,
-    inter, halo_mat, src_pick, oper_slot, slot_ids, oper_own, own_rows,
+    field, interp, anterp, weights, pair_src, pair_op, pair_target, oper,
+    inter, halo_mat, src_pick, oper_slot, slot_ids, oper_own, own_rows, own_mat,
 ):
     columns = own_columns(interp[...])
     shape = (NS, NS)
@@ -152,6 +155,12 @@
         mats = split(band(columns, j_col - g_row + base, t_row == t_col))
         for part in range(2):
             halo_mat[side, part] = mats[part]
+
+    shape = (NS, NS)
+    t_row, f_row = local_place(shape, 0)
+    t_col, g_col = local_place(shape, 1)
+    columns = own_columns(anterp[...]) * sample_weights(weights[...])
+    own_mat[:, :NS], own_mat[:, NS:] = split(band(columns, g_col - f_row + WIDTH, t_row == t_col))
 
     src_row, op_row = pair_src[...].reshape(1, PAIR), pair_op[...].reshape(1, PAIR)
     ahead = pair_target[...].reshape(1, PAIR) - lax.axis_index("box") * BOX
@@ -192,7 +201,8 @@
 
 
 def with_edge(inter, mats, edge, cur):
-    re, im = radiate(edge[: 2 * EDGE, :], cur, EDGE)
+    rows = jnp.concatenate([edge[i * 2 * EDGE : (i + 1) * 2 * EDGE, :] for i in range(RANKS)], axis=1)
+    re, im = radiate(rows, cur, EDGE)
     halo = jnp.concatenate([re, im], axis=1).astype(BF)
     return inter[...] + dot(mats[0], halo) + dot(mats[1], halo)
 
@@ -206,14 +216,12 @@
     return (o_re * re - o_im * im).astype(BF), (o_re * im + o_im * re).astype(BF)
 
 
-def send_kernel(inter, halo_mat, edge, cur, src_pick, oper_slot, slot_ids, out0, out1, out2, out3, parts):
+def send_kernel(inter, halo_mat, edge, cur, src_pick, oper_slot, slot_ids, out0, out1, out2, out3, rounded):
     whole = with_edge(inter, (halo_mat[1, 0], halo_mat[1, 1]), edge, cur)
-    hi, lo = split(whole)
-    parts[0] = hi
-    parts[1] = lo
+    whole = whole.astype(BF)
+    rounded[...] = whole
     pick = src_pick[...]
-    re = dot(hi[:, :BOX], pick) + dot(lo[:, :BOX], pick)
-    im = dot(hi[:, BOX:], pick) + dot(lo[:, BOX:], pick)
+    re, im = dot(whole[:, :BOX], pick), dot(whole[:, BOX:], pick)
     c_re, c_im = multiply(oper_slot[...], re, im)
     for k, out in enumerate((out0, out1, out2, out3)):
         cols = slice(k * CAP, (k + 1) * CAP)
@@ -222,50 +230,43 @@
         out[2 * NS :, :] = slot_ids[:, cols]
 
 
-def own_kernel(parts, own_rows, oper_own, own):
+def own_kernel(rounded, own_rows, oper_own, own):
     pick = one_hot(BOX, own_rows[0:1, :])
-    hi, lo = parts[0], parts[1]
-    re = dot(hi[:, :BOX], pick) + dot(lo[:, :BOX], pick)
-    im = dot(hi[:, BOX:], pick) + dot(lo[:, BOX:], pick)
+    re, im = dot(rounded[:, :BOX], pick), dot(rounded[:, BOX:], pick)
     c_re, c_im = multiply(oper_own[...], re, im)
     table = one_hot(BOX, own_rows[1:2, :])
     own[:, :BOX] = dot(c_re, table, NTR)
     own[:, BOX:] = dot(c_im, table, NTR)
 
 
-def matrix_rows(rad, edge0, edge1, mats, steps, out):
+def matrix_rows(rad, edge0, edge1, own_mat, edge_mat, steps, out):
     me = lax.axis_index("samp")
     side = 1 - 2 * parity()
     for c in range(2):
-        blocks = []
+        mine, beside = [], []
         for j in steps:
-            cols = pl.ds(pl.multiple_of(((me + side * j) & (RANKS - 1)) * CAP, CAP), CAP)
-            mine = rad[c * NS : (c + 1) * NS, cols]
-            rows = slice(c * EDGE, (c + 1) * EDGE)
-            blocks.append(jnp.concatenate([mine, edge0[rows, cols], edge1[rows, cols]], axis=0))
-        both = dot(jnp.concatenate(blocks, axis=1), mats[...], TN)
+            block = (me + side * j) & (RANKS - 1)
+            mine.append(rad[c * NS : (c + 1) * NS, pl.ds(pl.multiple_of(block * CAP, CAP), CAP)])
+            rows = pl.ds(pl.multiple_of(block * 2 * EDGE + c * EDGE, 32), EDGE)
+            beside.append(jnp.concatenate([edge0[rows, :], edge1[rows, :]], axis=0))
+        both = dot(jnp.concatenate(mine, axis=1), own_mat[...], TN)
+        both = both + dot(jnp.concatenate(beside, axis=1), edge_mat[...], TN)
         out[:, c * NS : (c + 1) * NS] = (both[:, :NS] + both[:, NS:]).astype(BF)
 
 
-def matrix_kernel(rad, edge0, edge1, anterp, weights, mats, out):
-    shape = (NS, NS)
-    t_row, f_row = local_place(shape, 0)
-    t_col, g_col = local_place(shape, 1)
-    columns = own_columns(anterp[...]) * sample_weights(weights[...])
-    bands = [band(columns, g_col - f_row + WIDTH, t_row == t_col)]
+def matrix_kernel(rad, edge0, edge1, own_mat, edge_mat, out):
     shape = (EDGE, NS)
     t_row, j_row = edge_place(shape, 0)
     t_col, g_col = local_place(shape, 1)
     odd = parity()
+    bands = []
     for side, edge in enumerate((edge0, edge1)):
-        tail = edge[2 * EDGE :, 0:CAP].astype(F32)
+        tail = edge[TAIL:, :].astype(F32)
         cols = (tail[0:8] + tail[8:16]).T[:EDGE]
         base = jnp.where(odd == side, 2 * WIDTH, WIDTH - FD)
         bands.append(band(cols, g_col - j_row + base, t_row == t_col))
-    high, low = split(jnp.concatenate(bands, axis=0))
-    mats[:, :NS] = high
-    mats[:, NS:] = low
-    matrix_rows(rad, edge0, edge1, mats, OUTWARD, out)
+    edge_mat[:, :NS], edge_mat[:, NS:] = split(jnp.concatenate(bands, axis=0))
+    matrix_rows(rad, edge0, edge1, own_mat, edge_mat, OUTWARD, out)
 
 
 def far_kernel(own, matrix, got0, got1, got2, got3, out, stack):
@@ -283,8 +284,8 @@
     out[...] = dot(matrix[...], stack[...]).astype(BF)
 
 
-def near_kernel(rad, edge0, edge1, mats, stack, inward, keep, matrix):
-    matrix_rows(rad, edge0, edge1, mats, INWARD + KEPT, matrix)
+def near_kernel(rad, edge0, edge1, own_mat, edge_mat, stack, inward, keep, matrix):
+    matrix_rows(rad, edge0, edge1, own_mat, edge_mat, INWARD + KEPT, matrix)
     cut = len(INWARD) * CAP
     inward[...] = dot(matrix[0:cut, :], stack[...]).astype(BF)
     keep[...] = dot(matrix[cut:, :], stack[...])
@@ -350,40 +351,40 @@
     weights = weights.reshape(1, NT)
     (edge,) = call(
         edge_kernel,
-        [((2 * EDGE + 16, P_SIZE), BF)],
-        rad, anterp, weights,
+        [((TAIL + 16, CAP), BF)],
+        *(pltpu.with_memory_space_constraint(a, pltpu.HBM) for a in (rad, anterp, weights)),
         scratch=[
             pltpu.VMEM((2 * NS, P_SIZE), BF),
             pltpu.VMEM((2 * WIDTH + 1, FD), F32),
             pltpu.VMEM((1, NT), F32),
             pltpu.SemaphoreType.DMA((EDGE_PARTS + 2,)),
         ],
-        vmem=58,
         name="edge",
         in_specs=[HBM] * 3,
     )
     edge0 = outward(edge, 1)
 
     (field,) = call(field_kernel, [((NS, 2 * BOX), F32)], rad, currents, flops=10**9, name="field")
-    inter, halo_mat, src_pick, oper_slot, slot_ids, oper_own, own_rows = call(
+    inter, halo_mat, src_pick, oper_slot, slot_ids, oper_own, own_rows, own_mat = call(
         prepare_kernel,
         [
             ((NS, 2 * BOX), F32), ((2, 2, NS, EDGE), BF), ((BOX, SLOTS), BF),
             ((2 * NS, SLOTS), BF), ((16, SLOTS), BF), ((2 * NS, PAIR), BF), ((8, PAIR), jnp.int32),
+            ((NS, 2 * NS), BF),
         ],
-        field, interp, pair_src, pair_op, pair_target, oper,
+        field, interp, anterp, weights, pair_src, pair_op, pair_target, oper,
         flops=10**9,
         name="prepare",
     )
-    edge0, inter = lax.optimization_barrier((edge0, inter))
+    edge0, inter, own_mat = lax.optimization_barrier((edge0, inter, own_mat))
     edge1 = across(edge0)
     (inter,) = call(
         first_edge_kernel, [((NS, 2 * BOX), F32)], inter, halo_mat, edge0, currents,
         flops=4 * 10**8, name="first_edge",
     )
-    *buffers, parts = call(
+    *buffers, rounded = call(
         send_kernel,
-        [((BUF, CAP), BF)] * 4 + [((2, NS, 2 * BOX), BF)],
+        [((BUF, CAP), BF)] * 4 + [((NS, 2 * BOX), BF)],
         inter, halo_mat, edge1, currents, src_pick, oper_slot, slot_ids,
         flops=4 * 10**8,
         name="send",
@@ -392,14 +393,14 @@
     (own,) = call(
         own_kernel,
         [((NS, 2 * BOX), F32)],
-        parts, own_rows, oper_own,
+        rounded, own_rows, oper_own,
         flops=10**9,
         name="own",
     )
-    mats, matrix = call(
+    edge_mat, matrix = call(
         matrix_kernel,
-        [((NS + 2 * EDGE, 2 * NS), BF), ((len(OUTWARD) * CAP, 2 * NS), BF)],
-        rad, edge0, edge1, anterp, weights,
+        [((2 * EDGE, 2 * NS), BF), ((len(OUTWARD) * CAP, 2 * NS), BF)],
+        rad, edge0, edge1, own_mat,
         flops=10**9,
         name="matrix",
     )
@@ -415,7 +416,7 @@
     inward, keep = call(
         near_kernel,
         [(blocks(len(INWARD)), BF), (blocks(len(KEPT)), F32)],
-        rad, edge0, edge1, mats, stack,
+        rad, edge0, edge1, own_mat, edge_mat, stack,
         scratch=[pltpu.VMEM(((len(INWARD) + len(KEPT)) * CAP, 2 * NS), BF)],
         flops=10**9,
         name="near",

time: 77 us -> 74.8 us (0.971)
  Pallas kernels: 15.2 us -> 13.6 us
  starting transfers between devices: 36 us -> 35.1 us
    pallas_call x12, Pallas kernels: 15.2 us -> 13.6 us  [call(): pl.pallas_call(kernel, out_shape=shapes, scratch_shapes=list(scratch), co...]
    ppermute x1, starting transfers between devices: 2.86 us -> 2.04 us  [across(): return lax.ppermute(value, 'box', [(b, b ^ 1) for b in range(groups)])]
where the time goes in v5:
time: 74.8 us; the launch traced here: 74.3 us
  starting transfers between devices  35.1 us (47%)
  waiting for transfers between devices  22.7 us (30%)
  Pallas kernels  13.6 us (18%)
  local copies, waits for them, and re-layouts  2.67 us (4%)
    ppermute x5, waiting for transfers between devices, outward(): return lax.ppermute(value, ('box', 'samp'), pairs)  22 us
    ppermute x5, starting transfers between devices, outward(): return lax.ppermute(value, ('box', 'samp'), pairs)  20.3 us
    pallas_call x12, Pallas kernels, call(): pl.pallas_call(kernel, out_shape=shapes, scratch_shapes=list(scratch), co...  13.6 us
    ppermute x4, starting transfers between devices, sideways(): lax.ppermute(value, 'box', [(b, to) for b, to in pairs if 0 <= to < groups])  12.8 us
    unnamed x22, local copies, waits for them, and re-layouts  2.67 us
    ppermute x1, starting transfers between devices, across(): return lax.ppermute(value, 'box', [(b, b ^ 1) for b in range(groups)])  2.04 us
  transfers between devices with their start and end apart: 10, of which 5 were waited for; matrix products, arithmetic and copies ran while one was open for 0% of the time, Pallas kernels for 12%

profile of v5, /device:TPU:57, one launch (start us, length us, event | category | flops | bytes accessed | tf_op | source)
XLA Modules:
  0.0 74.3 jit_solution(11391381253850140462)
XLA Ops:
  0.0 1.9 %edge.1 = bf16[1552,128]{1,0:T(8,128)(2,1)S(1)} custom-call(bf16[512,1024]{1,0:T(8,128)(2,1)} %bitcast.5, f32[7,8]{1,0:T(8,128)} %anterp.1, f32[1,32]{1,0:T(1,128)} %bitcast.9), custom_call_target="tpu_custom_call" | custom-call | flops 100000000 | bytes 1446240 | tf_op jit(solution)/shard_map/edge/pallas_call | solution.py:314
  1.9 10.7 %collective-permute-start = (bf16[1552,128]{1,0:T(8,128)(2,1)S(1)}, bf16[1552,128]{1,0:T(8,128)(2,1)S(1)}, u32[]{:S(2)}, u32[]{:S(2)}) collective-permute-start(bf16[1552,128]{1,0:T(8,128)(2,1)S(1)} %edge.1), channel_id=1, source_target_pairs={{0,1},{1,2},{2,3},{3,4},{4,5},{5,6},{6,7},{7,0},{8,15},{9,8},{10,9... | collective-permute-start | bytes 1191944 | tf_op jit(solution)/shard_map/ppermute | solution.py:332
  12.6 0.0 copy-start
  12.6 1.4 %copy-done = bf16[2,1024,384]{2,1,0:T(8,128)(2,1)S(1)} copy-done((bf16[2,1024,384]{2,1,0:T(8,128)(2,1)S(1)}, bf16[2,1024,384]{2,1,0:T(8,128)(2,1)}, u32[]{:S(2)}) %copy-start) | copy-done | bytes 1572888
  14.0 1.2 %copy-done.2 = bf16[2,1024,32,8]{1,3,2,0:T(8,128)(2,1)S(1)} copy-done((bf16[2,1024,32,8]{1,3,2,0:T(8,128)(2,1)S(1)}, bf16[2,1024,32,8]{1,3,2,0:T(8,128)(2,1)}, u32[]{:S(2)}) %copy-start.2) | copy-done | bytes 1048600
  15.3 0.0 copy-start.8
  15.3 0.0 copy-start.9
  15.3 1.2 %field.1 = f32[256,768]{1,0:T(8,128)S(1)} custom-call(bf16[512,1024]{1,0:T(8,128)(2,1)S(1)} %bitcast.6, bf16[2,1024,384]{2,1,0:T(8,128)(2,1)S(1)} %copy-done), custom_call_target="tpu_custom_call" | custom-call | flops 1000000000 | bytes 3407872 | tf_op jit(solution)/shard_map/field/pallas_call | solution.py:314
  16.6 0.0 copy-start.1
  16.6 2.6 %prepare.1 = (f32[256,768]{1,0:T(8,128)S(1)}, bf16[2,2,256,96]{3,2,1,0:T(8,128)(2,1)S(1)}, bf16[384,512]{1,0:T(8,128)(2,1)S(1)}, bf16[512,512]{1,0:T(8,128)(2,1)...) custom-call(f32[256,768]{1,0:T(8,128)S(1)} %field.1, ...), custom_call_target="tpu_custom_call" | custom-call | flops 1000000000 | bytes 3973184 | tf_op jit(solution)/shard_map/prepare/pallas_call | solution.py:314
  19.2 2.0 %collective-permute-start.1 = (bf16[1552,128]{1,0:T(8,128)(2,1)S(1)}, bf16[1552,128]{1,0:T(8,128)(2,1)S(1)}, u32[]{:S(2)}, u32[]{:S(2)}) collective-permute-start(bf16[1552,128]{1,0:T(8,128)(2,1)S(1)} %collective-permute-done.edge0.edge), channel_id=1, source_target_pairs={{0,8},{8,0},{16,24},{24,16},{32,40},{40,32},{48,56},{56,48},{64,72... | collective-permute-start | bytes 1191944 | tf_op jit(solution)/shard_map/ppermute | solution.py:337
  21.3 0.9 %first_edge.1.inter = f32[256,768]{1,0:T(8,128)S(1)} custom-call(f32[256,768]{1,0:T(8,128)S(1)} %get-tuple-element.32.inter, bf16[2,2,256,96]{3,2,1,0:T(8,128)(2,1)S(1)} %get-tuple-element.33.halo_mat, bf16[1552,128]{1,0:T(8,128)(2,1)S(1)} %collective-permute-done.edge0.edge, bf16[2,1024,384]{2,1,0:T(8,128)(2,1)S(1)} %copy-done.1), custom_call_target="tpu_custom_call" | custom-call | flops 400000000 | bytes 3739648 | tf_op jit(solution)/shard_map/first_edge/pallas_call | solution.py:314
  22.2 0.7 collective-permute-done.1.edge1.edge
  22.8 1.3 %send.1 = (bf16[528,128]{1,0:T(8,128)(2,1)S(1)}, bf16[528,128]{1,0:T(8,128)(2,1)S(1)}, bf16[528,128]{1,0:T(8,128)(2,1)S(1)}, bf16[528,128]{1,0:T(8,128)(2,1)S(1)}, bf16[256,768]{1,0:T(8,128)(2,1)S(1)}) custom-call(f32[256,768]{1,0:T(8,128)S(1)} %first_edge.1.inter, bf16[2,2,256,96]{3,2,1,0:T(8,128)(2,1)S(1)} %get-tuple-element.33.halo_mat, ...), custom_call_target="tpu_custom_call" | custom-call | flops 400000000 | bytes 4820992 | tf_op jit(solution)/shard_map/send/pallas_call | solution.py:314
  24.2 3.1 %collective-permute-start.2 = (bf16[528,128]{1,0:T(8,128)(2,1)S(1)}, bf16[528,128]{1,0:T(8,128)(2,1)S(1)}, u32[]{:S(2)}, u32[]{:S(2)}) collective-permute-start(bf16[528,128]{1,0:T(8,128)(2,1)S(1)} %get-tuple-element.41), channel_id=1, source_target_pairs={{8,24},{16,0},{24,40},{32,16},{40,56},{48,32},{56,72},{64,48},{72,... | collective-permute-start | bytes 405512 | tf_op jit(solution)/shard_map/ppermute | solution.py:343
  27.3 4.3 %collective-permute-start.3 = (bf16[528,128]{1,0:T(8,128)(2,1)S(1)}, bf16[528,128]{1,0:T(8,128)(2,1)S(1)}, u32[]{:S(2)}, u32[]{:S(2)}) collective-permute-start(bf16[528,128]{1,0:T(8,128)(2,1)S(1)} %get-tuple-element.42), channel_id=1, source_target_pairs={{0,16},{16,32},{24,8},{32,48},{40,24},{48,64},{56,40},{64,80},{72,... | collective-permute-start | bytes 405512 | tf_op jit(solution)/shard_map/ppermute | solution.py:343
  31.6 1.9 %collective-permute-start.4 = (bf16[528,128]{1,0:T(8,128)(2,1)S(1)}, bf16[528,128]{1,0:T(8,128)(2,1)S(1)}, u32[]{:S(2)}, u32[]{:S(2)}) collective-permute-start(bf16[528,128]{1,0:T(8,128)(2,1)S(1)} %get-tuple-element.43), channel_id=1, source_target_pairs={{8,16},{16,8},{24,32},{32,24},{40,48},{48,40},{56,64},{64,56},{72,... | collective-permute-start | bytes 405512 | tf_op jit(solution)/shard_map/ppermute | solution.py:343
  33.5 3.5 %collective-permute-start.5 = (bf16[528,128]{1,0:T(8,128)(2,1)S(1)}, bf16[528,128]{1,0:T(8,128)(2,1)S(1)}, u32[]{:S(2)}, u32[]{:S(2)}) collective-permute-start(bf16[528,128]{1,0:T(8,128)(2,1)S(1)} %get-tuple-element.44), channel_id=1, source_target_pairs={{0,8},{8,0},{16,24},{24,16},{32,40},{40,32},{48,56},{56,48},{64,72... | collective-permute-start | bytes 405512 | tf_op jit(solution)/shard_map/ppermute | solution.py:343
  37.0 1.2 %own.1 = f32[256,768]{1,0:T(8,128)S(1)} custom-call(bf16[256,768]{1,0:T(8,128)(2,1)S(1)} %get-tuple-element.37.rounded, s32[8,640]{1,0:T(8,128)S(1)} %get-tuple-element.38.own_rows, bf16[512,640]{1,0:T(8,128)(2,1)S(1)} %get-tuple-element.39.oper_own), custom_call_target="tpu_custom_call" | custom-call | flops 1000000000 | bytes 1855488 | tf_op jit(solution)/shard_map/own/pallas_call | solution.py:314
  38.3 1.0 %matrix.1 = (bf16[192,512]{1,0:T(8,128)(2,1)S(1)}, bf16[384,512]{1,0:T(8,128)(2,1)S(1)}) custom-call(bf16[512,1024]{1,0:T(8,128)(2,1)S(1)} %bitcast.7, bf16[1552,128]{1,0:T(8,128)(2,1)S(1)} %collective-permute-done.edge0.edge, bf16[1552,128]{1,0:T(8,128)(2,1)S(1)} %collective-permute-done.1.edge1.edge, bf16[256,512]{1,0:T(8,128)(2,1)S(1)} %get-tuple-element.30.own_mat), custom_call_target="tpu_custom_call" | custom-call | flops 1000000000 | bytes 2695168 | tf_op jit(solution)/shard_map/matrix/pallas_call | solution.py:314
  39.3 0.9 %far.1 = (bf16[384,768]{1,0:T(8,128)(2,1)S(1)}, bf16[512,768]{1,0:T(8,128)(2,1)S(1)}) custom-call(f32[256,768]{1,0:T(8,128)S(1)} %own.1, bf16[384,512]{1,0:T(8,128)(2,1)S(1)} %get-tuple-element.40.matrix, bf16[528,128]{1,0:T(8,128)(2,1)S(1)} %collective-permute-done.2.got0, bf16[528,128]{1,0:T(8,128)(2,1)S(1)} %collective-permute-done.3.got1, ...), custom_call_target="tpu_custom_call" | custom-call | flops 500000000 | bytes 3096576 | tf_op jit(solution)/shard_map/far/pallas_call | solution.py:314
  40.2 3.4 %collective-permute-start.6 = (bf16[384,768]{1,0:T(8,128)(2,1)S(1)}, bf16[384,768]{1,0:T(8,128)(2,1)S(1)}, u32[]{:S(2)}, u32[]{:S(2)}) collective-permute-start(bf16[384,768]{1,0:T(8,128)(2,1)S(1)} %get-tuple-element.47), channel_id=1, source_target_pairs={{0,1},{1,2},{2,3},{3,4},{4,5},{5,6},{6,7},{7,0},{8,15},{9,8},{10,9... | collective-permute-start | bytes 1769480 | tf_op jit(solution)/shard_map/ppermute | solution.py:332
  43.6 1.5 %near.1 = (bf16[256,768]{1,0:T(8,128)(2,1)S(1)}, f32[384,768]{1,0:T(8,128)S(1)}) custom-call(bf16[512,1024]{1,0:T(8,128)(2,1)S(1)} %bitcast.8, bf16[1552,128]{1,0:T(8,128)(2,1)S(1)} %collective-permute-done.edge0.edge, bf16[1552,128]{1,0:T(8,128)(2,1)S(1)} %collective-permute-done.1.edge1.edge, bf16[256,512]{1,0:T(8,128)(2,1)S(1)} %get-tuple-element.30.own_mat, ...), custom_call_target="tpu_custom_call" | custom-call | flops 1000000000 | bytes 4661248 | tf_op jit(solution)/shard_map/near/pallas_call | solution.py:314
  45.1 1.9 %collective-permute-start.7 = (bf16[256,768]{1,0:T(8,128)(2,1)S(1)}, bf16[256,768]{1,0:T(8,128)(2,1)S(1)}, u32[]{:S(2)}, u32[]{:S(2)}) collective-permute-start(bf16[256,768]{1,0:T(8,128)(2,1)S(1)} %get-tuple-element.48), channel_id=1, source_target_pairs={{0,7},{1,0},{2,1},{3,2},{4,3},{5,4},{6,5},{7,6},{8,9},{9,10},{10,1... | collective-permute-start | bytes 1179656 | tf_op jit(solution)/shard_map/ppermute | solution.py:332
  47.1 5.4 %collective-permute-done.6.from_inner = bf16[384,768]{1,0:T(8,128)(2,1)S(1)} collective-permute-done((bf16[384,768]{1,0:T(8,128)(2,1)S(1)}, bf16[384,768]{1,0:T(8,128)(2,1)S(1)}, u32[]{:S(2)}, u32[]{:S(2)}) %collective-permute-start.6) | collective-permute-done | bytes 589856 | tf_op jit(solution)/shard_map/ppermute | solution.py:332
  52.5 2.3 %collective-permute-start.8 = (bf16[128,768]{1,0:T(8,128)(2,1)S(1)}, bf16[128,768]{1,0:T(8,128)(2,1)S(1)}, u32[]{:S(2)}, u32[]{:S(2)}) collective-permute-start(bf16[128,768]{1,0:T(8,128)(2,1)S(1)} %relay_out.1), channel_id=1, source_target_pairs={{0,2},{1,3},{2,4},{3,5},{4,6},{5,7},{6,0},{7,1},{8,14},{9,15},{10,... | collective-permute-start | bytes 589832 | tf_op jit(solution)/shard_map/ppermute | solution.py:332
  54.8 2.9 %collective-permute-done.7.from_outer = bf16[256,768]{1,0:T(8,128)(2,1)S(1)} collective-permute-done((bf16[256,768]{1,0:T(8,128)(2,1)S(1)}, bf16[256,768]{1,0:T(8,128)(2,1)S(1)}, u32[]{:S(2)}, u32[]{:S(2)}) %collective-permute-start.7) | collective-permute-done | bytes 393248 | tf_op jit(solution)/shard_map/ppermute | solution.py:332
  57.7 0.1 relay_in.1
  57.8 2.0 %collective-permute-start.9 = (bf16[128,768]{1,0:T(8,128)(2,1)S(1)}, bf16[128,768]{1,0:T(8,128)(2,1)S(1)}, u32[]{:S(2)}, u32[]{:S(2)}) collective-permute-start(bf16[128,768]{1,0:T(8,128)(2,1)S(1)} %relay_in.1), channel_id=1, source_target_pairs={{0,5},{1,6},{2,7},{3,0},{4,1},{5,2},{6,3},{7,4},{8,11},{9,12},{10,... | collective-permute-start | bytes 589832 | tf_op jit(solution)/shard_map/ppermute | solution.py:332
  59.8 1.5 %collective-permute-done.8.out2 = bf16[128,768]{1,0:T(8,128)(2,1)S(1)} collective-permute-done((bf16[128,768]{1,0:T(8,128)(2,1)S(1)}, bf16[128,768]{1,0:T(8,128)(2,1)S(1)}, u32[]{:S(2)}, u32[]{:S(2)}) %collective-permute-start.8) | collective-permute-done | bytes 196640 | tf_op jit(solution)/shard_map/ppermute | solution.py:332
  61.2 12.3 %collective-permute-done.9.in3 = bf16[128,768]{1,0:T(8,128)(2,1)S(1)} collective-permute-done((bf16[128,768]{1,0:T(8,128)(2,1)S(1)}, bf16[128,768]{1,0:T(8,128)(2,1)S(1)}, u32[]{:S(2)}, u32[]{:S(2)}) %collective-permute-start.9) | collective-permute-done | bytes 196640 | tf_op jit(solution)/shard_map/ppermute | solution.py:332
  73.5 0.8 %total.1 = bf16[2,128,384]{2,1,0:T(8,128)(2,1)} custom-call(f32[384,768]{1,0:T(8,128)S(1)} %get-tuple-element.46.keep, bf16[384,768]{1,0:T(8,128)(2,1)S(1)} %collective-permute-done.6.from_inner, bf16[256,768]{1,0:T(8,128)(2,1)S(1)} %collective-permute-done.7.from_outer, bf16[128,768]{1,0:T(8,128)(2,1)S(1)} %collective-permute-done.8.out2, ...), custom_call_target="tpu_custom_call" | custom-call | flops 100000000 | bytes 2752512 | tf_op jit(solution)/shard_map/total/pallas_call | solution.py:314
  (22 shorter events, 0.1 us)
Async XLA Ops:
  1.9 17.3 %collective-permute-start = (bf16[1552,128]{1,0:T(8,128)(2,1)S(1)}, bf16[1552,128]{1,0:T(8,128)(2,1)S(1)}, u32[]{:S(2)}, u32[]{:S(2)}) collective-permute-start(bf16[1552,128]{1,0:T(8,128)(2,1)S(1)} %edge.1), channel_id=1, source_target_pairs={{0,1},{1,2},{2,3},{3,4},{4,5},{5,6},{6,7},{7,0},{8,15},{9,8},{10,9... | collective-permute-start | bytes 1191944 | tf_op jit(solution)/shard_map/ppermute | solution.py:332
  12.6 1.4 %copy-start = (bf16[2,1024,384]{2,1,0:T(8,128)(2,1)S(1)}, bf16[2,1024,384]{2,1,0:T(8,128)(2,1)}, u32[]{:S(2)}) copy-start(bf16[2,1024,384]{2,1,0:T(8,128)(2,1)} %cur.5) | copy-start | bytes 4718596
  14.0 1.2 %copy-start.2 = (bf16[2,1024,32,8]{1,3,2,0:T(8,128)(2,1)S(1)}, bf16[2,1024,32,8]{1,3,2,0:T(8,128)(2,1)}, u32[]{:S(2)}) copy-start(bf16[2,1024,32,8]{1,3,2,0:T(8,128)(2,1)} %param.10) | copy-start | bytes 3145732
  15.3 1.3 %copy-start.4 = (f32[7,8]{1,0:T(8,128)S(1)}, f32[7,8]{1,0:T(8,128)}, u32[]{:S(2)}) copy-start(f32[7,8]{1,0:T(8,128)} %anterp.1) | copy-start | bytes 676
  15.3 1.3 %copy-start.5 = (f32[32]{0:T(128)S(1)}, f32[32]{0:T(128)}, u32[]{:S(2)}) copy-start(f32[32]{0:T(128)} %param.13) | copy-start | bytes 388
  15.3 1.3 %copy-start.6 = (bf16[2,32,8,316]{3,2,1,0:T(8,128)(2,1)S(1)}, bf16[2,32,8,316]{3,2,1,0:T(8,128)(2,1)}, u32[]{:S(2)}) copy-start(bf16[2,32,8,316]{3,2,1,0:T(8,128)(2,1)} %param.14) | copy-start | bytes 970756
  15.3 1.3 %copy-start.7 = (f32[7,8]{1,0:T(8,128)S(1)}, f32[7,8]{1,0:T(8,128)}, u32[]{:S(2)}) copy-start(f32[7,8]{1,0:T(8,128)} %interp.1) | copy-start | bytes 676
  15.3 1.3 %copy-start.8 = (s32[640]{0:T(1024)S(1)}, s32[640]{0:T(1024)}, u32[]{:S(2)}) copy-start(s32[640]{0:T(1024)} %pair_src.1) | copy-start | bytes 7684
  15.3 1.3 %copy-start.9 = (s32[640]{0:T(1024)S(1)}, s32[640]{0:T(1024)}, u32[]{:S(2)}) copy-start(s32[640]{0:T(1024)} %pair_op.1) | copy-start | bytes 7684
  15.3 1.3 %copy-start.10 = (s32[640]{0:T(1024)S(1)}, s32[640]{0:T(1024)}, u32[]{:S(2)}) copy-start(s32[640]{0:T(1024)} %pair_target.1) | copy-start | bytes 7684
  16.6 4.6 %copy-start.1 = (bf16[2,1024,384]{2,1,0:T(8,128)(2,1)S(1)}, bf16[2,1024,384]{2,1,0:T(8,128)(2,1)}, u32[]{:S(2)}) copy-start(bf16[2,1024,384]{2,1,0:T(8,128)(2,1)} %cur.5) | copy-start | bytes 4718596
  19.2 3.6 %collective-permute-start.1 = (bf16[1552,128]{1,0:T(8,128)(2,1)S(1)}, bf16[1552,128]{1,0:T(8,128)(2,1)S(1)}, u32[]{:S(2)}, u32[]{:S(2)}) collective-permute-start(bf16[1552,128]{1,0:T(8,128)(2,1)S(1)} %collective-permute-done.edge0.edge), channel_id=1, source_target_pairs={{0,8},{8,0},{16,24},{24,16},{32,40},{40,32},{48,56},{56,48},{64,72... | collective-permute-start | bytes 1191944 | tf_op jit(solution)/shard_map/ppermute | solution.py:337
  24.2 15.0 %collective-permute-start.2 = (bf16[528,128]{1,0:T(8,128)(2,1)S(1)}, bf16[528,128]{1,0:T(8,128)(2,1)S(1)}, u32[]{:S(2)}, u32[]{:S(2)}) collective-permute-start(bf16[528,128]{1,0:T(8,128)(2,1)S(1)} %get-tuple-element.41), channel_id=1, source_target_pairs={{8,24},{16,0},{24,40},{32,16},{40,56},{48,32},{56,72},{64,48},{72,... | collective-permute-start | bytes 405512 | tf_op jit(solution)/shard_map/ppermute | solution.py:343
  27.3 11.9 %collective-permute-start.3 = (bf16[528,128]{1,0:T(8,128)(2,1)S(1)}, bf16[528,128]{1,0:T(8,128)(2,1)S(1)}, u32[]{:S(2)}, u32[]{:S(2)}) collective-permute-start(bf16[528,128]{1,0:T(8,128)(2,1)S(1)} %get-tuple-element.42), channel_id=1, source_target_pairs={{0,16},{16,32},{24,8},{32,48},{40,24},{48,64},{56,40},{64,80},{72,... | collective-permute-start | bytes 405512 | tf_op jit(solution)/shard_map/ppermute | solution.py:343
  31.6 7.7 %collective-permute-start.4 = (bf16[528,128]{1,0:T(8,128)(2,1)S(1)}, bf16[528,128]{1,0:T(8,128)(2,1)S(1)}, u32[]{:S(2)}, u32[]{:S(2)}) collective-permute-start(bf16[528,128]{1,0:T(8,128)(2,1)S(1)} %get-tuple-element.43), channel_id=1, source_target_pairs={{8,16},{16,8},{24,32},{32,24},{40,48},{48,40},{56,64},{64,56},{72,... | collective-permute-start | bytes 405512 | tf_op jit(solution)/shard_map/ppermute | solution.py:343
  33.5 5.7 %collective-permute-start.5 = (bf16[528,128]{1,0:T(8,128)(2,1)S(1)}, bf16[528,128]{1,0:T(8,128)(2,1)S(1)}, u32[]{:S(2)}, u32[]{:S(2)}) collective-permute-start(bf16[528,128]{1,0:T(8,128)(2,1)S(1)} %get-tuple-element.44), channel_id=1, source_target_pairs={{0,8},{8,0},{16,24},{24,16},{32,40},{40,32},{48,56},{56,48},{64,72... | collective-permute-start | bytes 405512 | tf_op jit(solution)/shard_map/ppermute | solution.py:343
  37.0 1.2 %copy-start.3 = (bf16[2,1024,32,8]{1,3,2,0:T(8,128)(2,1)S(1)}, bf16[2,1024,32,8]{1,3,2,0:T(8,128)(2,1)}, u32[]{:S(2)}) copy-start(bf16[2,1024,32,8]{1,3,2,0:T(8,128)(2,1)} %param.10) | copy-start | bytes 3145732
  40.2 12.3 %collective-permute-start.6 = (bf16[384,768]{1,0:T(8,128)(2,1)S(1)}, bf16[384,768]{1,0:T(8,128)(2,1)S(1)}, u32[]{:S(2)}, u32[]{:S(2)}) collective-permute-start(bf16[384,768]{1,0:T(8,128)(2,1)S(1)} %get-tuple-element.47), channel_id=1, source_target_pairs={{0,1},{1,2},{2,3},{3,4},{4,5},{5,6},{6,7},{7,0},{8,15},{9,8},{10,9... | collective-permute-start | bytes 1769480 | tf_op jit(solution)/shard_map/ppermute | solution.py:332
  45.1 12.6 %collective-permute-start.7 = (bf16[256,768]{1,0:T(8,128)(2,1)S(1)}, bf16[256,768]{1,0:T(8,128)(2,1)S(1)}, u32[]{:S(2)}, u32[]{:S(2)}) collective-permute-start(bf16[256,768]{1,0:T(8,128)(2,1)S(1)} %get-tuple-element.48), channel_id=1, source_target_pairs={{0,7},{1,0},{2,1},{3,2},{4,3},{5,4},{6,5},{7,6},{8,9},{9,10},{10,1... | collective-permute-start | bytes 1179656 | tf_op jit(solution)/shard_map/ppermute | solution.py:332
  52.5 8.7 %collective-permute-start.8 = (bf16[128,768]{1,0:T(8,128)(2,1)S(1)}, bf16[128,768]{1,0:T(8,128)(2,1)S(1)}, u32[]{:S(2)}, u32[]{:S(2)}) collective-permute-start(bf16[128,768]{1,0:T(8,128)(2,1)S(1)} %relay_out.1), channel_id=1, source_target_pairs={{0,2},{1,3},{2,4},{3,5},{4,6},{5,7},{6,0},{7,1},{8,14},{9,15},{10,... | collective-permute-start | bytes 589832 | tf_op jit(solution)/shard_map/ppermute | solution.py:332
  57.8 15.8 %collective-permute-start.9 = (bf16[128,768]{1,0:T(8,128)(2,1)S(1)}, bf16[128,768]{1,0:T(8,128)(2,1)S(1)}, u32[]{:S(2)}, u32[]{:S(2)}) collective-permute-start(bf16[128,768]{1,0:T(8,128)(2,1)S(1)} %relay_in.1), channel_id=1, source_target_pairs={{0,5},{1,6},{2,7},{3,0},{4,1},{5,2},{6,3},{7,4},{8,11},{9,12},{10,... | collective-permute-start | bytes 589832 | tf_op jit(solution)/shard_map/ppermute | solution.py:332

commit v6 on v5

--- a/solution.py
+++ b/solution.py
@@ -28,7 +28,9 @@
 KEPT = (0, 2, 5)
 BF = jnp.bfloat16
 HBM = pl.BlockSpec(memory_space=pltpu.HBM)
-EDGE_PARTS = 4
+VMEM = pl.BlockSpec(memory_space=pltpu.VMEM)
+EDGE_PARTS = 2
+FIELD_PARTS = 4
 F32 = jnp.float32
 
 NN = (((1,), (0,)), ((), ()))
@@ -129,10 +131,22 @@
     return with_re[:rows] - with_im[rows:], with_im[:rows] + with_re[rows:]
 
 
-def field_kernel(rad, cur, field):
-    re, im = radiate(rad[...], cur, NS)
-    field[:, :BOX] = re
-    field[:, BOX:] = im
+def field_kernel(rad, cur_all, field, cur, sems):
+    depth = P_SIZE // FIELD_PARTS
+    copies = []
+    for i in range(FIELD_PARTS):
+        rows = pl.ds(i * depth, depth)
+        copies.append(pltpu.make_async_copy(cur_all.at[:, rows, :], cur.at[:, rows, :], sems.at[i]))
+    for copy in copies:
+        copy.start()
+    with_re, with_im = 0.0, 0.0
+    for i in range(FIELD_PARTS):
+        copies[i].wait()
+        rows = slice(i * depth, (i + 1) * depth)
+        with_re = with_re + dot(rad[:, rows], cur[0, rows, :])
+        with_im = with_im + dot(rad[:, rows], cur[1, rows, :])
+    field[:, :BOX] = with_re[:NS] - with_im[NS:]
+    field[:, BOX:] = with_im[:NS] + with_re[NS:]
 
 
 def prepare_kernel(
@@ -239,22 +253,35 @@
     own[:, BOX:] = dot(c_im, table, NTR)
 
 
-def matrix_rows(rad, edge0, edge1, own_mat, edge_mat, steps, out):
-    me = lax.axis_index("samp")
-    side = 1 - 2 * parity()
+def halves(product):
+    return product[:, :NS] + product[:, NS:]
+
+
+def own_terms(rad, own_mat, steps, c):
+    me, side = lax.axis_index("samp"), 1 - 2 * parity()
+    blocks = []
+    for j in steps:
+        cols = pl.ds(pl.multiple_of(((me + side * j) & (RANKS - 1)) * CAP, CAP), CAP)
+        blocks.append(rad[c * NS : (c + 1) * NS, cols])
+    return halves(dot(jnp.concatenate(blocks, axis=1), own_mat[...], TN))
+
+
+def edge_terms(edge0, edge1, edge_mat, steps, c):
+    me, side = lax.axis_index("samp"), 1 - 2 * parity()
+    blocks = []
+    for j in steps:
+        first = ((me + side * j) & (RANKS - 1)) * 2 * EDGE + c * EDGE
+        rows = pl.ds(pl.multiple_of(first, 32), EDGE)
+        blocks.append(jnp.concatenate([edge0[rows, :], edge1[rows, :]], axis=0))
+    return halves(dot(jnp.concatenate(blocks, axis=1), edge_mat[...], TN))
+
+
+def own_matrix_kernel(rad, own_mat, out):
     for c in range(2):
-        mine, beside = [], []
-        for j in steps:
-            block = (me + side * j) & (RANKS - 1)
-            mine.append(rad[c * NS : (c + 1) * NS, pl.ds(pl.multiple_of(block * CAP, CAP), CAP)])
-            rows = pl.ds(pl.multiple_of(block * 2 * EDGE + c * EDGE, 32), EDGE)
-            beside.append(jnp.concatenate([edge0[rows, :], edge1[rows, :]], axis=0))
-        both = dot(jnp.concatenate(mine, axis=1), own_mat[...], TN)
-        both = both + dot(jnp.concatenate(beside, axis=1), edge_mat[...], TN)
-        out[:, c * NS : (c + 1) * NS] = (both[:, :NS] + both[:, NS:]).astype(BF)
-
-
-def matrix_kernel(rad, edge0, edge1, own_mat, edge_mat, out):
+        out[:, c * NS : (c + 1) * NS] = own_terms(rad, own_mat, OUTWARD, c)
+
+
+def matrix_kernel(own, edge0, edge1, edge_mat, out):
     shape = (EDGE, NS)
     t_row, j_row = edge_place(shape, 0)
     t_col, g_col = local_place(shape, 1)
@@ -266,7 +293,9 @@
         base = jnp.where(odd == side, 2 * WIDTH, WIDTH - FD)
         bands.append(band(cols, g_col - j_row + base, t_row == t_col))
     edge_mat[:, :NS], edge_mat[:, NS:] = split(jnp.concatenate(bands, axis=0))
-    matrix_rows(rad, edge0, edge1, own_mat, edge_mat, OUTWARD, out)
+    for c in range(2):
+        cols = slice(c * NS, (c + 1) * NS)
+        out[:, cols] = (own[:, cols] + edge_terms(edge0, edge1, edge_mat, OUTWARD, c)).astype(BF)
 
 
 def far_kernel(own, matrix, got0, got1, got2, got3, out, stack):
@@ -285,7 +314,10 @@
 
 
 def near_kernel(rad, edge0, edge1, own_mat, edge_mat, stack, inward, keep, matrix):
-    matrix_rows(rad, edge0, edge1, own_mat, edge_mat, INWARD + KEPT, matrix)
+    steps = INWARD + KEPT
+    for c in range(2):
+        terms = own_terms(rad, own_mat, steps, c) + edge_terms(edge0, edge1, edge_mat, steps, c)
+        matrix[:, c * NS : (c + 1) * NS] = terms.astype(BF)
     cut = len(INWARD) * CAP
     inward[...] = dot(matrix[0:cut, :], stack[...]).astype(BF)
     keep[...] = dot(matrix[cut:, :], stack[...])
@@ -349,12 +381,11 @@
     rad = jnp.transpose(radiation, (0, 2, 3, 1)).reshape(2 * NS, P_SIZE)
     oper = operators.reshape(2 * NS, NOPS)
     weights = weights.reshape(1, NT)
-    (edge,) = call(
+    edge, rad = call(
         edge_kernel,
-        [((TAIL + 16, CAP), BF)],
+        [((TAIL + 16, CAP), BF), (rad.shape, BF)],
         *(pltpu.with_memory_space_constraint(a, pltpu.HBM) for a in (rad, anterp, weights)),
         scratch=[
-            pltpu.VMEM((2 * NS, P_SIZE), BF),
             pltpu.VMEM((2 * WIDTH + 1, FD), F32),
             pltpu.VMEM((1, NT), F32),
             pltpu.SemaphoreType.DMA((EDGE_PARTS + 2,)),
@@ -364,7 +395,15 @@
     )
     edge0 = outward(edge, 1)
 
-    (field,) = call(field_kernel, [((NS, 2 * BOX), F32)], rad, currents, flops=10**9, name="field")
+    field, currents = call(
+        field_kernel,
+        [((NS, 2 * BOX), F32), (currents.shape, BF)],
+        rad, pltpu.with_memory_space_constraint(currents, pltpu.HBM),
+        scratch=[pltpu.SemaphoreType.DMA((FIELD_PARTS,))],
+        flops=10**9,
+        name="field",
+        in_specs=[VMEM, HBM],
+    )
     inter, halo_mat, src_pick, oper_slot, slot_ids, oper_own, own_rows, own_mat = call(
         prepare_kernel,
         [
@@ -376,7 +415,14 @@
         flops=10**9,
         name="prepare",
     )
-    edge0, inter, own_mat = lax.optimization_barrier((edge0, inter, own_mat))
+    (own_matrix,) = call(
+        own_matrix_kernel,
+        [((len(OUTWARD) * CAP, 2 * NS), F32)],
+        rad, own_mat,
+        flops=5 * 10**8,
+        name="own_matrix",
+    )
+    edge0, inter, own_matrix = lax.optimization_barrier((edge0, inter, own_matrix))
     edge1 = across(edge0)
     (inter,) = call(
         first_edge_kernel, [((NS, 2 * BOX), F32)], inter, halo_mat, edge0, currents,
@@ -400,7 +446,7 @@
     edge_mat, matrix = call(
         matrix_kernel,
         [((2 * EDGE, 2 * NS), BF), ((len(OUTWARD) * CAP, 2 * NS), BF)],
-        rad, edge0, edge1, own_mat,
+        own_matrix, edge0, edge1,
         flops=10**9,
         name="matrix",
     )

time: 74.8 us -> 74.7 us (level); the launches traced: 74.3 us -> 73.2 us
  local copies, waits for them, and re-layouts: 2.67 us -> 0.04 us
  starting transfers between devices: 35.1 us -> 36.6 us
  Pallas kernels: 13.6 us -> 14.9 us
  waiting for transfers between devices: 22.7 us -> 21.4 us
    unnamed x22 -> x14, local copies, waits for them, and re-layouts: 2.67 us -> 0.04 us
    pallas_call x12 -> x13, Pallas kernels: 13.6 us -> 14.9 us  [call(): pl.pallas_call(kernel, out_shape=shapes, scratch_shapes=list(scratch), co...]
    ppermute x5, waiting for transfers between devices: 22 us -> 21 us  [outward(): return lax.ppermute(value, ('box', 'samp'), pairs)]
    ppermute x1, starting transfers between devices: 2.04 us -> 2.91 us  [across(): return lax.ppermute(value, 'box', [(b, b ^ 1) for b in range(groups)])]
  transfers between devices with their start and end apart: 10 -> 10, of which waited for: 5 -> 5; matrix products, arithmetic and copies ran while one was open for 0% -> 0% of each run, Pallas kernels for 12% -> 14%
where the time goes in v6:
time: 74.7 us; the launch traced here: 73.2 us
  starting transfers between devices  36.6 us (49%)
  waiting for transfers between devices  21.4 us (29%)
  Pallas kernels  14.9 us (20%)
    ppermute x5, waiting for transfers between devices, outward(): return lax.ppermute(value, ('box', 'samp'), pairs)  21 us
    ppermute x5, starting transfers between devices, outward(): return lax.ppermute(value, ('box', 'samp'), pairs)  20.9 us
    pallas_call x13, Pallas kernels, call(): pl.pallas_call(kernel, out_shape=shapes, scratch_shapes=list(scratch), co...  14.9 us
    ppermute x4, starting transfers between devices, sideways(): lax.ppermute(value, 'box', [(b, to) for b, to in pairs if 0 <= to < groups])  12.8 us
    ppermute x1, starting transfers between devices, across(): return lax.ppermute(value, 'box', [(b, b ^ 1) for b in range(groups)])  2.91 us
  transfers between devices with their start and end apart: 10, of which 5 were waited for; matrix products, arithmetic and copies ran while one was open for 0% of the time, Pallas kernels for 14%

profile of v6, /device:TPU:57, one launch (start us, length us, event | category | flops | bytes accessed | tf_op | source)
XLA Modules:
  0.0 73.2 jit_solution(3224663216919350945)
XLA Ops:
  0.0 1.7 %edge.1 = (bf16[1552,128]{1,0:T(8,128)(2,1)S(1)}, bf16[512,1024]{1,0:T(8,128)(2,1)S(1)}) custom-call(bf16[512,1024]{1,0:T(8,128)(2,1)} %bitcast.8, f32[7,8]{1,0:T(8,128)} %anterp.1, f32[1,32]{1,0:T(1,128)} %bitcast.5), custom_call_target="tpu_custom_call" | custom-call | flops 100000000 | bytes 2494816 | tf_op jit(solution)/shard_map/edge/pallas_call | solution.py:346
  1.7 10.7 %collective-permute-start = (bf16[1552,128]{1,0:T(8,128)(2,1)S(1)}, bf16[1552,128]{1,0:T(8,128)(2,1)S(1)}, u32[]{:S(2)}, u32[]{:S(2)}) collective-permute-start(bf16[1552,128]{1,0:T(8,128)(2,1)S(1)} %get-tuple-element.32), channel_id=1, source_target_pairs={{0,1},{1,2},{2,3},{3,4},{4,5},{5,6},{6,7},{7,0},{8,15},{9,8},{10,9... | collective-permute-start | bytes 1191944 | tf_op jit(solution)/shard_map/ppermute | solution.py:364
  12.4 0.0 copy-start
  12.4 0.0 copy-start.1
  12.4 0.0 copy-start.2
  12.5 0.0 copy-start.5
  12.5 0.0 copy-start.6
  12.5 2.6 %field.1 = (f32[256,768]{1,0:T(8,128)S(1)}, bf16[2,1024,384]{2,1,0:T(8,128)(2,1)S(1)}) custom-call(bf16[512,1024]{1,0:T(8,128)(2,1)S(1)} %get-tuple-element.31.rad, bf16[2,1024,384]{2,1,0:T(8,128)(2,1)} %cur_all.1), custom_call_target="tpu_custom_call" | custom-call | flops 1000000000 | bytes 4980736 | tf_op jit(solution)/shard_map/field/pallas_call | solution.py:346
  15.1 2.6 %prepare.1 = (f32[256,768]{1,0:T(8,128)S(1)}, bf16[2,2,256,96]{3,2,1,0:T(8,128)(2,1)S(1)}, bf16[384,512]{1,0:T(8,128)(2,1)S(1)}, bf16[512,512]{1,0:T(8,128)(2,1)...) custom-call(f32[256,768]{1,0:T(8,128)S(1)} %get-tuple-element.33.fie, ...), custom_call_target="tpu_custom_call" | custom-call | flops 1000000000 | bytes 3973184 | tf_op jit(solution)/shard_map/prepare/pallas_call | solution.py:346
  17.7 0.4 own_matrix.1.own
  18.1 2.9 %collective-permute-start.1 = (bf16[1552,128]{1,0:T(8,128)(2,1)S(1)}, bf16[1552,128]{1,0:T(8,128)(2,1)S(1)}, u32[]{:S(2)}, u32[]{:S(2)}) collective-permute-start(bf16[1552,128]{1,0:T(8,128)(2,1)S(1)} %collective-permute-done.edge0.edge), channel_id=1, source_target_pairs={{0,8},{8,0},{16,24},{24,16},{32,40},{40,32},{48,56},{56,48},{64,72... | collective-permute-start | bytes 1191944 | tf_op jit(solution)/shard_map/ppermute | solution.py:369
  21.0 0.9 %first_edge.1.inter = f32[256,768]{1,0:T(8,128)S(1)} custom-call(f32[256,768]{1,0:T(8,128)S(1)} %get-tuple-element.39.inter, bf16[2,2,256,96]{3,2,1,0:T(8,128)(2,1)S(1)} %get-tuple-element.40.halo_mat, bf16[1552,128]{1,0:T(8,128)(2,1)S(1)} %collective-permute-done.edge0.edge, bf16[2,1024,384]{2,1,0:T(8,128)(2,1)S(1)} %get-tuple-element.41.cur), custom_call_target="tpu_custom_call" | custom-call | flops 400000000 | bytes 3739648 | tf_op jit(solution)/shard_map/first_edge/pallas_call | solution.py:346
  22.0 0.4 collective-permute-done.1.edge1.edge
  22.4 1.4 %send.1 = (bf16[528,128]{1,0:T(8,128)(2,1)S(1)}, bf16[528,128]{1,0:T(8,128)(2,1)S(1)}, bf16[528,128]{1,0:T(8,128)(2,1)S(1)}, bf16[528,128]{1,0:T(8,128)(2,1)S(1)}, bf16[256,768]{1,0:T(8,128)(2,1)S(1)}) custom-call(f32[256,768]{1,0:T(8,128)S(1)} %first_edge.1.inter, bf16[2,2,256,96]{3,2,1,0:T(8,128)(2,1)S(1)} %get-tuple-element.40.halo_mat, ...), custom_call_target="tpu_custom_call" | custom-call | flops 400000000 | bytes 4820992 | tf_op jit(solution)/shard_map/send/pallas_call | solution.py:346
  23.7 3.1 %collective-permute-start.2 = (bf16[528,128]{1,0:T(8,128)(2,1)S(1)}, bf16[528,128]{1,0:T(8,128)(2,1)S(1)}, u32[]{:S(2)}, u32[]{:S(2)}) collective-permute-start(bf16[528,128]{1,0:T(8,128)(2,1)S(1)} %get-tuple-element.49), channel_id=1, source_target_pairs={{8,24},{16,0},{24,40},{32,16},{40,56},{48,32},{56,72},{64,48},{72,... | collective-permute-start | bytes 405512 | tf_op jit(solution)/shard_map/ppermute | solution.py:375
  26.9 4.3 %collective-permute-start.3 = (bf16[528,128]{1,0:T(8,128)(2,1)S(1)}, bf16[528,128]{1,0:T(8,128)(2,1)S(1)}, u32[]{:S(2)}, u32[]{:S(2)}) collective-permute-start(bf16[528,128]{1,0:T(8,128)(2,1)S(1)} %get-tuple-element.50), channel_id=1, source_target_pairs={{0,16},{16,32},{24,8},{32,48},{40,24},{48,64},{56,40},{64,80},{72,... | collective-permute-start | bytes 405512 | tf_op jit(solution)/shard_map/ppermute | solution.py:375
  31.1 1.9 %collective-permute-start.4 = (bf16[528,128]{1,0:T(8,128)(2,1)S(1)}, bf16[528,128]{1,0:T(8,128)(2,1)S(1)}, u32[]{:S(2)}, u32[]{:S(2)}) collective-permute-start(bf16[528,128]{1,0:T(8,128)(2,1)S(1)} %get-tuple-element.51), channel_id=1, source_target_pairs={{8,16},{16,8},{24,32},{32,24},{40,48},{48,40},{56,64},{64,56},{72,... | collective-permute-start | bytes 405512 | tf_op jit(solution)/shard_map/ppermute | solution.py:375
  33.1 3.4 %collective-permute-start.5 = (bf16[528,128]{1,0:T(8,128)(2,1)S(1)}, bf16[528,128]{1,0:T(8,128)(2,1)S(1)}, u32[]{:S(2)}, u32[]{:S(2)}) collective-permute-start(bf16[528,128]{1,0:T(8,128)(2,1)S(1)} %get-tuple-element.52), channel_id=1, source_target_pairs={{0,8},{8,0},{16,24},{24,16},{32,40},{40,32},{48,56},{56,48},{64,72... | collective-permute-start | bytes 405512 | tf_op jit(solution)/shard_map/ppermute | solution.py:375
  36.5 1.2 %own.1 = f32[256,768]{1,0:T(8,128)S(1)} custom-call(bf16[256,768]{1,0:T(8,128)(2,1)S(1)} %get-tuple-element.45.rounded, s32[8,640]{1,0:T(8,128)S(1)} %get-tuple-element.46.own_rows, bf16[512,640]{1,0:T(8,128)(2,1)S(1)} %get-tuple-element.47.oper_own), custom_call_target="tpu_custom_call" | custom-call | flops 1000000000 | bytes 1855488 | tf_op jit(solution)/shard_map/own/pallas_call | solution.py:346
  37.8 0.8 %matrix.1 = (bf16[192,512]{1,0:T(8,128)(2,1)S(1)}, bf16[384,512]{1,0:T(8,128)(2,1)S(1)}) custom-call(f32[384,512]{1,0:T(8,128)S(1)} %own_matrix.1.own, bf16[1552,128]{1,0:T(8,128)(2,1)S(1)} %collective-permute-done.edge0.edge, bf16[1552,128]{1,0:T(8,128)(2,1)S(1)} %collective-permute-done.1.edge1.edge), custom_call_target="tpu_custom_call" | custom-call | flops 1000000000 | bytes 2170880 | tf_op jit(solution)/shard_map/matrix/pallas_call | solution.py:346
  38.6 0.9 %far.1 = (bf16[384,768]{1,0:T(8,128)(2,1)S(1)}, bf16[512,768]{1,0:T(8,128)(2,1)S(1)}) custom-call(f32[256,768]{1,0:T(8,128)S(1)} %own.1, bf16[384,512]{1,0:T(8,128)(2,1)S(1)} %get-tuple-element.48.matrix, bf16[528,128]{1,0:T(8,128)(2,1)S(1)} %collective-permute-done.2.got0, bf16[528,128]{1,0:T(8,128)(2,1)S(1)} %collective-permute-done.3.got1, ...), custom_call_target="tpu_custom_call" | custom-call | flops 500000000 | bytes 3096576 | tf_op jit(solution)/shard_map/far/pallas_call | solution.py:346
  39.5 3.6 %collective-permute-start.6 = (bf16[384,768]{1,0:T(8,128)(2,1)S(1)}, bf16[384,768]{1,0:T(8,128)(2,1)S(1)}, u32[]{:S(2)}, u32[]{:S(2)}) collective-permute-start(bf16[384,768]{1,0:T(8,128)(2,1)S(1)} %get-tuple-element.55), channel_id=1, source_target_pairs={{0,1},{1,2},{2,3},{3,4},{4,5},{5,6},{6,7},{7,0},{8,15},{9,8},{10,9... | collective-permute-start | bytes 1769480 | tf_op jit(solution)/shard_map/ppermute | solution.py:364
  43.2 1.5 %near.1 = (bf16[256,768]{1,0:T(8,128)(2,1)S(1)}, f32[384,768]{1,0:T(8,128)S(1)}) custom-call(bf16[512,1024]{1,0:T(8,128)(2,1)S(1)} %get-tuple-element.31.rad, bf16[1552,128]{1,0:T(8,128)(2,1)S(1)} %collective-permute-done.edge0.edge, bf16[1552,128]{1,0:T(8,128)(2,1)S(1)} %collective-permute-done.1.edge1.edge, ...), custom_call_target="tpu_custom_call" | custom-call | flops 1000000000 | bytes 4661248 | tf_op jit(solution)/shard_map/near/pallas_call | solution.py:346
  44.7 1.9 %collective-permute-start.7 = (bf16[256,768]{1,0:T(8,128)(2,1)S(1)}, bf16[256,768]{1,0:T(8,128)(2,1)S(1)}, u32[]{:S(2)}, u32[]{:S(2)}) collective-permute-start(bf16[256,768]{1,0:T(8,128)(2,1)S(1)} %get-tuple-element.56), channel_id=1, source_target_pairs={{0,7},{1,0},{2,1},{3,2},{4,3},{5,4},{6,5},{7,6},{8,9},{9,10},{10,1... | collective-permute-start | bytes 1179656 | tf_op jit(solution)/shard_map/ppermute | solution.py:364
  46.6 4.7 %collective-permute-done.6.from_inner = bf16[384,768]{1,0:T(8,128)(2,1)S(1)} collective-permute-done((bf16[384,768]{1,0:T(8,128)(2,1)S(1)}, bf16[384,768]{1,0:T(8,128)(2,1)S(1)}, u32[]{:S(2)}, u32[]{:S(2)}) %collective-permute-start.6) | collective-permute-done | bytes 589856 | tf_op jit(solution)/shard_map/ppermute | solution.py:364
  51.4 2.7 %collective-permute-start.8 = (bf16[128,768]{1,0:T(8,128)(2,1)S(1)}, bf16[128,768]{1,0:T(8,128)(2,1)S(1)}, u32[]{:S(2)}, u32[]{:S(2)}) collective-permute-start(bf16[128,768]{1,0:T(8,128)(2,1)S(1)} %relay_out.1), channel_id=1, source_target_pairs={{0,2},{1,3},{2,4},{3,5},{4,6},{5,7},{6,0},{7,1},{8,14},{9,15},{10,... | collective-permute-start | bytes 589832 | tf_op jit(solution)/shard_map/ppermute | solution.py:364
  54.1 3.4 %collective-permute-done.7.from_outer = bf16[256,768]{1,0:T(8,128)(2,1)S(1)} collective-permute-done((bf16[256,768]{1,0:T(8,128)(2,1)S(1)}, bf16[256,768]{1,0:T(8,128)(2,1)S(1)}, u32[]{:S(2)}, u32[]{:S(2)}) %collective-permute-start.7) | collective-permute-done | bytes 393248 | tf_op jit(solution)/shard_map/ppermute | solution.py:364
  57.5 0.1 relay_in.1
  57.5 1.9 %collective-permute-start.9 = (bf16[128,768]{1,0:T(8,128)(2,1)S(1)}, bf16[128,768]{1,0:T(8,128)(2,1)S(1)}, u32[]{:S(2)}, u32[]{:S(2)}) collective-permute-start(bf16[128,768]{1,0:T(8,128)(2,1)S(1)} %relay_in.1), channel_id=1, source_target_pairs={{0,5},{1,6},{2,7},{3,0},{4,1},{5,2},{6,3},{7,4},{8,11},{9,12},{10,... | collective-permute-start | bytes 589832 | tf_op jit(solution)/shard_map/ppermute | solution.py:364
  59.5 0.4 collective-permute-done.8.out2
  59.9 12.5 %collective-permute-done.9.in3 = bf16[128,768]{1,0:T(8,128)(2,1)S(1)} collective-permute-done((bf16[128,768]{1,0:T(8,128)(2,1)S(1)}, bf16[128,768]{1,0:T(8,128)(2,1)S(1)}, u32[]{:S(2)}, u32[]{:S(2)}) %collective-permute-start.9) | collective-permute-done | bytes 196640 | tf_op jit(solution)/shard_map/ppermute | solution.py:364
  72.4 0.8 %total.1 = bf16[2,128,384]{2,1,0:T(8,128)(2,1)} custom-call(f32[384,768]{1,0:T(8,128)S(1)} %get-tuple-element.54.keep, bf16[384,768]{1,0:T(8,128)(2,1)S(1)} %collective-permute-done.6.from_inner, bf16[256,768]{1,0:T(8,128)(2,1)S(1)} %collective-permute-done.7.from_outer, bf16[128,768]{1,0:T(8,128)(2,1)S(1)} %collective-permute-done.8.out2, ...), custom_call_target="tpu_custom_call" | custom-call | flops 100000000 | bytes 2752512 | tf_op jit(solution)/shard_map/total/pallas_call | solution.py:346
  (15 shorter events, 0.1 us)
Async XLA Ops:
  1.7 16.4 %collective-permute-start = (bf16[1552,128]{1,0:T(8,128)(2,1)S(1)}, bf16[1552,128]{1,0:T(8,128)(2,1)S(1)}, u32[]{:S(2)}, u32[]{:S(2)}) collective-permute-start(bf16[1552,128]{1,0:T(8,128)(2,1)S(1)} %get-tuple-element.32), channel_id=1, source_target_pairs={{0,1},{1,2},{2,3},{3,4},{4,5},{5,6},{6,7},{7,0},{8,15},{9,8},{10,9... | collective-permute-start | bytes 1191944 | tf_op jit(solution)/shard_map/ppermute | solution.py:364
  12.4 2.6 %copy-start = (f32[7,8]{1,0:T(8,128)S(1)}, f32[7,8]{1,0:T(8,128)}, u32[]{:S(2)}) copy-start(f32[7,8]{1,0:T(8,128)} %anterp.1) | copy-start | bytes 676
  12.4 2.6 %copy-start.1 = (f32[32]{0:T(128)S(1)}, f32[32]{0:T(128)}, u32[]{:S(2)}) copy-start(f32[32]{0:T(128)} %param.13) | copy-start | bytes 388
  12.4 2.6 %copy-start.2 = (bf16[2,32,8,316]{3,2,1,0:T(8,128)(2,1)S(1)}, bf16[2,32,8,316]{3,2,1,0:T(8,128)(2,1)}, u32[]{:S(2)}) copy-start(bf16[2,32,8,316]{3,2,1,0:T(8,128)(2,1)} %param.14) | copy-start | bytes 970756
  12.4 2.6 %copy-start.3 = (f32[7,8]{1,0:T(8,128)S(1)}, f32[7,8]{1,0:T(8,128)}, u32[]{:S(2)}) copy-start(f32[7,8]{1,0:T(8,128)} %interp.1) | copy-start | bytes 676
  12.5 2.6 %copy-start.4 = (s32[640]{0:T(1024)S(1)}, s32[640]{0:T(1024)}, u32[]{:S(2)}) copy-start(s32[640]{0:T(1024)} %pair_src.1) | copy-start | bytes 7684
  12.5 2.6 %copy-start.5 = (s32[640]{0:T(1024)S(1)}, s32[640]{0:T(1024)}, u32[]{:S(2)}) copy-start(s32[640]{0:T(1024)} %pair_op.1) | copy-start | bytes 7684
  12.5 2.6 %copy-start.6 = (s32[640]{0:T(1024)S(1)}, s32[640]{0:T(1024)}, u32[]{:S(2)}) copy-start(s32[640]{0:T(1024)} %pair_target.1) | copy-start | bytes 7684
  18.1 4.3 %collective-permute-start.1 = (bf16[1552,128]{1,0:T(8,128)(2,1)S(1)}, bf16[1552,128]{1,0:T(8,128)(2,1)S(1)}, u32[]{:S(2)}, u32[]{:S(2)}) collective-permute-start(bf16[1552,128]{1,0:T(8,128)(2,1)S(1)} %collective-permute-done.edge0.edge), channel_id=1, source_target_pairs={{0,8},{8,0},{16,24},{24,16},{32,40},{40,32},{48,56},{56,48},{64,72... | collective-permute-start | bytes 1191944 | tf_op jit(solution)/shard_map/ppermute | solution.py:369
  23.7 14.8 %collective-permute-start.2 = (bf16[528,128]{1,0:T(8,128)(2,1)S(1)}, bf16[528,128]{1,0:T(8,128)(2,1)S(1)}, u32[]{:S(2)}, u32[]{:S(2)}) collective-permute-start(bf16[528,128]{1,0:T(8,128)(2,1)S(1)} %get-tuple-element.49), channel_id=1, source_target_pairs={{8,24},{16,0},{24,40},{32,16},{40,56},{48,32},{56,72},{64,48},{72,... | collective-permute-start | bytes 405512 | tf_op jit(solution)/shard_map/ppermute | solution.py:375
  26.9 11.7 %collective-permute-start.3 = (bf16[528,128]{1,0:T(8,128)(2,1)S(1)}, bf16[528,128]{1,0:T(8,128)(2,1)S(1)}, u32[]{:S(2)}, u32[]{:S(2)}) collective-permute-start(bf16[528,128]{1,0:T(8,128)(2,1)S(1)} %get-tuple-element.50), channel_id=1, source_target_pairs={{0,16},{16,32},{24,8},{32,48},{40,24},{48,64},{56,40},{64,80},{72,... | collective-permute-start | bytes 405512 | tf_op jit(solution)/shard_map/ppermute | solution.py:375
  31.1 7.4 %collective-permute-start.4 = (bf16[528,128]{1,0:T(8,128)(2,1)S(1)}, bf16[528,128]{1,0:T(8,128)(2,1)S(1)}, u32[]{:S(2)}, u32[]{:S(2)}) collective-permute-start(bf16[528,128]{1,0:T(8,128)(2,1)S(1)} %get-tuple-element.51), channel_id=1, source_target_pairs={{8,16},{16,8},{24,32},{32,24},{40,48},{48,40},{56,64},{64,56},{72,... | collective-permute-start | bytes 405512 | tf_op jit(solution)/shard_map/ppermute | solution.py:375
  33.1 5.5 %collective-permute-start.5 = (bf16[528,128]{1,0:T(8,128)(2,1)S(1)}, bf16[528,128]{1,0:T(8,128)(2,1)S(1)}, u32[]{:S(2)}, u32[]{:S(2)}) collective-permute-start(bf16[528,128]{1,0:T(8,128)(2,1)S(1)} %get-tuple-element.52), channel_id=1, source_target_pairs={{0,8},{8,0},{16,24},{24,16},{32,40},{40,32},{48,56},{56,48},{64,72... | collective-permute-start | bytes 405512 | tf_op jit(solution)/shard_map/ppermute | solution.py:375
  39.5 11.8 %collective-permute-start.6 = (bf16[384,768]{1,0:T(8,128)(2,1)S(1)}, bf16[384,768]{1,0:T(8,128)(2,1)S(1)}, u32[]{:S(2)}, u32[]{:S(2)}) collective-permute-start(bf16[384,768]{1,0:T(8,128)(2,1)S(1)} %get-tuple-element.55), channel_id=1, source_target_pairs={{0,1},{1,2},{2,3},{3,4},{4,5},{5,6},{6,7},{7,0},{8,15},{9,8},{10,9... | collective-permute-start | bytes 1769480 | tf_op jit(solution)/shard_map/ppermute | solution.py:364
  44.7 12.8 %collective-permute-start.7 = (bf16[256,768]{1,0:T(8,128)(2,1)S(1)}, bf16[256,768]{1,0:T(8,128)(2,1)S(1)}, u32[]{:S(2)}, u32[]{:S(2)}) collective-permute-start(bf16[256,768]{1,0:T(8,128)(2,1)S(1)} %get-tuple-element.56), channel_id=1, source_target_pairs={{0,7},{1,0},{2,1},{3,2},{4,3},{5,4},{6,5},{7,6},{8,9},{9,10},{10,1... | collective-permute-start | bytes 1179656 | tf_op jit(solution)/shard_map/ppermute | solution.py:364
  51.4 8.5 %collective-permute-start.8 = (bf16[128,768]{1,0:T(8,128)(2,1)S(1)}, bf16[128,768]{1,0:T(8,128)(2,1)S(1)}, u32[]{:S(2)}, u32[]{:S(2)}) collective-permute-start(bf16[128,768]{1,0:T(8,128)(2,1)S(1)} %relay_out.1), channel_id=1, source_target_pairs={{0,2},{1,3},{2,4},{3,5},{4,6},{5,7},{6,0},{7,1},{8,14},{9,15},{10,... | collective-permute-start | bytes 589832 | tf_op jit(solution)/shard_map/ppermute | solution.py:364
  57.5 14.8 %collective-permute-start.9 = (bf16[128,768]{1,0:T(8,128)(2,1)S(1)}, bf16[128,768]{1,0:T(8,128)(2,1)S(1)}, u32[]{:S(2)}, u32[]{:S(2)}) collective-permute-start(bf16[128,768]{1,0:T(8,128)(2,1)S(1)} %relay_in.1), channel_id=1, source_target_pairs={{0,5},{1,6},{2,7},{3,0},{4,1},{5,2},{6,3},{7,4},{8,11},{9,12},{10,... | collective-permute-start | bytes 589832 | tf_op jit(solution)/shard_map/ppermute | solution.py:364

commit v7 on v6

--- a/solution.py
+++ b/solution.py
@@ -151,7 +151,7 @@
 
 def prepare_kernel(
     field, interp, anterp, weights, pair_src, pair_op, pair_target, oper,
-    inter, halo_mat, src_pick, oper_slot, slot_ids, oper_own, own_rows, own_mat,
+    inter, halo_mat, src_pick, oper_slot, slot_ids, oper_own, own_pick, own_table, own_mat,
 ):
     columns = own_columns(interp[...])
     shape = (NS, NS)
@@ -183,7 +183,8 @@
         step_of = step_of + (ahead >= k * BOX).astype(jnp.int32)
     target = ahead - step_of * BOX
     row = iota((8, PAIR), 0)
-    own_rows[...] = jnp.where(row == 0, src_row, jnp.where(step_of == 0, target, -1))
+    own_pick[...] = one_hot(BOX, src_row)
+    own_table[...] = one_hot(BOX, jnp.where(step_of == 0, target, -1))
     step_of = step_of * (2 * odd - 1)
     digits = jnp.ones((8, PAIR), jnp.int32)
     for k, value in enumerate((src_row, op_row, target)):
@@ -244,11 +245,11 @@
         out[2 * NS :, :] = slot_ids[:, cols]
 
 
-def own_kernel(rounded, own_rows, oper_own, own):
-    pick = one_hot(BOX, own_rows[0:1, :])
+def own_kernel(rounded, own_pick, own_table, oper_own, own):
+    pick = own_pick[...]
     re, im = dot(rounded[:, :BOX], pick), dot(rounded[:, BOX:], pick)
     c_re, c_im = multiply(oper_own[...], re, im)
-    table = one_hot(BOX, own_rows[1:2, :])
+    table = own_table[...]
     own[:, :BOX] = dot(c_re, table, NTR)
     own[:, BOX:] = dot(c_im, table, NTR)
 
@@ -404,11 +405,11 @@
         name="field",
         in_specs=[VMEM, HBM],
     )
-    inter, halo_mat, src_pick, oper_slot, slot_ids, oper_own, own_rows, own_mat = call(
+    inter, halo_mat, src_pick, oper_slot, slot_ids, oper_own, own_pick, own_table, own_mat = call(
         prepare_kernel,
         [
             ((NS, 2 * BOX), F32), ((2, 2, NS, EDGE), BF), ((BOX, SLOTS), BF),
-            ((2 * NS, SLOTS), BF), ((16, SLOTS), BF), ((2 * NS, PAIR), BF), ((8, PAIR), jnp.int32),
+            ((2 * NS, SLOTS), BF), ((16, SLOTS), BF), ((2 * NS, PAIR), BF), ((BOX, PAIR), BF), ((BOX, PAIR), BF),
             ((NS, 2 * NS), BF),
         ],
         field, interp, anterp, weights, pair_src, pair_op, pair_target, oper,
@@ -439,7 +440,7 @@
     (own,) = call(
         own_kernel,
         [((NS, 2 * BOX), F32)],
-        rounded, own_rows, oper_own,
+        rounded, own_pick, own_table, oper_own,
         flops=10**9,
         name="own",
     )

time: 74.7 us -> 74.9 us (level); the launches traced: 73.2 us -> 74.2 us
  waiting for transfers between devices: 21.4 us -> 22.4 us
    ppermute x5, waiting for transfers between devices: 21 us -> 22 us  [outward(): return lax.ppermute(value, ('box', 'samp'), pairs)]
where the time goes in v7:
time: 74.9 us; the launch traced here: 74.2 us
  starting transfers between devices  36.3 us (48%)
  waiting for transfers between devices  22.4 us (30%)
  Pallas kernels  15.2 us (20%)
    ppermute x5, waiting for transfers between devices, outward(): return lax.ppermute(value, ('box', 'samp'), pairs)  22 us
    ppermute x5, starting transfers between devices, outward(): return lax.ppermute(value, ('box', 'samp'), pairs)  21 us
    pallas_call x13, Pallas kernels, call(): pl.pallas_call(kernel, out_shape=shapes, scratch_shapes=list(scratch), co...  15.2 us
    ppermute x4, starting transfers between devices, sideways(): lax.ppermute(value, 'box', [(b, to) for b, to in pairs if 0 <= to < groups])  12.8 us
    ppermute x1, starting transfers between devices, across(): return lax.ppermute(value, 'box', [(b, b ^ 1) for b in range(groups)])  2.52 us
  transfers between devices with their start and end apart: 10, of which 5 were waited for; matrix products, arithmetic and copies ran while one was open for 0% of the time, Pallas kernels for 14%

profile of v7, /device:TPU:57, one launch (start us, length us, event | category | flops | bytes accessed | tf_op | source)
XLA Modules:
  0.0 74.2 jit_solution(9749277642593626466)
XLA Ops:
  0.0 1.7 %edge.1 = (bf16[1552,128]{1,0:T(8,128)(2,1)S(1)}, bf16[512,1024]{1,0:T(8,128)(2,1)S(1)}) custom-call(bf16[512,1024]{1,0:T(8,128)(2,1)} %bitcast.8, f32[7,8]{1,0:T(8,128)} %anterp.1, f32[1,32]{1,0:T(1,128)} %bitcast.5), custom_call_target="tpu_custom_call" | custom-call | flops 100000000 | bytes 2494816 | tf_op jit(solution)/shard_map/edge/pallas_call | solution.py:347
  1.7 10.7 %collective-permute-start = (bf16[1552,128]{1,0:T(8,128)(2,1)S(1)}, bf16[1552,128]{1,0:T(8,128)(2,1)S(1)}, u32[]{:S(2)}, u32[]{:S(2)}) collective-permute-start(bf16[1552,128]{1,0:T(8,128)(2,1)S(1)} %get-tuple-element.33), channel_id=1, source_target_pairs={{0,1},{1,2},{2,3},{3,4},{4,5},{5,6},{6,7},{7,0},{8,15},{9,8},{10,9... | collective-permute-start | bytes 1191944 | tf_op jit(solution)/shard_map/ppermute | solution.py:365
  12.4 0.0 copy-start
  12.4 0.0 copy-start.1
  12.4 0.0 copy-start.2
  12.5 0.0 copy-start.5
  12.5 0.0 copy-start.6
  12.5 2.5 %field.1 = (f32[256,768]{1,0:T(8,128)S(1)}, bf16[2,1024,384]{2,1,0:T(8,128)(2,1)S(1)}) custom-call(bf16[512,1024]{1,0:T(8,128)(2,1)S(1)} %get-tuple-element.32.rad, bf16[2,1024,384]{2,1,0:T(8,128)(2,1)} %cur_all.1), custom_call_target="tpu_custom_call" | custom-call | flops 1000000000 | bytes 4980736 | tf_op jit(solution)/shard_map/field/pallas_call | solution.py:347
  15.1 2.9 %prepare.1 = (f32[256,768]{1,0:T(8,128)S(1)}, bf16[2,2,256,96]{3,2,1,0:T(8,128)(2,1)S(1)}, bf16[384,512]{1,0:T(8,128)(2,1)S(1)}, bf16[512,512]{1,0:T(8,128)(2,1)...) custom-call(f32[256,768]{1,0:T(8,128)S(1)} %get-tuple-element.34.fie, ...), custom_call_target="tpu_custom_call" | custom-call | flops 1000000000 | bytes 4935744 | tf_op jit(solution)/shard_map/prepare/pallas_call | solution.py:347
  18.1 0.4 own_matrix.1.own
  18.5 2.5 %collective-permute-start.1 = (bf16[1552,128]{1,0:T(8,128)(2,1)S(1)}, bf16[1552,128]{1,0:T(8,128)(2,1)S(1)}, u32[]{:S(2)}, u32[]{:S(2)}) collective-permute-start(bf16[1552,128]{1,0:T(8,128)(2,1)S(1)} %collective-permute-done.edge0.edge), channel_id=1, source_target_pairs={{0,8},{8,0},{16,24},{24,16},{32,40},{40,32},{48,56},{56,48},{64,72... | collective-permute-start | bytes 1191944 | tf_op jit(solution)/shard_map/ppermute | solution.py:370
  21.0 0.9 %first_edge.1.inter = f32[256,768]{1,0:T(8,128)S(1)} custom-call(f32[256,768]{1,0:T(8,128)S(1)} %get-tuple-element.40.inter, bf16[2,2,256,96]{3,2,1,0:T(8,128)(2,1)S(1)} %get-tuple-element.41.halo_mat, bf16[1552,128]{1,0:T(8,128)(2,1)S(1)} %collective-permute-done.edge0.edge, bf16[2,1024,384]{2,1,0:T(8,128)(2,1)S(1)} %get-tuple-element.42.cur), custom_call_target="tpu_custom_call" | custom-call | flops 400000000 | bytes 3739648 | tf_op jit(solution)/shard_map/first_edge/pallas_call | solution.py:347
  22.0 0.4 collective-permute-done.1.edge1.edge
  22.4 1.4 %send.1 = (bf16[528,128]{1,0:T(8,128)(2,1)S(1)}, bf16[528,128]{1,0:T(8,128)(2,1)S(1)}, bf16[528,128]{1,0:T(8,128)(2,1)S(1)}, bf16[528,128]{1,0:T(8,128)(2,1)S(1)}, bf16[256,768]{1,0:T(8,128)(2,1)S(1)}) custom-call(f32[256,768]{1,0:T(8,128)S(1)} %first_edge.1.inter, bf16[2,2,256,96]{3,2,1,0:T(8,128)(2,1)S(1)} %get-tuple-element.41.halo_mat, ...), custom_call_target="tpu_custom_call" | custom-call | flops 400000000 | bytes 4820992 | tf_op jit(solution)/shard_map/send/pallas_call | solution.py:347
  23.7 3.1 %collective-permute-start.2 = (bf16[528,128]{1,0:T(8,128)(2,1)S(1)}, bf16[528,128]{1,0:T(8,128)(2,1)S(1)}, u32[]{:S(2)}, u32[]{:S(2)}) collective-permute-start(bf16[528,128]{1,0:T(8,128)(2,1)S(1)} %get-tuple-element.51), channel_id=1, source_target_pairs={{8,24},{16,0},{24,40},{32,16},{40,56},{48,32},{56,72},{64,48},{72,... | collective-permute-start | bytes 405512 | tf_op jit(solution)/shard_map/ppermute | solution.py:376
  26.9 4.3 %collective-permute-start.3 = (bf16[528,128]{1,0:T(8,128)(2,1)S(1)}, bf16[528,128]{1,0:T(8,128)(2,1)S(1)}, u32[]{:S(2)}, u32[]{:S(2)}) collective-permute-start(bf16[528,128]{1,0:T(8,128)(2,1)S(1)} %get-tuple-element.52), channel_id=1, source_target_pairs={{0,16},{16,32},{24,8},{32,48},{40,24},{48,64},{56,40},{64,80},{72,... | collective-permute-start | bytes 405512 | tf_op jit(solution)/shard_map/ppermute | solution.py:376
  31.1 1.9 %collective-permute-start.4 = (bf16[528,128]{1,0:T(8,128)(2,1)S(1)}, bf16[528,128]{1,0:T(8,128)(2,1)S(1)}, u32[]{:S(2)}, u32[]{:S(2)}) collective-permute-start(bf16[528,128]{1,0:T(8,128)(2,1)S(1)} %get-tuple-element.53), channel_id=1, source_target_pairs={{8,16},{16,8},{24,32},{32,24},{40,48},{48,40},{56,64},{64,56},{72,... | collective-permute-start | bytes 405512 | tf_op jit(solution)/shard_map/ppermute | solution.py:376
  33.1 3.4 %collective-permute-start.5 = (bf16[528,128]{1,0:T(8,128)(2,1)S(1)}, bf16[528,128]{1,0:T(8,128)(2,1)S(1)}, u32[]{:S(2)}, u32[]{:S(2)}) collective-permute-start(bf16[528,128]{1,0:T(8,128)(2,1)S(1)} %get-tuple-element.54), channel_id=1, source_target_pairs={{0,8},{8,0},{16,24},{24,16},{32,40},{40,32},{48,56},{56,48},{64,72... | collective-permute-start | bytes 405512 | tf_op jit(solution)/shard_map/ppermute | solution.py:376
  36.5 1.1 %own.1 = f32[256,768]{1,0:T(8,128)S(1)} custom-call(bf16[256,768]{1,0:T(8,128)(2,1)S(1)} %get-tuple-element.46.rounded, bf16[384,640]{1,0:T(8,128)(2,1)S(1)} %get-tuple-element.47.own_pick, bf16[384,640]{1,0:T(8,128)(2,1)S(1)} %get-tuple-element.48.own_table, bf16[512,640]{1,0:T(8,128)(2,1)S(1)} %get-tuple-element.49.oper_own), custom_call_target="tpu_custom_call" | custom-call | flops 1000000000 | bytes 2818048 | tf_op jit(solution)/shard_map/own/pallas_call | solution.py:347
  37.6 0.8 %matrix.1 = (bf16[192,512]{1,0:T(8,128)(2,1)S(1)}, bf16[384,512]{1,0:T(8,128)(2,1)S(1)}) custom-call(f32[384,512]{1,0:T(8,128)S(1)} %own_matrix.1.own, bf16[1552,128]{1,0:T(8,128)(2,1)S(1)} %collective-permute-done.edge0.edge, bf16[1552,128]{1,0:T(8,128)(2,1)S(1)} %collective-permute-done.1.edge1.edge), custom_call_target="tpu_custom_call" | custom-call | flops 1000000000 | bytes 2170880 | tf_op jit(solution)/shard_map/matrix/pallas_call | solution.py:347
  38.5 0.9 %far.1 = (bf16[384,768]{1,0:T(8,128)(2,1)S(1)}, bf16[512,768]{1,0:T(8,128)(2,1)S(1)}) custom-call(f32[256,768]{1,0:T(8,128)S(1)} %own.1, bf16[384,512]{1,0:T(8,128)(2,1)S(1)} %get-tuple-element.50.matrix, bf16[528,128]{1,0:T(8,128)(2,1)S(1)} %collective-permute-done.2.got0, bf16[528,128]{1,0:T(8,128)(2,1)S(1)} %collective-permute-done.3.got1, ...), custom_call_target="tpu_custom_call" | custom-call | flops 500000000 | bytes 3096576 | tf_op jit(solution)/shard_map/far/pallas_call | solution.py:347
  39.4 3.6 %collective-permute-start.6 = (bf16[384,768]{1,0:T(8,128)(2,1)S(1)}, bf16[384,768]{1,0:T(8,128)(2,1)S(1)}, u32[]{:S(2)}, u32[]{:S(2)}) collective-permute-start(bf16[384,768]{1,0:T(8,128)(2,1)S(1)} %get-tuple-element.57), channel_id=1, source_target_pairs={{0,1},{1,2},{2,3},{3,4},{4,5},{5,6},{6,7},{7,0},{8,15},{9,8},{10,9... | collective-permute-start | bytes 1769480 | tf_op jit(solution)/shard_map/ppermute | solution.py:365
  43.0 1.5 %near.1 = (bf16[256,768]{1,0:T(8,128)(2,1)S(1)}, f32[384,768]{1,0:T(8,128)S(1)}) custom-call(bf16[512,1024]{1,0:T(8,128)(2,1)S(1)} %get-tuple-element.32.rad, bf16[1552,128]{1,0:T(8,128)(2,1)S(1)} %collective-permute-done.edge0.edge, bf16[1552,128]{1,0:T(8,128)(2,1)S(1)} %collective-permute-done.1.edge1.edge, ...), custom_call_target="tpu_custom_call" | custom-call | flops 1000000000 | bytes 4661248 | tf_op jit(solution)/shard_map/near/pallas_call | solution.py:347
  44.6 1.9 %collective-permute-start.7 = (bf16[256,768]{1,0:T(8,128)(2,1)S(1)}, bf16[256,768]{1,0:T(8,128)(2,1)S(1)}, u32[]{:S(2)}, u32[]{:S(2)}) collective-permute-start(bf16[256,768]{1,0:T(8,128)(2,1)S(1)} %get-tuple-element.58), channel_id=1, source_target_pairs={{0,7},{1,0},{2,1},{3,2},{4,3},{5,4},{6,5},{7,6},{8,9},{9,10},{10,1... | collective-permute-start | bytes 1179656 | tf_op jit(solution)/shard_map/ppermute | solution.py:365
  46.5 4.6 %collective-permute-done.6.from_inner = bf16[384,768]{1,0:T(8,128)(2,1)S(1)} collective-permute-done((bf16[384,768]{1,0:T(8,128)(2,1)S(1)}, bf16[384,768]{1,0:T(8,128)(2,1)S(1)}, u32[]{:S(2)}, u32[]{:S(2)}) %collective-permute-start.6) | collective-permute-done | bytes 589856 | tf_op jit(solution)/shard_map/ppermute | solution.py:365
  51.1 2.9 %collective-permute-start.8 = (bf16[128,768]{1,0:T(8,128)(2,1)S(1)}, bf16[128,768]{1,0:T(8,128)(2,1)S(1)}, u32[]{:S(2)}, u32[]{:S(2)}) collective-permute-start(bf16[128,768]{1,0:T(8,128)(2,1)S(1)} %relay_out.1), channel_id=1, source_target_pairs={{0,2},{1,3},{2,4},{3,5},{4,6},{5,7},{6,0},{7,1},{8,14},{9,15},{10,... | collective-permute-start | bytes 589832 | tf_op jit(solution)/shard_map/ppermute | solution.py:365
  54.0 3.5 %collective-permute-done.7.from_outer = bf16[256,768]{1,0:T(8,128)(2,1)S(1)} collective-permute-done((bf16[256,768]{1,0:T(8,128)(2,1)S(1)}, bf16[256,768]{1,0:T(8,128)(2,1)S(1)}, u32[]{:S(2)}, u32[]{:S(2)}) %collective-permute-start.7) | collective-permute-done | bytes 393248 | tf_op jit(solution)/shard_map/ppermute | solution.py:365
  57.5 0.1 relay_in.1
  57.5 1.9 %collective-permute-start.9 = (bf16[128,768]{1,0:T(8,128)(2,1)S(1)}, bf16[128,768]{1,0:T(8,128)(2,1)S(1)}, u32[]{:S(2)}, u32[]{:S(2)}) collective-permute-start(bf16[128,768]{1,0:T(8,128)(2,1)S(1)} %relay_in.1), channel_id=1, source_target_pairs={{0,5},{1,6},{2,7},{3,0},{4,1},{5,2},{6,3},{7,4},{8,11},{9,12},{10,... | collective-permute-start | bytes 589832 | tf_op jit(solution)/shard_map/ppermute | solution.py:365
  59.5 0.1 collective-permute-done.8.out2
  59.6 13.8 %collective-permute-done.9.in3 = bf16[128,768]{1,0:T(8,128)(2,1)S(1)} collective-permute-done((bf16[128,768]{1,0:T(8,128)(2,1)S(1)}, bf16[128,768]{1,0:T(8,128)(2,1)S(1)}, u32[]{:S(2)}, u32[]{:S(2)}) %collective-permute-start.9) | collective-permute-done | bytes 196640 | tf_op jit(solution)/shard_map/ppermute | solution.py:365
  73.4 0.8 %total.1 = bf16[2,128,384]{2,1,0:T(8,128)(2,1)} custom-call(f32[384,768]{1,0:T(8,128)S(1)} %get-tuple-element.56.keep, bf16[384,768]{1,0:T(8,128)(2,1)S(1)} %collective-permute-done.6.from_inner, bf16[256,768]{1,0:T(8,128)(2,1)S(1)} %collective-permute-done.7.from_outer, bf16[128,768]{1,0:T(8,128)(2,1)S(1)} %collective-permute-done.8.out2, ...), custom_call_target="tpu_custom_call" | custom-call | flops 100000000 | bytes 2752512 | tf_op jit(solution)/shard_map/total/pallas_call | solution.py:347
  (15 shorter events, 0.1 us)
Async XLA Ops:
  1.7 16.8 %collective-permute-start = (bf16[1552,128]{1,0:T(8,128)(2,1)S(1)}, bf16[1552,128]{1,0:T(8,128)(2,1)S(1)}, u32[]{:S(2)}, u32[]{:S(2)}) collective-permute-start(bf16[1552,128]{1,0:T(8,128)(2,1)S(1)} %get-tuple-element.33), channel_id=1, source_target_pairs={{0,1},{1,2},{2,3},{3,4},{4,5},{5,6},{6,7},{7,0},{8,15},{9,8},{10,9... | collective-permute-start | bytes 1191944 | tf_op jit(solution)/shard_map/ppermute | solution.py:365
  12.4 2.6 %copy-start = (f32[7,8]{1,0:T(8,128)S(1)}, f32[7,8]{1,0:T(8,128)}, u32[]{:S(2)}) copy-start(f32[7,8]{1,0:T(8,128)} %anterp.1) | copy-start | bytes 676
  12.4 2.6 %copy-start.1 = (f32[32]{0:T(128)S(1)}, f32[32]{0:T(128)}, u32[]{:S(2)}) copy-start(f32[32]{0:T(128)} %param.13) | copy-start | bytes 388
  12.4 2.6 %copy-start.2 = (bf16[2,32,8,316]{3,2,1,0:T(8,128)(2,1)S(1)}, bf16[2,32,8,316]{3,2,1,0:T(8,128)(2,1)}, u32[]{:S(2)}) copy-start(bf16[2,32,8,316]{3,2,1,0:T(8,128)(2,1)} %param.14) | copy-start | bytes 970756
  12.4 2.6 %copy-start.3 = (f32[7,8]{1,0:T(8,128)S(1)}, f32[7,8]{1,0:T(8,128)}, u32[]{:S(2)}) copy-start(f32[7,8]{1,0:T(8,128)} %interp.1) | copy-start | bytes 676
  12.5 2.6 %copy-start.4 = (s32[640]{0:T(1024)S(1)}, s32[640]{0:T(1024)}, u32[]{:S(2)}) copy-start(s32[640]{0:T(1024)} %pair_src.1) | copy-start | bytes 7684
  12.5 2.6 %copy-start.5 = (s32[640]{0:T(1024)S(1)}, s32[640]{0:T(1024)}, u32[]{:S(2)}) copy-start(s32[640]{0:T(1024)} %pair_op.1) | copy-start | bytes 7684
  12.5 2.6 %copy-start.6 = (s32[640]{0:T(1024)S(1)}, s32[640]{0:T(1024)}, u32[]{:S(2)}) copy-start(s32[640]{0:T(1024)} %pair_target.1) | copy-start | bytes 7684
  18.5 3.9 %collective-permute-start.1 = (bf16[1552,128]{1,0:T(8,128)(2,1)S(1)}, bf16[1552,128]{1,0:T(8,128)(2,1)S(1)}, u32[]{:S(2)}, u32[]{:S(2)}) collective-permute-start(bf16[1552,128]{1,0:T(8,128)(2,1)S(1)} %collective-permute-done.edge0.edge), channel_id=1, source_target_pairs={{0,8},{8,0},{16,24},{24,16},{32,40},{40,32},{48,56},{56,48},{64,72... | collective-permute-start | bytes 1191944 | tf_op jit(solution)/shard_map/ppermute | solution.py:370
  23.7 14.7 %collective-permute-start.2 = (bf16[528,128]{1,0:T(8,128)(2,1)S(1)}, bf16[528,128]{1,0:T(8,128)(2,1)S(1)}, u32[]{:S(2)}, u32[]{:S(2)}) collective-permute-start(bf16[528,128]{1,0:T(8,128)(2,1)S(1)} %get-tuple-element.51), channel_id=1, source_target_pairs={{8,24},{16,0},{24,40},{32,16},{40,56},{48,32},{56,72},{64,48},{72,... | collective-permute-start | bytes 405512 | tf_op jit(solution)/shard_map/ppermute | solution.py:376
  26.9 11.6 %collective-permute-start.3 = (bf16[528,128]{1,0:T(8,128)(2,1)S(1)}, bf16[528,128]{1,0:T(8,128)(2,1)S(1)}, u32[]{:S(2)}, u32[]{:S(2)}) collective-permute-start(bf16[528,128]{1,0:T(8,128)(2,1)S(1)} %get-tuple-element.52), channel_id=1, source_target_pairs={{0,16},{16,32},{24,8},{32,48},{40,24},{48,64},{56,40},{64,80},{72,... | collective-permute-start | bytes 405512 | tf_op jit(solution)/shard_map/ppermute | solution.py:376
  31.1 7.3 %collective-permute-start.4 = (bf16[528,128]{1,0:T(8,128)(2,1)S(1)}, bf16[528,128]{1,0:T(8,128)(2,1)S(1)}, u32[]{:S(2)}, u32[]{:S(2)}) collective-permute-start(bf16[528,128]{1,0:T(8,128)(2,1)S(1)} %get-tuple-element.53), channel_id=1, source_target_pairs={{8,16},{16,8},{24,32},{32,24},{40,48},{48,40},{56,64},{64,56},{72,... | collective-permute-start | bytes 405512 | tf_op jit(solution)/shard_map/ppermute | solution.py:376
  33.1 5.4 %collective-permute-start.5 = (bf16[528,128]{1,0:T(8,128)(2,1)S(1)}, bf16[528,128]{1,0:T(8,128)(2,1)S(1)}, u32[]{:S(2)}, u32[]{:S(2)}) collective-permute-start(bf16[528,128]{1,0:T(8,128)(2,1)S(1)} %get-tuple-element.54), channel_id=1, source_target_pairs={{0,8},{8,0},{16,24},{24,16},{32,40},{40,32},{48,56},{56,48},{64,72... | collective-permute-start | bytes 405512 | tf_op jit(solution)/shard_map/ppermute | solution.py:376
  39.4 11.7 %collective-permute-start.6 = (bf16[384,768]{1,0:T(8,128)(2,1)S(1)}, bf16[384,768]{1,0:T(8,128)(2,1)S(1)}, u32[]{:S(2)}, u32[]{:S(2)}) collective-permute-start(bf16[384,768]{1,0:T(8,128)(2,1)S(1)} %get-tuple-element.57), channel_id=1, source_target_pairs={{0,1},{1,2},{2,3},{3,4},{4,5},{5,6},{6,7},{7,0},{8,15},{9,8},{10,9... | collective-permute-start | bytes 1769480 | tf_op jit(solution)/shard_map/ppermute | solution.py:365
  44.6 12.9 %collective-permute-start.7 = (bf16[256,768]{1,0:T(8,128)(2,1)S(1)}, bf16[256,768]{1,0:T(8,128)(2,1)S(1)}, u32[]{:S(2)}, u32[]{:S(2)}) collective-permute-start(bf16[256,768]{1,0:T(8,128)(2,1)S(1)} %get-tuple-element.58), channel_id=1, source_target_pairs={{0,7},{1,0},{2,1},{3,2},{4,3},{5,4},{6,5},{7,6},{8,9},{9,10},{10,1... | collective-permute-start | bytes 1179656 | tf_op jit(solution)/shard_map/ppermute | solution.py:365
  51.1 8.5 %collective-permute-start.8 = (bf16[128,768]{1,0:T(8,128)(2,1)S(1)}, bf16[128,768]{1,0:T(8,128)(2,1)S(1)}, u32[]{:S(2)}, u32[]{:S(2)}) collective-permute-start(bf16[128,768]{1,0:T(8,128)(2,1)S(1)} %relay_out.1), channel_id=1, source_target_pairs={{0,2},{1,3},{2,4},{3,5},{4,6},{5,7},{6,0},{7,1},{8,14},{9,15},{10,... | collective-permute-start | bytes 589832 | tf_op jit(solution)/shard_map/ppermute | solution.py:365
  57.5 15.9 %collective-permute-start.9 = (bf16[128,768]{1,0:T(8,128)(2,1)S(1)}, bf16[128,768]{1,0:T(8,128)(2,1)S(1)}, u32[]{:S(2)}, u32[]{:S(2)}) collective-permute-start(bf16[128,768]{1,0:T(8,128)(2,1)S(1)} %relay_in.1), channel_id=1, source_target_pairs={{0,5},{1,6},{2,7},{3,0},{4,1},{5,2},{6,3},{7,4},{8,11},{9,12},{10,... | collective-permute-start | bytes 589832 | tf_op jit(solution)/shard_map/ppermute | solution.py:365

commit v8 on v5

--- a/solution.py
+++ b/solution.py
@@ -28,7 +28,7 @@
 KEPT = (0, 2, 5)
 BF = jnp.bfloat16
 HBM = pl.BlockSpec(memory_space=pltpu.HBM)
-EDGE_PARTS = 4
+EDGE_PARTS = 2
 F32 = jnp.float32
 
 NN = (((1,), (0,)), ((), ()))

time: 74.8 us -> 74.5 us (level)
  no operation moved by 1% of the time
where the time goes in v8:
time: 74.5 us; the launch traced here: 74.1 us
  starting transfers between devices  35.1 us (47%)
  waiting for transfers between devices  22.7 us (30%)
  Pallas kernels  13.4 us (18%)
  local copies, waits for them, and re-layouts  2.67 us (4%)
    ppermute x5, waiting for transfers between devices, outward(): return lax.ppermute(value, ('box', 'samp'), pairs)  22 us
    ppermute x5, starting transfers between devices, outward(): return lax.ppermute(value, ('box', 'samp'), pairs)  20.3 us
    pallas_call x12, Pallas kernels, call(): pl.pallas_call(kernel, out_shape=shapes, scratch_shapes=list(scratch), co...  13.4 us
    ppermute x4, starting transfers between devices, sideways(): lax.ppermute(value, 'box', [(b, to) for b, to in pairs if 0 <= to < groups])  12.8 us
    unnamed x22, local copies, waits for them, and re-layouts  2.67 us
    ppermute x1, starting transfers between devices, across(): return lax.ppermute(value, 'box', [(b, b ^ 1) for b in range(groups)])  2.04 us
  transfers between devices with their start and end apart: 10, of which 5 were waited for; matrix products, arithmetic and copies ran while one was open for 0% of the time, Pallas kernels for 12%

profile of v8, /device:TPU:57, one launch (start us, length us, event | category | flops | bytes accessed | tf_op | source)
XLA Modules:
  0.0 74.1 jit_solution(4505663407512621747)
XLA Ops:
  0.0 1.7 %edge.1 = bf16[1552,128]{1,0:T(8,128)(2,1)S(1)} custom-call(bf16[512,1024]{1,0:T(8,128)(2,1)} %bitcast.5, f32[7,8]{1,0:T(8,128)} %anterp.1, f32[1,32]{1,0:T(1,128)} %bitcast.9), custom_call_target="tpu_custom_call" | custom-call | flops 100000000 | bytes 1446240 | tf_op jit(solution)/shard_map/edge/pallas_call | solution.py:314
  1.7 10.7 %collective-permute-start = (bf16[1552,128]{1,0:T(8,128)(2,1)S(1)}, bf16[1552,128]{1,0:T(8,128)(2,1)S(1)}, u32[]{:S(2)}, u32[]{:S(2)}) collective-permute-start(bf16[1552,128]{1,0:T(8,128)(2,1)S(1)} %edge.1), channel_id=1, source_target_pairs={{0,1},{1,2},{2,3},{3,4},{4,5},{5,6},{6,7},{7,0},{8,15},{9,8},{10,9... | collective-permute-start | bytes 1191944 | tf_op jit(solution)/shard_map/ppermute | solution.py:332
  12.4 0.0 copy-start
  12.4 1.4 %copy-done = bf16[2,1024,384]{2,1,0:T(8,128)(2,1)S(1)} copy-done((bf16[2,1024,384]{2,1,0:T(8,128)(2,1)S(1)}, bf16[2,1024,384]{2,1,0:T(8,128)(2,1)}, u32[]{:S(2)}) %copy-start) | copy-done | bytes 1572888
  13.8 1.2 %copy-done.2 = bf16[2,1024,32,8]{1,3,2,0:T(8,128)(2,1)S(1)} copy-done((bf16[2,1024,32,8]{1,3,2,0:T(8,128)(2,1)S(1)}, bf16[2,1024,32,8]{1,3,2,0:T(8,128)(2,1)}, u32[]{:S(2)}) %copy-start.2) | copy-done | bytes 1048600
  15.0 0.0 copy-start.8
  15.1 0.0 copy-start.10
  15.1 1.2 %field.1 = f32[256,768]{1,0:T(8,128)S(1)} custom-call(bf16[512,1024]{1,0:T(8,128)(2,1)S(1)} %bitcast.6, bf16[2,1024,384]{2,1,0:T(8,128)(2,1)S(1)} %copy-done), custom_call_target="tpu_custom_call" | custom-call | flops 1000000000 | bytes 3407872 | tf_op jit(solution)/shard_map/field/pallas_call | solution.py:314
  16.4 2.6 %prepare.1 = (f32[256,768]{1,0:T(8,128)S(1)}, bf16[2,2,256,96]{3,2,1,0:T(8,128)(2,1)S(1)}, bf16[384,512]{1,0:T(8,128)(2,1)S(1)}, bf16[512,512]{1,0:T(8,128)(2,1)...) custom-call(f32[256,768]{1,0:T(8,128)S(1)} %field.1, ...), custom_call_target="tpu_custom_call" | custom-call | flops 1000000000 | bytes 3973184 | tf_op jit(solution)/shard_map/prepare/pallas_call | solution.py:314
  19.0 2.0 %collective-permute-start.1 = (bf16[1552,128]{1,0:T(8,128)(2,1)S(1)}, bf16[1552,128]{1,0:T(8,128)(2,1)S(1)}, u32[]{:S(2)}, u32[]{:S(2)}) collective-permute-start(bf16[1552,128]{1,0:T(8,128)(2,1)S(1)} %collective-permute-done.edge0.edge), channel_id=1, source_target_pairs={{0,8},{8,0},{16,24},{24,16},{32,40},{40,32},{48,56},{56,48},{64,72... | collective-permute-start | bytes 1191944 | tf_op jit(solution)/shard_map/ppermute | solution.py:337
  21.1 0.9 %first_edge.1.inter = f32[256,768]{1,0:T(8,128)S(1)} custom-call(f32[256,768]{1,0:T(8,128)S(1)} %get-tuple-element.32.inter, bf16[2,2,256,96]{3,2,1,0:T(8,128)(2,1)S(1)} %get-tuple-element.33.halo_mat, bf16[1552,128]{1,0:T(8,128)(2,1)S(1)} %collective-permute-done.edge0.edge, bf16[2,1024,384]{2,1,0:T(8,128)(2,1)S(1)} %copy-done.1), custom_call_target="tpu_custom_call" | custom-call | flops 400000000 | bytes 3739648 | tf_op jit(solution)/shard_map/first_edge/pallas_call | solution.py:314
  22.0 0.7 collective-permute-done.1.edge1.edge
  22.6 1.4 %send.1 = (bf16[528,128]{1,0:T(8,128)(2,1)S(1)}, bf16[528,128]{1,0:T(8,128)(2,1)S(1)}, bf16[528,128]{1,0:T(8,128)(2,1)S(1)}, bf16[528,128]{1,0:T(8,128)(2,1)S(1)}, bf16[256,768]{1,0:T(8,128)(2,1)S(1)}) custom-call(f32[256,768]{1,0:T(8,128)S(1)} %first_edge.1.inter, bf16[2,2,256,96]{3,2,1,0:T(8,128)(2,1)S(1)} %get-tuple-element.33.halo_mat, ...), custom_call_target="tpu_custom_call" | custom-call | flops 400000000 | bytes 4820992 | tf_op jit(solution)/shard_map/send/pallas_call | solution.py:314
  24.0 3.1 %collective-permute-start.2 = (bf16[528,128]{1,0:T(8,128)(2,1)S(1)}, bf16[528,128]{1,0:T(8,128)(2,1)S(1)}, u32[]{:S(2)}, u32[]{:S(2)}) collective-permute-start(bf16[528,128]{1,0:T(8,128)(2,1)S(1)} %get-tuple-element.41), channel_id=1, source_target_pairs={{8,24},{16,0},{24,40},{32,16},{40,56},{48,32},{56,72},{64,48},{72,... | collective-permute-start | bytes 405512 | tf_op jit(solution)/shard_map/ppermute | solution.py:343
  27.1 4.3 %collective-permute-start.3 = (bf16[528,128]{1,0:T(8,128)(2,1)S(1)}, bf16[528,128]{1,0:T(8,128)(2,1)S(1)}, u32[]{:S(2)}, u32[]{:S(2)}) collective-permute-start(bf16[528,128]{1,0:T(8,128)(2,1)S(1)} %get-tuple-element.42), channel_id=1, source_target_pairs={{0,16},{16,32},{24,8},{32,48},{40,24},{48,64},{56,40},{64,80},{72,... | collective-permute-start | bytes 405512 | tf_op jit(solution)/shard_map/ppermute | solution.py:343
  31.4 1.9 %collective-permute-start.4 = (bf16[528,128]{1,0:T(8,128)(2,1)S(1)}, bf16[528,128]{1,0:T(8,128)(2,1)S(1)}, u32[]{:S(2)}, u32[]{:S(2)}) collective-permute-start(bf16[528,128]{1,0:T(8,128)(2,1)S(1)} %get-tuple-element.43), channel_id=1, source_target_pairs={{8,16},{16,8},{24,32},{32,24},{40,48},{48,40},{56,64},{64,56},{72,... | collective-permute-start | bytes 405512 | tf_op jit(solution)/shard_map/ppermute | solution.py:343
  33.3 3.4 %collective-permute-start.5 = (bf16[528,128]{1,0:T(8,128)(2,1)S(1)}, bf16[528,128]{1,0:T(8,128)(2,1)S(1)}, u32[]{:S(2)}, u32[]{:S(2)}) collective-permute-start(bf16[528,128]{1,0:T(8,128)(2,1)S(1)} %get-tuple-element.44), channel_id=1, source_target_pairs={{0,8},{8,0},{16,24},{24,16},{32,40},{40,32},{48,56},{56,48},{64,72... | collective-permute-start | bytes 405512 | tf_op jit(solution)/shard_map/ppermute | solution.py:343
  36.8 0.0 copy-start.3
  36.8 1.2 %own.1 = f32[256,768]{1,0:T(8,128)S(1)} custom-call(bf16[256,768]{1,0:T(8,128)(2,1)S(1)} %get-tuple-element.37.rounded, s32[8,640]{1,0:T(8,128)S(1)} %get-tuple-element.38.own_rows, bf16[512,640]{1,0:T(8,128)(2,1)S(1)} %get-tuple-element.39.oper_own), custom_call_target="tpu_custom_call" | custom-call | flops 1000000000 | bytes 1855488 | tf_op jit(solution)/shard_map/own/pallas_call | solution.py:314
  38.0 1.0 %matrix.1 = (bf16[192,512]{1,0:T(8,128)(2,1)S(1)}, bf16[384,512]{1,0:T(8,128)(2,1)S(1)}) custom-call(bf16[512,1024]{1,0:T(8,128)(2,1)S(1)} %bitcast.7, bf16[1552,128]{1,0:T(8,128)(2,1)S(1)} %collective-permute-done.edge0.edge, bf16[1552,128]{1,0:T(8,128)(2,1)S(1)} %collective-permute-done.1.edge1.edge, bf16[256,512]{1,0:T(8,128)(2,1)S(1)} %get-tuple-element.30.own_mat), custom_call_target="tpu_custom_call" | custom-call | flops 1000000000 | bytes 2695168 | tf_op jit(solution)/shard_map/matrix/pallas_call | solution.py:314
  39.1 0.9 %far.1 = (bf16[384,768]{1,0:T(8,128)(2,1)S(1)}, bf16[512,768]{1,0:T(8,128)(2,1)S(1)}) custom-call(f32[256,768]{1,0:T(8,128)S(1)} %own.1, bf16[384,512]{1,0:T(8,128)(2,1)S(1)} %get-tuple-element.40.matrix, bf16[528,128]{1,0:T(8,128)(2,1)S(1)} %collective-permute-done.2.got0, bf16[528,128]{1,0:T(8,128)(2,1)S(1)} %collective-permute-done.3.got1, ...), custom_call_target="tpu_custom_call" | custom-call | flops 500000000 | bytes 3096576 | tf_op jit(solution)/shard_map/far/pallas_call | solution.py:314
  40.0 3.4 %collective-permute-start.6 = (bf16[384,768]{1,0:T(8,128)(2,1)S(1)}, bf16[384,768]{1,0:T(8,128)(2,1)S(1)}, u32[]{:S(2)}, u32[]{:S(2)}) collective-permute-start(bf16[384,768]{1,0:T(8,128)(2,1)S(1)} %get-tuple-element.47), channel_id=1, source_target_pairs={{0,1},{1,2},{2,3},{3,4},{4,5},{5,6},{6,7},{7,0},{8,15},{9,8},{10,9... | collective-permute-start | bytes 1769480 | tf_op jit(solution)/shard_map/ppermute | solution.py:332
  43.4 1.5 %near.1 = (bf16[256,768]{1,0:T(8,128)(2,1)S(1)}, f32[384,768]{1,0:T(8,128)S(1)}) custom-call(bf16[512,1024]{1,0:T(8,128)(2,1)S(1)} %bitcast.8, bf16[1552,128]{1,0:T(8,128)(2,1)S(1)} %collective-permute-done.edge0.edge, bf16[1552,128]{1,0:T(8,128)(2,1)S(1)} %collective-permute-done.1.edge1.edge, bf16[256,512]{1,0:T(8,128)(2,1)S(1)} %get-tuple-element.30.own_mat, ...), custom_call_target="tpu_custom_call" | custom-call | flops 1000000000 | bytes 4661248 | tf_op jit(solution)/shard_map/near/pallas_call | solution.py:314
  44.9 1.9 %collective-permute-start.7 = (bf16[256,768]{1,0:T(8,128)(2,1)S(1)}, bf16[256,768]{1,0:T(8,128)(2,1)S(1)}, u32[]{:S(2)}, u32[]{:S(2)}) collective-permute-start(bf16[256,768]{1,0:T(8,128)(2,1)S(1)} %get-tuple-element.48), channel_id=1, source_target_pairs={{0,7},{1,0},{2,1},{3,2},{4,3},{5,4},{6,5},{7,6},{8,9},{9,10},{10,1... | collective-permute-start | bytes 1179656 | tf_op jit(solution)/shard_map/ppermute | solution.py:332
  46.8 5.4 %collective-permute-done.6.from_inner = bf16[384,768]{1,0:T(8,128)(2,1)S(1)} collective-permute-done((bf16[384,768]{1,0:T(8,128)(2,1)S(1)}, bf16[384,768]{1,0:T(8,128)(2,1)S(1)}, u32[]{:S(2)}, u32[]{:S(2)}) %collective-permute-start.6) | collective-permute-done | bytes 589856 | tf_op jit(solution)/shard_map/ppermute | solution.py:332
  52.3 2.3 %collective-permute-start.8 = (bf16[128,768]{1,0:T(8,128)(2,1)S(1)}, bf16[128,768]{1,0:T(8,128)(2,1)S(1)}, u32[]{:S(2)}, u32[]{:S(2)}) collective-permute-start(bf16[128,768]{1,0:T(8,128)(2,1)S(1)} %relay_out.1), channel_id=1, source_target_pairs={{0,2},{1,3},{2,4},{3,5},{4,6},{5,7},{6,0},{7,1},{8,14},{9,15},{10,... | collective-permute-start | bytes 589832 | tf_op jit(solution)/shard_map/ppermute | solution.py:332
  54.6 2.9 %collective-permute-done.7.from_outer = bf16[256,768]{1,0:T(8,128)(2,1)S(1)} collective-permute-done((bf16[256,768]{1,0:T(8,128)(2,1)S(1)}, bf16[256,768]{1,0:T(8,128)(2,1)S(1)}, u32[]{:S(2)}, u32[]{:S(2)}) %collective-permute-start.7) | collective-permute-done | bytes 393248 | tf_op jit(solution)/shard_map/ppermute | solution.py:332
  57.5 0.1 relay_in.1
  57.5 2.0 %collective-permute-start.9 = (bf16[128,768]{1,0:T(8,128)(2,1)S(1)}, bf16[128,768]{1,0:T(8,128)(2,1)S(1)}, u32[]{:S(2)}, u32[]{:S(2)}) collective-permute-start(bf16[128,768]{1,0:T(8,128)(2,1)S(1)} %relay_in.1), channel_id=1, source_target_pairs={{0,5},{1,6},{2,7},{3,0},{4,1},{5,2},{6,3},{7,4},{8,11},{9,12},{10,... | collective-permute-start | bytes 589832 | tf_op jit(solution)/shard_map/ppermute | solution.py:332
  59.5 1.5 %collective-permute-done.8.out2 = bf16[128,768]{1,0:T(8,128)(2,1)S(1)} collective-permute-done((bf16[128,768]{1,0:T(8,128)(2,1)S(1)}, bf16[128,768]{1,0:T(8,128)(2,1)S(1)}, u32[]{:S(2)}, u32[]{:S(2)}) %collective-permute-start.8) | collective-permute-done | bytes 196640 | tf_op jit(solution)/shard_map/ppermute | solution.py:332
  61.0 12.3 %collective-permute-done.9.in3 = bf16[128,768]{1,0:T(8,128)(2,1)S(1)} collective-permute-done((bf16[128,768]{1,0:T(8,128)(2,1)S(1)}, bf16[128,768]{1,0:T(8,128)(2,1)S(1)}, u32[]{:S(2)}, u32[]{:S(2)}) %collective-permute-start.9) | collective-permute-done | bytes 196640 | tf_op jit(solution)/shard_map/ppermute | solution.py:332
  73.3 0.8 %total.1 = bf16[2,128,384]{2,1,0:T(8,128)(2,1)} custom-call(f32[384,768]{1,0:T(8,128)S(1)} %get-tuple-element.46.keep, bf16[384,768]{1,0:T(8,128)(2,1)S(1)} %collective-permute-done.6.from_inner, bf16[256,768]{1,0:T(8,128)(2,1)S(1)} %collective-permute-done.7.from_outer, bf16[128,768]{1,0:T(8,128)(2,1)S(1)} %collective-permute-done.8.out2, ...), custom_call_target="tpu_custom_call" | custom-call | flops 100000000 | bytes 2752512 | tf_op jit(solution)/shard_map/total/pallas_call | solution.py:314
  (22 shorter events, 0.1 us)
Async XLA Ops:
  1.7 17.3 %collective-permute-start = (bf16[1552,128]{1,0:T(8,128)(2,1)S(1)}, bf16[1552,128]{1,0:T(8,128)(2,1)S(1)}, u32[]{:S(2)}, u32[]{:S(2)}) collective-permute-start(bf16[1552,128]{1,0:T(8,128)(2,1)S(1)} %edge.1), channel_id=1, source_target_pairs={{0,1},{1,2},{2,3},{3,4},{4,5},{5,6},{6,7},{7,0},{8,15},{9,8},{10,9... | collective-permute-start | bytes 1191944 | tf_op jit(solution)/shard_map/ppermute | solution.py:332
  12.4 1.4 %copy-start = (bf16[2,1024,384]{2,1,0:T(8,128)(2,1)S(1)}, bf16[2,1024,384]{2,1,0:T(8,128)(2,1)}, u32[]{:S(2)}) copy-start(bf16[2,1024,384]{2,1,0:T(8,128)(2,1)} %cur.5) | copy-start | bytes 4718596
  13.8 1.2 %copy-start.2 = (bf16[2,1024,32,8]{1,3,2,0:T(8,128)(2,1)S(1)}, bf16[2,1024,32,8]{1,3,2,0:T(8,128)(2,1)}, u32[]{:S(2)}) copy-start(bf16[2,1024,32,8]{1,3,2,0:T(8,128)(2,1)} %param.10) | copy-start | bytes 3145732
  15.0 1.3 %copy-start.4 = (f32[7,8]{1,0:T(8,128)S(1)}, f32[7,8]{1,0:T(8,128)}, u32[]{:S(2)}) copy-start(f32[7,8]{1,0:T(8,128)} %anterp.1) | copy-start | bytes 676
  15.0 1.3 %copy-start.5 = (f32[32]{0:T(128)S(1)}, f32[32]{0:T(128)}, u32[]{:S(2)}) copy-start(f32[32]{0:T(128)} %param.13) | copy-start | bytes 388
  15.0 1.3 %copy-start.6 = (bf16[2,32,8,316]{3,2,1,0:T(8,128)(2,1)S(1)}, bf16[2,32,8,316]{3,2,1,0:T(8,128)(2,1)}, u32[]{:S(2)}) copy-start(bf16[2,32,8,316]{3,2,1,0:T(8,128)(2,1)} %param.14) | copy-start | bytes 970756
  15.0 1.3 %copy-start.7 = (f32[7,8]{1,0:T(8,128)S(1)}, f32[7,8]{1,0:T(8,128)}, u32[]{:S(2)}) copy-start(f32[7,8]{1,0:T(8,128)} %interp.1) | copy-start | bytes 676
  15.0 1.3 %copy-start.8 = (s32[640]{0:T(1024)S(1)}, s32[640]{0:T(1024)}, u32[]{:S(2)}) copy-start(s32[640]{0:T(1024)} %pair_src.1) | copy-start | bytes 7684
  15.1 1.3 %copy-start.9 = (s32[640]{0:T(1024)S(1)}, s32[640]{0:T(1024)}, u32[]{:S(2)}) copy-start(s32[640]{0:T(1024)} %pair_op.1) | copy-start | bytes 7684
  15.1 1.3 %copy-start.10 = (s32[640]{0:T(1024)S(1)}, s32[640]{0:T(1024)}, u32[]{:S(2)}) copy-start(s32[640]{0:T(1024)} %pair_target.1) | copy-start | bytes 7684
  16.4 4.6 %copy-start.1 = (bf16[2,1024,384]{2,1,0:T(8,128)(2,1)S(1)}, bf16[2,1024,384]{2,1,0:T(8,128)(2,1)}, u32[]{:S(2)}) copy-start(bf16[2,1024,384]{2,1,0:T(8,128)(2,1)} %cur.5) | copy-start | bytes 4718596
  19.0 3.6 %collective-permute-start.1 = (bf16[1552,128]{1,0:T(8,128)(2,1)S(1)}, bf16[1552,128]{1,0:T(8,128)(2,1)S(1)}, u32[]{:S(2)}, u32[]{:S(2)}) collective-permute-start(bf16[1552,128]{1,0:T(8,128)(2,1)S(1)} %collective-permute-done.edge0.edge), channel_id=1, source_target_pairs={{0,8},{8,0},{16,24},{24,16},{32,40},{40,32},{48,56},{56,48},{64,72... | collective-permute-start | bytes 1191944 | tf_op jit(solution)/shard_map/ppermute | solution.py:337
  24.0 15.0 %collective-permute-start.2 = (bf16[528,128]{1,0:T(8,128)(2,1)S(1)}, bf16[528,128]{1,0:T(8,128)(2,1)S(1)}, u32[]{:S(2)}, u32[]{:S(2)}) collective-permute-start(bf16[528,128]{1,0:T(8,128)(2,1)S(1)} %get-tuple-element.41), channel_id=1, source_target_pairs={{8,24},{16,0},{24,40},{32,16},{40,56},{48,32},{56,72},{64,48},{72,... | collective-permute-start | bytes 405512 | tf_op jit(solution)/shard_map/ppermute | solution.py:343
  27.1 11.9 %collective-permute-start.3 = (bf16[528,128]{1,0:T(8,128)(2,1)S(1)}, bf16[528,128]{1,0:T(8,128)(2,1)S(1)}, u32[]{:S(2)}, u32[]{:S(2)}) collective-permute-start(bf16[528,128]{1,0:T(8,128)(2,1)S(1)} %get-tuple-element.42), channel_id=1, source_target_pairs={{0,16},{16,32},{24,8},{32,48},{40,24},{48,64},{56,40},{64,80},{72,... | collective-permute-start | bytes 405512 | tf_op jit(solution)/shard_map/ppermute | solution.py:343
  31.4 7.7 %collective-permute-start.4 = (bf16[528,128]{1,0:T(8,128)(2,1)S(1)}, bf16[528,128]{1,0:T(8,128)(2,1)S(1)}, u32[]{:S(2)}, u32[]{:S(2)}) collective-permute-start(bf16[528,128]{1,0:T(8,128)(2,1)S(1)} %get-tuple-element.43), channel_id=1, source_target_pairs={{8,16},{16,8},{24,32},{32,24},{40,48},{48,40},{56,64},{64,56},{72,... | collective-permute-start | bytes 405512 | tf_op jit(solution)/shard_map/ppermute | solution.py:343
  33.3 5.7 %collective-permute-start.5 = (bf16[528,128]{1,0:T(8,128)(2,1)S(1)}, bf16[528,128]{1,0:T(8,128)(2,1)S(1)}, u32[]{:S(2)}, u32[]{:S(2)}) collective-permute-start(bf16[528,128]{1,0:T(8,128)(2,1)S(1)} %get-tuple-element.44), channel_id=1, source_target_pairs={{0,8},{8,0},{16,24},{24,16},{32,40},{40,32},{48,56},{56,48},{64,72... | collective-permute-start | bytes 405512 | tf_op jit(solution)/shard_map/ppermute | solution.py:343
  36.8 1.2 %copy-start.3 = (bf16[2,1024,32,8]{1,3,2,0:T(8,128)(2,1)S(1)}, bf16[2,1024,32,8]{1,3,2,0:T(8,128)(2,1)}, u32[]{:S(2)}) copy-start(bf16[2,1024,32,8]{1,3,2,0:T(8,128)(2,1)} %param.10) | copy-start | bytes 3145732
  40.0 12.3 %collective-permute-start.6 = (bf16[384,768]{1,0:T(8,128)(2,1)S(1)}, bf16[384,768]{1,0:T(8,128)(2,1)S(1)}, u32[]{:S(2)}, u32[]{:S(2)}) collective-permute-start(bf16[384,768]{1,0:T(8,128)(2,1)S(1)} %get-tuple-element.47), channel_id=1, source_target_pairs={{0,1},{1,2},{2,3},{3,4},{4,5},{5,6},{6,7},{7,0},{8,15},{9,8},{10,9... | collective-permute-start | bytes 1769480 | tf_op jit(solution)/shard_map/ppermute | solution.py:332
  44.9 12.6 %collective-permute-start.7 = (bf16[256,768]{1,0:T(8,128)(2,1)S(1)}, bf16[256,768]{1,0:T(8,128)(2,1)S(1)}, u32[]{:S(2)}, u32[]{:S(2)}) collective-permute-start(bf16[256,768]{1,0:T(8,128)(2,1)S(1)} %get-tuple-element.48), channel_id=1, source_target_pairs={{0,7},{1,0},{2,1},{3,2},{4,3},{5,4},{6,5},{7,6},{8,9},{9,10},{10,1... | collective-permute-start | bytes 1179656 | tf_op jit(solution)/shard_map/ppermute | solution.py:332
  52.3 8.7 %collective-permute-start.8 = (bf16[128,768]{1,0:T(8,128)(2,1)S(1)}, bf16[128,768]{1,0:T(8,128)(2,1)S(1)}, u32[]{:S(2)}, u32[]{:S(2)}) collective-permute-start(bf16[128,768]{1,0:T(8,128)(2,1)S(1)} %relay_out.1), channel_id=1, source_target_pairs={{0,2},{1,3},{2,4},{3,5},{4,6},{5,7},{6,0},{7,1},{8,14},{9,15},{10,... | collective-permute-start | bytes 589832 | tf_op jit(solution)/shard_map/ppermute | solution.py:332
  57.5 15.7 %collective-permute-start.9 = (bf16[128,768]{1,0:T(8,128)(2,1)S(1)}, bf16[128,768]{1,0:T(8,128)(2,1)S(1)}, u32[]{:S(2)}, u32[]{:S(2)}) collective-permute-start(bf16[128,768]{1,0:T(8,128)(2,1)S(1)} %relay_in.1), channel_id=1, source_target_pairs={{0,5},{1,6},{2,7},{3,0},{4,1},{5,2},{6,3},{7,4},{8,11},{9,12},{10,... | collective-permute-start | bytes 589832 | tf_op jit(solution)/shard_map/ppermute | solution.py:332
